TPU v7x, 32 devices: a whole 2x2x4 slice. The times are simulated.
32 devices in a mesh: seq: 2 (over y), exp: 16 (over z, x, core).
Axes of the slice: x: 2, y: 2, z: 4, core: 2. Of those that a mesh axis runs over, the one named last changes fastest.
Arguments:
- tokens: bfloat16 [2048, 4096], P(('seq', 'exp')), may hold values from -6 to 6
- norm_gain: float32 [4096], replicated, may hold values from 0.1 to 1.9
- queries: bfloat16 [2048, 2048], P(('seq', 'exp')), may hold values from -24 to 24
- attn_keys: bfloat16 [2048, 2048], P(('seq', 'exp')), may hold values from -4.5 to 4.5
- attn_values: bfloat16 [2048, 2048], P(('seq', 'exp')), may hold values from -6 to 6
- expert_ids: int32 [2048, 2], P(('seq', 'exp')), may hold values from 0 to 63, all different within a row; in each aligned block of 64 rows (0 to 63, 64 to 127, ...) at most 2 rows name the same one
- route_weights: float32 [2048, 2], P(('seq', 'exp')), may hold values from 0.1 to 1
- gate_proj: bfloat16 [64, 1408, 4096], P('exp', 'seq'), may hold values from -0.09375 to 0.09375
- up_proj: bfloat16 [64, 1408, 4096], P('exp', 'seq'), may hold values from -0.09375 to 0.09375
- down_proj: bfloat16 [64, 1408, 4096], P('exp', 'seq'), may hold values from -0.15625 to 0.15625
Outputs:
- attention: bfloat16 [2048, 2048], P(('seq', 'exp'))
- expert_mix: bfloat16 [2048, 4096], P(('seq', 'exp'))
Inputs may be any that keep to these rules, and one draw needn't show every extreme that they name: `expert_ids`: the two experts of a token differ. Among the rows of one device (64 consecutive tokens, aligned), every expert is named exactly 2 times.
All inputs are finite; a program needn't handle non-finite values.
Results may differ from a plain program's by a relative error of at most 0.015.
Values may be sent and summed in bfloat16 or wider, within the bound.
No kernel may reach another device: no remote copies, remote signals or barrier semaphores. Data moves between devices by JAX's collectives and lax.ppermute only.
A program may use at most 128 MiB of HBM per device.

v0:
```python
import functools
import math

import jax
import jax.numpy as jnp
from jax import lax
from jax.experimental import pallas as pl
from jax.experimental.pallas import tpu as pltpu
from jax.sharding import PartitionSpec as P

EXPERTS = 64
HDIM = 64
SUMS = 64
SEG_DEV = 2
CAP = 2
CHUNKS = 2

EPS = 1e-05
NEG = -1e30
F32 = jnp.float32
BF16 = jnp.bfloat16

VMEM = pl.BlockSpec(memory_space=pltpu.VMEM)
ANY = pl.BlockSpec(memory_space=pl.ANY)
LITTLE = pl.CostEstimate(flops=1000, bytes_accessed=1000, transcendentals=0)
SMEM = pl.BlockSpec(memory_space=pltpu.SMEM)


def params(mib):
    return pltpu.CompilerParams(vmem_limit_bytes=mib * 2**20)


def as_row(column):
    n = column.shape[0]
    eye = lax.broadcasted_iota(jnp.int32, (n, n), 0) == lax.broadcasted_iota(jnp.int32, (n, n), 1)
    return jnp.sum(jnp.where(eye, column, 0), axis=0, keepdims=True)


def slots(ids):
    n = ids.shape[0]
    columns = [ids[:, 0:1], ids[:, 1:2]]
    rows = [as_row(column) for column in columns]
    earlier = lax.broadcasted_iota(jnp.int32, (n, n), 1) < lax.broadcasted_iota(jnp.int32, (n, n), 0)
    found = []
    for column in columns:
        same = (rows[0] == column) | (rows[1] == column)
        before = jnp.sum(jnp.where(same & earlier, 1, 0), axis=1, keepdims=True)
        found.append(column * CAP + before)
    return found


def prep_kernel(tok_ref, gain_ref, ids_ref, *out_refs):
    n = tok_ref.shape[0]
    values = tok_ref[...].astype(F32)
    inv_rms = lax.rsqrt(jnp.mean(values * values, axis=-1, keepdims=True) + EPS)
    normed = (values * inv_rms * gain_ref[...]).astype(BF16)
    first, second = [as_row(column) for column in slots(ids_ref[...])]
    place = lax.broadcasted_iota(jnp.int32, (EXPERTS * CAP, n), 0)
    pick = jnp.where((place == first) | (place == second), 1.0, 0.0).astype(BF16)
    rows = jnp.dot(pick, normed, preferred_element_type=F32)
    dests, step = out_refs[0].shape[0], out_refs[0].shape[1]
    for dest in range(dests):
        for chunk, out_ref in enumerate(out_refs):
            lower = (dest * len(out_refs) + chunk) * step
            out_ref[dest] = rows[lower : lower + step].astype(BF16)


def sums_kernel(block, k_ref, v_ref, out_ref):
    total, _ = k_ref.shape
    count = total // block
    row = lax.broadcasted_iota(jnp.int32, (count, total), 0)
    column = lax.broadcasted_iota(jnp.int32, (count, total), 1)
    member = jnp.where(column // block == row, 1.0, 0.0).astype(BF16)
    for which, ref in enumerate((k_ref, v_ref)):
        summed = jnp.dot(member, ref[...], preferred_element_type=F32) * (1.0 / math.sqrt(block))
        out_ref[which * count : (which + 1) * count] = summed.astype(BF16)


def pack_kernel(q_ref, k_ref, v_ref, *refs):
    sum_refs, out_ref = refs[:-1], refs[-1]
    dests, _, width = out_ref.shape
    for dest in range(dests):
        lower = 0
        for ref in (q_ref, k_ref, v_ref, *sum_refs):
            upper = lower + ref.shape[0]
            out_ref[dest, lower:upper] = ref[:, dest * width : (dest + 1) * width]
            lower = upper


def attend_kernel(query_rows, tokens, segs, at_ref, recv_ref, *refs):
    out_refs, mixed_ref = refs[:-1], refs[-1]
    sources, _, width = recv_ref.shape
    seg_len = sources * tokens
    query, key, value = (
        recv_ref[:, which * tokens : (which + 1) * tokens].reshape(seg_len, width) for which in range(3)
    )
    sum_total = segs * SUMS
    per = SUMS // sources
    sum_rows = [
        recv_ref[:, 3 * tokens + at * per : 3 * tokens + (at + 1) * per].reshape(SUMS, width)
        for at in range(2 * segs)
    ]
    sum_keys = jnp.concatenate(sum_rows[0::2], axis=0)
    sum_values = jnp.concatenate(sum_rows[1::2], axis=0)
    scale = 1.0 / math.sqrt(HDIM)
    segment = at_ref[0]
    lane = lax.broadcasted_iota(jnp.int32, (1, width), 1)
    nt = (((1,), (1,)), ((), ()))
    for first in range(0, seg_len, query_rows):
        last = first + query_rows
        local_ok = (
            lax.broadcasted_iota(jnp.int32, (query_rows, last), 1)
            <= lax.broadcasted_iota(jnp.int32, (query_rows, last), 0) + first
        )
        summ_seg = lax.broadcasted_iota(jnp.int32, (query_rows, sum_total), 1) // SUMS
        summ_ok = jnp.bitwise_xor(summ_seg, segment) < segment
        mixed = jnp.zeros((query_rows, width), F32)
        for head in range(width // HDIM):
            mine = (lane >= head * HDIM) & (lane < (head + 1) * HDIM)
            rows = jnp.where(mine, query[first:last], jnp.zeros((), BF16))
            local_sc = lax.dot_general(rows, key[:last], nt, preferred_element_type=F32) * scale
            summ_sc = lax.dot_general(rows, sum_keys, nt, preferred_element_type=F32) * scale
            local_sc = jnp.where(local_ok, local_sc, NEG)
            summ_sc = jnp.where(summ_ok, summ_sc, NEG)
            top = jnp.maximum(
                jnp.max(local_sc, axis=-1, keepdims=True), jnp.max(summ_sc, axis=-1, keepdims=True)
            )
            local_ex = jnp.exp(local_sc - top)
            summ_ex = jnp.exp(summ_sc - top)
            inv = 1.0 / (
                jnp.sum(local_ex, axis=-1, keepdims=True) + jnp.sum(summ_ex, axis=-1, keepdims=True)
            )
            got = jnp.dot((local_ex * inv).astype(BF16), value[:last], preferred_element_type=F32)
            got += jnp.dot((summ_ex * inv).astype(BF16), sum_values, preferred_element_type=F32)
            mixed = jnp.where(mine, got, mixed)
        for source in range(first // tokens, last // tokens):
            lower = source * tokens - first
            mixed_ref[source] = mixed[lower : lower + tokens].astype(BF16)
    for other, out_ref in enumerate(out_refs):
        out_ref[...] = mixed_ref[jnp.bitwise_xor(at_ref[1], other)]


def place_kernel(at_ref, *refs):
    in_refs, out_ref = refs[:-1], refs[-1]
    width = in_refs[0].shape[1]
    for other, ref in enumerate(in_refs):
        lower = pl.multiple_of(jnp.bitwise_xor(at_ref[1], other) * width, width)
        out_ref[:, pl.ds(lower, width)] = ref[...]


def ffn_kernel(base, planes, *refs):
    row_refs, (gate_ref, up_ref, down_ref) = refs[:planes], refs[planes : planes + 3]
    out_refs = refs[planes + 3 : 2 * planes + 3]
    buf, x_ref, y_ref, sem = refs[2 * planes + 3 :]
    sources, step, width = row_refs[0].shape
    experts = step // CAP
    copies = []
    for expert in range(experts):
        for which, ref in enumerate((gate_ref, up_ref, down_ref)):
            at = expert * 3 + which
            copy = pltpu.make_async_copy(ref.at[base + expert], buf.at[at], sem.at[at])
            copy.start()
            copies.append(copy)
    total = planes * sources * step
    for plane in range(planes):
        for source in range(sources):
            lower = (plane * sources + source) * step
            y_ref[lower : lower + step] = row_refs[plane][source].astype(F32)
    to = lax.broadcasted_iota(jnp.int32, (total, total), 0)
    frm = lax.broadcasted_iota(jnp.int32, (total, total), 1)
    per = total // experts
    order = (to % per // CAP) * step + (to // per) * CAP + to % CAP
    sort = jnp.where(frm == order, 1.0, 0.0).astype(BF16)
    x_ref[...] = jnp.dot(sort, y_ref[...].astype(BF16), preferred_element_type=F32).astype(BF16)
    nt = (((1,), (1,)), ((), ()))
    for expert in range(experts):
        rows = x_ref[expert * per : (expert + 1) * per]
        copies[expert * 3].wait()
        gate = lax.dot_general(rows, buf[expert * 3], nt, preferred_element_type=F32)
        copies[expert * 3 + 1].wait()
        up = lax.dot_general(rows, buf[expert * 3 + 1], nt, preferred_element_type=F32)
        hidden = (gate / (1.0 + jnp.exp(-gate)) * up).astype(BF16)
        copies[expert * 3 + 2].wait()
        piece = jnp.dot(hidden, buf[expert * 3 + 2], preferred_element_type=F32)
        x_ref[expert * per : (expert + 1) * per] = piece.astype(BF16)
    inverse = (to // step) * CAP + (to % step // CAP) * per + to % CAP
    unsort = jnp.where(frm == inverse, 1.0, 0.0).astype(BF16)
    y_ref[...] = jnp.dot(unsort, x_ref[...], preferred_element_type=F32)
    for plane in range(planes):
        for source in range(sources):
            lower = (plane * sources + source) * step
            out_refs[plane][source] = y_ref[lower : lower + step].astype(BF16)


def mix_kernel(ids_ref, weight_ref, *refs):
    in_refs, out_ref, y_ref = refs[:-2], refs[-2], refs[-1]
    dests, step = in_refs[0].shape[0], in_refs[0].shape[1]
    for dest in range(dests):
        for chunk, ref in enumerate(in_refs):
            lower = (dest * len(in_refs) + chunk) * step
            y_ref[lower : lower + step] = ref[dest].astype(F32)
    rows = y_ref[...].astype(BF16)
    n = ids_ref.shape[0]
    place = lax.broadcasted_iota(jnp.int32, (n, EXPERTS * CAP), 1)
    total = None
    for k, column in enumerate(slots(ids_ref[...])):
        pick = jnp.where(place == column, 1.0, 0.0).astype(BF16)
        part = weight_ref[:, k : k + 1] * jnp.dot(pick, rows, preferred_element_type=F32)
        total = part if total is None else total + part
    out_ref[...] = total.astype(BF16)


def after(value, earlier):
    return lax.optimization_barrier((value, earlier))[0]


def shape(dims, kind=BF16):
    return jax.ShapeDtypeStruct(dims, kind)


def on_device(
    tokens,
    norm_gain,
    queries,
    attn_keys,
    attn_values,
    expert_ids,
    route_weights,
    gate_proj,
    up_proj,
    down_proj,
):
    exp_count = lax.axis_size("exp")
    seq_count = lax.axis_size("seq")
    local_tokens, features = tokens.shape
    exp_dev, hidden = gate_proj.shape[0], gate_proj.shape[1]
    chunks = CHUNKS
    experts = exp_dev // chunks
    step = experts * CAP
    group = exp_count // SEG_DEV
    seg_len = group * local_tokens
    segs = seq_count * SEG_DEV
    att = queries.shape[1]
    width = att // group

    send = pl.pallas_call(
        prep_kernel,
        out_shape=[shape((exp_count, step, features))] * chunks,
        in_specs=[VMEM] * 3,
        out_specs=[VMEM] * chunks,
        compiler_params=params(32),
        cost_estimate=LITTLE,
        name="prep",
    )(tokens, norm_gain.reshape(1, -1), expert_ids)

    block = seg_len // SUMS
    sums = pl.pallas_call(
        functools.partial(sums_kernel, block),
        out_shape=shape((2 * local_tokens // block, att)),
        in_specs=[VMEM] * 2,
        out_specs=VMEM,
        compiler_params=params(32),
        cost_estimate=LITTLE,
        name="sums",
    )(after(attn_keys, send[0]), attn_values)
    halved = lax.ppermute(sums, "exp", [(i, i ^ group) for i in range(exp_count)])
    sums = jnp.concatenate([sums, halved], axis=0)
    parts = [sums]
    for other in range(1, seq_count):
        parts.append(lax.ppermute(sums, "seq", [(i, i ^ other) for i in range(seq_count)]))
    packed_rows = 3 * local_tokens + segs * 2 * local_tokens // block
    packed = pl.pallas_call(
        pack_kernel,
        out_shape=shape((group, packed_rows, width)),
        in_specs=[VMEM] * (3 + seq_count),
        out_specs=VMEM,
        compiler_params=params(32),
        cost_estimate=LITTLE,
        name="pack",
    )(queries, attn_keys, attn_values, *parts)
    recv = []
    for rows in send:
        if recv:
            rows = after(rows, recv[-1])
        recv.append(lax.all_to_all(rows, "exp", 0, 0, tiled=True))
    packed = after(packed, recv[-1])
    halves = [[half * group + j for j in range(group)] for half in range(SEG_DEV)]
    got = lax.all_to_all(packed, "exp", 0, 0, axis_index_groups=halves, tiled=True)
    segment = lax.axis_index("seq") * SEG_DEV + lax.axis_index("exp") // group
    place = lax.axis_index("exp") % group
    position = jnp.stack([segment, place]).astype(jnp.int32)
    head_out = pl.pallas_call(
        functools.partial(attend_kernel, min(256, seg_len), local_tokens, segs),
        out_shape=[shape((local_tokens, width))] * group,
        in_specs=[SMEM, VMEM],
        out_specs=[VMEM] * group,
        scratch_shapes=[pltpu.VMEM((group, local_tokens, width), BF16)],
        compiler_params=params(48),
        cost_estimate=LITTLE,
        name="attend",
    )(position, got)
    heads = [
        rows
        if other == 0
        else lax.ppermute(rows, "exp", [(i, i ^ other) for i in range(exp_count)])
        for other, rows in enumerate(head_out)
    ]
    attention = pl.pallas_call(
        place_kernel,
        out_shape=shape((local_tokens, att)),
        in_specs=[SMEM] + [VMEM] * group,
        out_specs=VMEM,
        compiler_params=params(32),
        cost_estimate=LITTLE,
        name="place",
    )(position, *heads)

    mine = []
    for chunk in range(chunks):
        rows = after(recv[chunk], pieces[0]) if chunk else recv[chunk]
        planes = [rows]
        for other in range(1, seq_count):
            pairs = [(i, i ^ other) for i in range(seq_count)]
            planes.append(lax.ppermute(rows, "seq", pairs))
        total = seq_count * exp_count * step
        pieces = pl.pallas_call(
            functools.partial(ffn_kernel, chunk * experts, seq_count),
            out_shape=[shape((exp_count, step, features))] * seq_count,
            in_specs=[VMEM] * seq_count + [ANY] * 3,
            out_specs=[VMEM] * seq_count,
            scratch_shapes=[
                pltpu.VMEM((experts * 3, hidden, features), BF16),
                pltpu.VMEM((total, features), BF16),
                pltpu.VMEM((total, features), F32),
                pltpu.SemaphoreType.DMA((experts * 3,)),
            ],
            compiler_params=params(44),
            cost_estimate=LITTLE,
            name="experts",
        )(*planes, gate_proj, up_proj, down_proj)
        summed = pieces[0].astype(F32)
        for other in range(1, seq_count):
            pairs = [(i, i ^ other) for i in range(seq_count)]
            summed = summed + lax.ppermute(pieces[other], "seq", pairs).astype(F32)
        mine.append(summed.astype(BF16))
    back = [lax.all_to_all(rows, "exp", 0, 0, tiled=True) for rows in mine]
    expert_mix = pl.pallas_call(
        mix_kernel,
        out_shape=shape((local_tokens, features)),
        in_specs=[VMEM] * (2 + chunks),
        out_specs=VMEM,
        scratch_shapes=[pltpu.VMEM((EXPERTS * CAP, features), F32)],
        compiler_params=params(32),
        cost_estimate=LITTLE,
        name="mix",
    )(expert_ids, route_weights, *back)
    return (attention, expert_mix)


def solution(mesh):
    return jax.shard_map(
        on_device,
        mesh=mesh,
        in_specs=(
            P(("seq", "exp"), None),
            P(),
            P(("seq", "exp"), None),
            P(("seq", "exp"), None),
            P(("seq", "exp"), None),
            P(("seq", "exp"), None),
            P(("seq", "exp"), None),
            P("exp", "seq", None),
            P("exp", "seq", None),
            P("exp", "seq", None),
        ),
        out_specs=(P(("seq", "exp"), None), P(("seq", "exp"), None)),
        check_vma=False,
    )
```

profile of v0, /device:TPU:0, one launch (start us, length us, event | category | flops | bytes accessed | tf_op | source)
XLA Modules:
  0.0 159.6 jit_solution(10832246487192147189)
XLA Ops:
  3.2 1.5 prep.1
  4.7 21.6 %all_to_all.25.refs_0_ = bf16[16,4,4096]{2,1,0:T(4,128)(2,1)S(1)} all-to-all(bf16[16,4,4096]{2,1,0:T(4,128)(2,1)S(1)} %get-tuple-element.20), channel_id=1, replica_groups=mesh['seq'=2,'exp'=16] {'exp'}, dimensions={0} | all-to-all | bytes 1048576 | tf_op jit(solution)/shard_map/all_to_all | solution.py:285
  26.3 1.5 collective-permute-start.9
  27.8 12.3 %collective-permute-done.9.refs_1_ = bf16[16,4,4096]{2,1,0:T(4,128)(2,1)S(1)} collective-permute-done((bf16[16,4,4096]{2,1,0:T(4,128)(2,1)S(1)}, bf16[16,4,4096]{2,1,0:T(4,128)(2,1)S(1)}, u32[]{:S(2)}, u32[]{:S(2)}) %collective-permute-start.9) | collective-permute-done | bytes 524320 | tf_op jit(solution)/shard_map/ppermute | solution.py:324
  40.1 14.7 %experts.2 = (bf16[16,4,4096]{2,1,0:T(4,128)(2,1)S(1)}, bf16[16,4,4096]{2,1,0:T(4,128)(2,1)S(1)}) custom-call(bf16[16,4,4096]{2,1,0:T(4,128)(2,1)S(1)} %all_to_all.25.refs_0_, bf16[16,4,4096]{2,1,0:T(4,128)(2,1)S(1)} %collective-permute-done.9.refs_1_, bf16[4,704,4096]{2,1,0:T(8,128)(2,1)} %refs_2_.3, bf16[4,704,4096]{2,1,0:T(8,128)(2,1)} %refs_3_.3, ...), custom_call_target="tpu_custom_call" | custom-call | flops 1000 | bytes 1000 | tf_op jit(solution)/shard_map/experts/pallas_call | solution.py:326
  54.8 1.6 collective-permute-start.10
  56.4 4.4 %all-to-all-start.1 = ((bf16[16,4,4096]{2,1,0:T(4,128)(2,1)}), bf16[16,4,4096]{2,1,0:T(4,128)(2,1)S(1)}, u32[]{:S(2)}, u32[]{:S(2)}) async-start(bf16[16,4,4096]{2,1,0:T(4,128)(2,1)} %get-tuple-element.23), calls=%async_computation.1 | async-start | bytes 1048576 | tf_op jit(solution)/shard_map/all_to_all | solution.py:285
  60.8 7.1 %collective-permute-done.10 = bf16[16,4,4096]{2,1,0:T(4,128)(2,1)S(1)} collective-permute-done((bf16[16,4,4096]{2,1,0:T(4,128)(2,1)S(1)}, bf16[16,4,4096]{2,1,0:T(4,128)(2,1)S(1)}, u32[]{:S(2)}, u32[]{:S(2)}) %collective-permute-start.10) | collective-permute-done | bytes 524320 | tf_op jit(solution)/shard_map/ppermute | solution.py:344
  69.0 6.2 %all-to-all-done.1.refs_0_ = bf16[16,4,4096]{2,1,0:T(4,128)(2,1)S(1)} async-done(((bf16[16,4,4096]{2,1,0:T(4,128)(2,1)}), bf16[16,4,4096]{2,1,0:T(4,128)(2,1)S(1)}, u32[]{:S(2)}, u32[]{:S(2)}) %all-to-all-start.1) | async-done | bytes 524320 | tf_op jit(solution)/shard_map/all_to_all | solution.py:285
  75.3 4.1 %all-to-all-start.3 = ((bf16[16,4,4096]{2,1,0:T(4,128)(2,1)}), bf16[16,4,4096]{2,1,0:T(4,128)(2,1)S(1)}, u32[]{:S(2)}, u32[]{:S(2)}) async-start(bf16[16,4,4096]{2,1,0:T(4,128)(2,1)} %add_convert_fusion.1), calls=%async_computation.3 | async-start | bytes 1048576 | tf_op jit(solution)/shard_map/all_to_all | solution.py:346
  79.6 2.9 %collective-permute-start = (bf16[16,2048]{1,0:T(8,128)(2,1)S(1)}, bf16[16,2048]{1,0:T(8,128)(2,1)S(1)}, u32[]{:S(2)}, u32[]{:S(2)}) collective-permute-start(bf16[16,2048]{1,0:T(8,128)(2,1)S(1)} %sums.1), channel_id=1, source_target_pairs={{0,8},{1,9},{2,10},{3,11},{4,12},{5,13},{6,14},{7,15},{8,0},{9,1},... | collective-permute-start | bytes 196616 | tf_op jit(solution)/shard_map/ppermute | solution.py:266
  83.0 14.5 %collective-permute-done = bf16[16,2048]{1,0:T(8,128)(2,1)S(1)} collective-permute-done((bf16[16,2048]{1,0:T(8,128)(2,1)S(1)}, bf16[16,2048]{1,0:T(8,128)(2,1)S(1)}, u32[]{:S(2)}, u32[]{:S(2)}) %collective-permute-start) | collective-permute-done | bytes 65568 | tf_op jit(solution)/shard_map/ppermute | solution.py:266
  98.0 4.5 %collective-permute-done.1.refs_1_ = bf16[32,2048]{1,0:T(8,128)(2,1)S(1)} collective-permute-done((bf16[32,2048]{1,0:T(8,128)(2,1)S(1)}, bf16[32,2048]{1,0:T(8,128)(2,1)S(1)}, u32[]{:S(2)}, u32[]{:S(2)}) %collective-permute-start.1) | collective-permute-done | bytes 131104 | tf_op jit(solution)/shard_map/ppermute | solution.py:270
  103.6 3.7 %all-to-all-start.2 = ((bf16[8,256,256]{2,1,0:T(8,128)(2,1)}), bf16[8,256,256]{2,1,0:T(8,128)(2,1)S(1)}, u32[]{:S(2)}, u32[]{:S(2)}) async-start(bf16[8,256,256]{2,1,0:T(8,128)(2,1)} %pack.1), calls=%async_computation.2 | async-start | bytes 2097152 | tf_op jit(solution)/shard_map/all_to_all | solution.py:288
  107.4 14.3 %experts.3 = (bf16[16,4,4096]{2,1,0:T(4,128)(2,1)S(1)}, bf16[16,4,4096]{2,1,0:T(4,128)(2,1)S(1)}) custom-call(bf16[16,4,4096]{2,1,0:T(4,128)(2,1)S(1)} %all-to-all-done.1.refs_0_, bf16[16,4,4096]{2,1,0:T(4,128)(2,1)S(1)} %collective-permute-done.11.refs_1_, bf16[4,704,4096]{2,1,0:T(8,128)(2,1)} %refs_2_.3, bf16[4,704,4096]{2,1,0:T(8,128)(2,1)} %refs_3_.3, ...), custom_call_target="tpu_custom_call" | custom-call | flops 1000 | bytes 1000 | tf_op jit(solution)/shard_map/experts/pallas_call | solution.py:326
  122.3 13.5 %collective-permute-done.12 = bf16[16,4,4096]{2,1,0:T(4,128)(2,1)S(1)} collective-permute-done((bf16[16,4,4096]{2,1,0:T(4,128)(2,1)S(1)}, bf16[16,4,4096]{2,1,0:T(4,128)(2,1)S(1)}, u32[]{:S(2)}, u32[]{:S(2)}) %collective-permute-start.12) | collective-permute-done | bytes 524320 | tf_op jit(solution)/shard_map/ppermute | solution.py:344
  136.9 4.2 %all-to-all-start.4 = ((bf16[16,4,4096]{2,1,0:T(4,128)(2,1)}), bf16[16,4,4096]{2,1,0:T(4,128)(2,1)S(1)}, u32[]{:S(2)}, u32[]{:S(2)}) async-start(bf16[16,4,4096]{2,1,0:T(4,128)(2,1)} %add_convert_fusion), calls=%async_computation.4 | async-start | bytes 1048576 | tf_op jit(solution)/shard_map/all_to_all | solution.py:346
  141.2 3.2 %attend.1 = (bf16[64,256]{1,0:T(8,128)(2,1)S(1)}, bf16[64,256]{1,0:T(8,128)(2,1)S(1)}, bf16[64,256]{1,0:T(8,128)(2,1)S(1)}, bf16[64,256]{1,0:T(8,128)(2,1)S(1)},...) custom-call(s32[2]{0:T(128)S(1)} %pad_add_fusion.at_ref, ...), custom_call_target="tpu_custom_call" | custom-call | flops 1000 | bytes 1000 | tf_op jit(solution)/shard_map/attend/pallas_call | solution.py:292
  144.8 1.7 %collective-permute-start.3 = (bf16[64,256]{1,0:T(8,128)(2,1)S(1)}, bf16[64,256]{1,0:T(8,128)(2,1)S(1)}, u32[]{:S(2)}, u32[]{:S(2)}) collective-permute-start(bf16[64,256]{1,0:T(8,128)(2,1)S(1)} %get-tuple-element.27), channel_id=1, source_target_pairs={{0,2},{1,3},{2,0},{3,1},{4,6},{5,7},{6,4},{7,5},{8,10},{9,11},{10,... | collective-permute-start | bytes 98312 | tf_op jit(solution)/shard_map/ppermute | solution.py:305
  146.5 1.7 %collective-permute-start.5 = (bf16[64,256]{1,0:T(8,128)(2,1)S(1)}, bf16[64,256]{1,0:T(8,128)(2,1)S(1)}, u32[]{:S(2)}, u32[]{:S(2)}) collective-permute-start(bf16[64,256]{1,0:T(8,128)(2,1)S(1)} %get-tuple-element.29), channel_id=1, source_target_pairs={{0,4},{1,5},{2,6},{3,7},{4,0},{5,1},{6,2},{7,3},{8,12},{9,13},{10,... | collective-permute-start | bytes 98312 | tf_op jit(solution)/shard_map/ppermute | solution.py:305
  148.3 2.6 %collective-permute-start.7 = (bf16[64,256]{1,0:T(8,128)(2,1)S(1)}, bf16[64,256]{1,0:T(8,128)(2,1)S(1)}, u32[]{:S(2)}, u32[]{:S(2)}) collective-permute-start(bf16[64,256]{1,0:T(8,128)(2,1)S(1)} %get-tuple-element.31), channel_id=1, source_target_pairs={{0,6},{1,7},{2,4},{3,5},{4,2},{5,3},{6,0},{7,1},{8,14},{9,15},{10,... | collective-permute-start | bytes 98312 | tf_op jit(solution)/shard_map/ppermute | solution.py:305
  152.6 2.7 %collective-permute-done.7.refs_6_ = bf16[64,256]{1,0:T(8,128)(2,1)S(1)} collective-permute-done((bf16[64,256]{1,0:T(8,128)(2,1)S(1)}, bf16[64,256]{1,0:T(8,128)(2,1)S(1)}, u32[]{:S(2)}, u32[]{:S(2)}) %collective-permute-start.7) | collective-permute-done | bytes 32800 | tf_op jit(solution)/shard_map/ppermute | solution.py:305
  155.3 1.4 collective-permute-done.8.refs_7_
  157.9 1.6 %mix.1 = bf16[64,4096]{1,0:T(8,128)(2,1)} custom-call(s32[64,2]{1,0:T(8,128)S(1)} %copy.12.ids_ref, f32[64,2]{1,0:T(8,128)S(1)} %copy.14.weight_ref, bf16[16,4,4096]{2,1,0:T(4,128)(2,1)S(1)} %all-to-all-done.3.refs_0_, bf16[16,4,4096]{2,1,0:T(4,128)(2,1)S(1)} %all-to-all-done.4.refs_1_), custom_call_target="tpu_custom_call" | custom-call | flops 1000 | bytes 1000 | tf_op jit(solution)/shard_map/mix/pallas_call | solution.py:347
  (37 shorter events, 11.2 us)
Async XLA Ops:
  1.4 1.0 copy-start.2
  2.4 0.7 copy-start.4
  26.3 53.1 %copy-start = (bf16[64,2048]{1,0:T(8,128)(2,1)S(1)}, bf16[64,2048]{1,0:T(8,128)(2,1)}, u32[]{:S(2)}) copy-start(bf16[64,2048]{1,0:T(8,128)(2,1)} %k_ref.2) | copy-start | bytes 786436
  26.3 53.1 %copy-start.1 = (bf16[64,2048]{1,0:T(8,128)(2,1)S(1)}, bf16[64,2048]{1,0:T(8,128)(2,1)}, u32[]{:S(2)}) copy-start(bf16[64,2048]{1,0:T(8,128)(2,1)} %v_ref.3) | copy-start | bytes 786436
  26.3 76.3 %copy-start.3 = (bf16[64,2048]{1,0:T(8,128)(2,1)S(1)}, bf16[64,2048]{1,0:T(8,128)(2,1)}, u32[]{:S(2)}) copy-start(bf16[64,2048]{1,0:T(8,128)(2,1)} %q_ref.1) | copy-start | bytes 786436
  26.3 13.8 %collective-permute-start.9 = (bf16[16,4,4096]{2,1,0:T(4,128)(2,1)S(1)}, bf16[16,4,4096]{2,1,0:T(4,128)(2,1)S(1)}, u32[]{:S(2)}, u32[]{:S(2)}) collective-permute-start(bf16[16,4,4096]{2,1,0:T(4,128)(2,1)S(1)} %all_to_all.25.refs_0_), channel_id=1, source_target_pairs={{0,16},{16,0},{1,17},{17,1},{2,18},{18,2},{3,19},{19,3},{4,20},{20... | collective-permute-start | bytes 1572872 | tf_op jit(solution)/shard_map/ppermute | solution.py:324
  54.8 13.1 %collective-permute-start.10 = (bf16[16,4,4096]{2,1,0:T(4,128)(2,1)S(1)}, bf16[16,4,4096]{2,1,0:T(4,128)(2,1)S(1)}, u32[]{:S(2)}, u32[]{:S(2)}) collective-permute-start(bf16[16,4,4096]{2,1,0:T(4,128)(2,1)S(1)} %get-tuple-element.34), channel_id=1, source_target_pairs={{0,16},{16,0},{1,17},{17,1},{2,18},{18,2},{3,19},{19,3},{4,20},{20... | collective-permute-start | bytes 1572872 | tf_op jit(solution)/shard_map/ppermute | solution.py:344
  56.4 18.8 %all-to-all-start.1 = ((bf16[16,4,4096]{2,1,0:T(4,128)(2,1)}), bf16[16,4,4096]{2,1,0:T(4,128)(2,1)S(1)}, u32[]{:S(2)}, u32[]{:S(2)}) async-start(bf16[16,4,4096]{2,1,0:T(4,128)(2,1)} %get-tuple-element.23), calls=%async_computation.1 | async-start | bytes 1048576 | tf_op jit(solution)/shard_map/all_to_all | solution.py:285
  75.3 28.4 %all-to-all-start.3 = ((bf16[16,4,4096]{2,1,0:T(4,128)(2,1)}), bf16[16,4,4096]{2,1,0:T(4,128)(2,1)S(1)}, u32[]{:S(2)}, u32[]{:S(2)}) async-start(bf16[16,4,4096]{2,1,0:T(4,128)(2,1)} %add_convert_fusion.1), calls=%async_computation.3 | async-start | bytes 1048576 | tf_op jit(solution)/shard_map/all_to_all | solution.py:346
  79.6 17.9 %collective-permute-start = (bf16[16,2048]{1,0:T(8,128)(2,1)S(1)}, bf16[16,2048]{1,0:T(8,128)(2,1)S(1)}, u32[]{:S(2)}, u32[]{:S(2)}) collective-permute-start(bf16[16,2048]{1,0:T(8,128)(2,1)S(1)} %sums.1), channel_id=1, source_target_pairs={{0,8},{1,9},{2,10},{3,11},{4,12},{5,13},{6,14},{7,15},{8,0},{9,1},... | collective-permute-start | bytes 196616 | tf_op jit(solution)/shard_map/ppermute | solution.py:266
  82.5 24.9 %collective-permute-start.11 = (bf16[16,4,4096]{2,1,0:T(4,128)(2,1)S(1)}, bf16[16,4,4096]{2,1,0:T(4,128)(2,1)S(1)}, u32[]{:S(2)}, u32[]{:S(2)}) collective-permute-start(bf16[16,4,4096]{2,1,0:T(4,128)(2,1)S(1)} %all-to-all-done.1.refs_0_), channel_id=1, source_target_pairs={{0,16},{16,0},{1,17},{17,1},{2,18},{18,2},{3,19},{19,3},{4,20},{20... | collective-permute-start | bytes 1572872 | tf_op jit(solution)/shard_map/ppermute | solution.py:324
  97.5 5.1 %collective-permute-start.1 = (bf16[32,2048]{1,0:T(8,128)(2,1)S(1)}, bf16[32,2048]{1,0:T(8,128)(2,1)S(1)}, u32[]{:S(2)}, u32[]{:S(2)}) collective-permute-start(bf16[32,2048]{1,0:T(8,128)(2,1)S(1)} %pad_maximum_fusion.refs_0_), channel_id=1, source_target_pairs={{0,16},{16,0},{1,17},{17,1},{2,18},{18,2},{3,19},{19,3},{4,20},{20... | collective-permute-start | bytes 393224 | tf_op jit(solution)/shard_map/ppermute | solution.py:270
  103.6 33.2 %all-to-all-start.2 = ((bf16[8,256,256]{2,1,0:T(8,128)(2,1)}), bf16[8,256,256]{2,1,0:T(8,128)(2,1)S(1)}, u32[]{:S(2)}, u32[]{:S(2)}) async-start(bf16[8,256,256]{2,1,0:T(8,128)(2,1)} %pack.1), calls=%async_computation.2 | async-start | bytes 2097152 | tf_op jit(solution)/shard_map/all_to_all | solution.py:288
  107.4 44.6 %copy-start.5 = (f32[64,2]{0,1:T(2,128)S(1)}, f32[64,2]{0,1:T(2,128)}, u32[]{:S(2)}) copy-start(f32[64,2]{0,1:T(2,128)} %param.16) | copy-start | bytes 1540
  121.7 14.1 %collective-permute-start.12 = (bf16[16,4,4096]{2,1,0:T(4,128)(2,1)S(1)}, bf16[16,4,4096]{2,1,0:T(4,128)(2,1)S(1)}, u32[]{:S(2)}, u32[]{:S(2)}) collective-permute-start(bf16[16,4,4096]{2,1,0:T(4,128)(2,1)S(1)} %get-tuple-element.37), channel_id=1, source_target_pairs={{0,16},{16,0},{1,17},{17,1},{2,18},{18,2},{3,19},{19,3},{4,20},{20... | collective-permute-start | bytes 1572872 | tf_op jit(solution)/shard_map/ppermute | solution.py:344
  136.9 21.1 %all-to-all-start.4 = ((bf16[16,4,4096]{2,1,0:T(4,128)(2,1)}), bf16[16,4,4096]{2,1,0:T(4,128)(2,1)S(1)}, u32[]{:S(2)}, u32[]{:S(2)}) async-start(bf16[16,4,4096]{2,1,0:T(4,128)(2,1)} %add_convert_fusion), calls=%async_computation.4 | async-start | bytes 1048576 | tf_op jit(solution)/shard_map/all_to_all | solution.py:346
  144.4 3.9 %collective-permute-start.2 = (bf16[64,256]{1,0:T(8,128)(2,1)S(1)}, bf16[64,256]{1,0:T(8,128)(2,1)S(1)}, u32[]{:S(2)}, u32[]{:S(2)}) collective-permute-start(bf16[64,256]{1,0:T(8,128)(2,1)S(1)} %get-tuple-element.26), channel_id=1, source_target_pairs={{0,1},{1,0},{2,3},{3,2},{4,5},{5,4},{6,7},{7,6},{8,9},{9,8},{10,11... | collective-permute-start | bytes 98312 | tf_op jit(solution)/shard_map/ppermute | solution.py:305
  144.8 6.1 %collective-permute-start.3 = (bf16[64,256]{1,0:T(8,128)(2,1)S(1)}, bf16[64,256]{1,0:T(8,128)(2,1)S(1)}, u32[]{:S(2)}, u32[]{:S(2)}) collective-permute-start(bf16[64,256]{1,0:T(8,128)(2,1)S(1)} %get-tuple-element.27), channel_id=1, source_target_pairs={{0,2},{1,3},{2,0},{3,1},{4,6},{5,7},{6,4},{7,5},{8,10},{9,11},{10,... | collective-permute-start | bytes 98312 | tf_op jit(solution)/shard_map/ppermute | solution.py:305
  146.5 5.5 %collective-permute-start.4 = (bf16[64,256]{1,0:T(8,128)(2,1)S(1)}, bf16[64,256]{1,0:T(8,128)(2,1)S(1)}, u32[]{:S(2)}, u32[]{:S(2)}) collective-permute-start(bf16[64,256]{1,0:T(8,128)(2,1)S(1)} %get-tuple-element.28), channel_id=1, source_target_pairs={{0,3},{1,2},{2,1},{3,0},{4,7},{5,6},{6,5},{7,4},{8,11},{9,10},{10,... | collective-permute-start | bytes 98312 | tf_op jit(solution)/shard_map/ppermute | solution.py:305
  146.5 5.5 %collective-permute-start.5 = (bf16[64,256]{1,0:T(8,128)(2,1)S(1)}, bf16[64,256]{1,0:T(8,128)(2,1)S(1)}, u32[]{:S(2)}, u32[]{:S(2)}) collective-permute-start(bf16[64,256]{1,0:T(8,128)(2,1)S(1)} %get-tuple-element.29), channel_id=1, source_target_pairs={{0,4},{1,5},{2,6},{3,7},{4,0},{5,1},{6,2},{7,3},{8,12},{9,13},{10,... | collective-permute-start | bytes 98312 | tf_op jit(solution)/shard_map/ppermute | solution.py:305
  148.2 4.4 %collective-permute-start.6 = (bf16[64,256]{1,0:T(8,128)(2,1)S(1)}, bf16[64,256]{1,0:T(8,128)(2,1)S(1)}, u32[]{:S(2)}, u32[]{:S(2)}) collective-permute-start(bf16[64,256]{1,0:T(8,128)(2,1)S(1)} %get-tuple-element.30), channel_id=1, source_target_pairs={{0,5},{1,4},{2,7},{3,6},{4,1},{5,0},{6,3},{7,2},{8,13},{9,12},{10,... | collective-permute-start | bytes 98312 | tf_op jit(solution)/shard_map/ppermute | solution.py:305
  148.3 6.9 %collective-permute-start.7 = (bf16[64,256]{1,0:T(8,128)(2,1)S(1)}, bf16[64,256]{1,0:T(8,128)(2,1)S(1)}, u32[]{:S(2)}, u32[]{:S(2)}) collective-permute-start(bf16[64,256]{1,0:T(8,128)(2,1)S(1)} %get-tuple-element.31), channel_id=1, source_target_pairs={{0,6},{1,7},{2,4},{3,5},{4,2},{5,3},{6,0},{7,1},{8,14},{9,15},{10,... | collective-permute-start | bytes 98312 | tf_op jit(solution)/shard_map/ppermute | solution.py:305
  150.9 5.8 %collective-permute-start.8 = (bf16[64,256]{1,0:T(8,128)(2,1)S(1)}, bf16[64,256]{1,0:T(8,128)(2,1)S(1)}, u32[]{:S(2)}, u32[]{:S(2)}) collective-permute-start(bf16[64,256]{1,0:T(8,128)(2,1)S(1)} %get-tuple-element.32), channel_id=1, source_target_pairs={{0,7},{1,6},{2,5},{3,4},{4,3},{5,2},{6,1},{7,0},{8,15},{9,14},{10,... | collective-permute-start | bytes 98312 | tf_op jit(solution)/shard_map/ppermute | solution.py:305
where the time goes:
time: 160 us
  waiting for transfers between devices  62.9 us (39%)
  Pallas kernels  37.8 us (24%)
  starting transfers between devices  31.6 us (20%)
  blocking collectives  21.6 us (14%)
  local copies, waits for them, and re-layouts  2.64 us (2%)
  other arithmetic  2.28 us (1%)
    pallas_call x2, Pallas kernels, on_device(): pl.pallas_call(functools.partial(ffn_kernel, chunk * experts, seq_count),...  28.9 us
    all_to_all x1, blocking collectives, on_device(): recv.append(lax.all_to_all(rows, 'exp', 0, 0, tiled=True))  21.6 us
    ppermute x2, waiting for transfers between devices, on_device(): summed = summed + lax.ppermute(pieces[other], 'seq', pairs).astype(F32)  20.6 us
    ppermute x1, waiting for transfers between devices, on_device(): lax.ppermute(sums, 'exp', [(i, i ^ group) for i in range(exp_count)])  14.5 us
    ppermute x2, waiting for transfers between devices, on_device(): planes.append(lax.ppermute(rows, 'seq', pairs))  12.3 us
    all_to_all x2, starting transfers between devices, on_device(): back = [lax.all_to_all(rows, 'exp', 0, 0, tiled=True) for rows in mine]  8.28 us
    ppermute x7, starting transfers between devices, on_device(): lax.ppermute(rows, 'exp', [(i, i ^ other) for i in range(exp_count)])  7.56 us
    all_to_all x1, waiting for transfers between devices, on_device(): recv.append(lax.all_to_all(rows, 'exp', 0, 0, tiled=True))  6.25 us
  transfers between devices with their start and end apart: 17, of which 9 were waited for; matrix products, arithmetic and copies ran while one was open for 1% of the time, Pallas kernels for 13%

commit v1 on v0

--- a/solution.py
+++ b/solution.py
@@ -281,7 +281,7 @@
     recv = []
     for rows in send:
         if recv:
-            rows = after(rows, recv[-1])
+            rows = after(after(rows, recv[-1]), parts)
         recv.append(lax.all_to_all(rows, "exp", 0, 0, tiled=True))
     packed = after(packed, recv[-1])
     halves = [[half * group + j for j in range(group)] for half in range(SEG_DEV)]
@@ -289,39 +289,12 @@
     segment = lax.axis_index("seq") * SEG_DEV + lax.axis_index("exp") // group
     place = lax.axis_index("exp") % group
     position = jnp.stack([segment, place]).astype(jnp.int32)
-    head_out = pl.pallas_call(
-        functools.partial(attend_kernel, min(256, seg_len), local_tokens, segs),
-        out_shape=[shape((local_tokens, width))] * group,
-        in_specs=[SMEM, VMEM],
-        out_specs=[VMEM] * group,
-        scratch_shapes=[pltpu.VMEM((group, local_tokens, width), BF16)],
-        compiler_params=params(48),
-        cost_estimate=LITTLE,
-        name="attend",
-    )(position, got)
-    heads = [
-        rows
-        if other == 0
-        else lax.ppermute(rows, "exp", [(i, i ^ other) for i in range(exp_count)])
-        for other, rows in enumerate(head_out)
-    ]
-    attention = pl.pallas_call(
-        place_kernel,
-        out_shape=shape((local_tokens, att)),
-        in_specs=[SMEM] + [VMEM] * group,
-        out_specs=VMEM,
-        compiler_params=params(32),
-        cost_estimate=LITTLE,
-        name="place",
-    )(position, *heads)
-
-    mine = []
+    done, mine = [], []
     for chunk in range(chunks):
-        rows = after(recv[chunk], pieces[0]) if chunk else recv[chunk]
-        planes = [rows]
+        planes = [after(recv[chunk], recv[-1])]
         for other in range(1, seq_count):
             pairs = [(i, i ^ other) for i in range(seq_count)]
-            planes.append(lax.ppermute(rows, "seq", pairs))
+            planes.append(lax.ppermute(recv[chunk], "seq", pairs))
         total = seq_count * exp_count * step
         pieces = pl.pallas_call(
             functools.partial(ffn_kernel, chunk * experts, seq_count),
@@ -338,11 +311,40 @@
             cost_estimate=LITTLE,
             name="experts",
         )(*planes, gate_proj, up_proj, down_proj)
-        summed = pieces[0].astype(F32)
+        done.append(pieces)
+    for chunk, pieces in enumerate(done):
+        summed = after(pieces[0], done[-1][0]).astype(F32)
         for other in range(1, seq_count):
             pairs = [(i, i ^ other) for i in range(seq_count)]
             summed = summed + lax.ppermute(pieces[other], "seq", pairs).astype(F32)
         mine.append(summed.astype(BF16))
+    got = after(got, mine[0])
+    head_out = pl.pallas_call(
+        functools.partial(attend_kernel, min(256, seg_len), local_tokens, segs),
+        out_shape=[shape((local_tokens, width))] * group,
+        in_specs=[SMEM, VMEM],
+        out_specs=[VMEM] * group,
+        scratch_shapes=[pltpu.VMEM((group, local_tokens, width), BF16)],
+        compiler_params=params(48),
+        cost_estimate=LITTLE,
+        name="attend",
+    )(position, got)
+    heads = [
+        rows
+        if other == 0
+        else lax.ppermute(rows, "exp", [(i, i ^ other) for i in range(exp_count)])
+        for other, rows in enumerate(head_out)
+    ]
+    attention = pl.pallas_call(
+        place_kernel,
+        out_shape=shape((local_tokens, att)),
+        in_specs=[SMEM] + [VMEM] * group,
+        out_specs=VMEM,
+        compiler_params=params(32),
+        cost_estimate=LITTLE,
+        name="place",
+    )(position, *heads)
+
     back = [lax.all_to_all(rows, "exp", 0, 0, tiled=True) for rows in mine]
     expert_mix = pl.pallas_call(
         mix_kernel,

time: 160 us -> 151 us (0.944)
  blocking collectives: 21.6 us -> 0 us
  starting transfers between devices: 31.6 us -> 42.4 us
  local copies, waits for them, and re-layouts: 2.64 us -> 4.54 us
    all_to_all x1 -> x0, blocking collectives: 21.6 us -> none  [on_device(): recv.append(lax.all_to_all(rows, 'exp', 0, 0, tiled=True))]
    all_to_all x2, waiting for transfers between devices: 0.01 us -> 13.4 us  [on_device(): back = [lax.all_to_all(rows, 'exp', 0, 0, tiled=True) for rows in mine]]
    ppermute x2, waiting for transfers between devices: 12.3 us -> 0.01 us  [on_device(): planes.append(lax.ppermute(recv[chunk], 'seq', pairs))]
    ppermute x2, waiting for transfers between devices: 20.6 us -> 13.6 us  [on_device(): summed = summed + lax.ppermute(pieces[other], 'seq', pairs).astype(F32)]
    all_to_all x1 -> x2, starting transfers between devices: 4.37 us -> 11.2 us  [on_device(): recv.append(lax.all_to_all(rows, 'exp', 0, 0, tiled=True))]
    all_to_all x1 -> x2, waiting for transfers between devices: 6.25 us -> 12.9 us  [on_device(): recv.append(lax.all_to_all(rows, 'exp', 0, 0, tiled=True))]
    all_to_all x2, starting transfers between devices: 8.28 us -> 10.7 us  [on_device(): back = [lax.all_to_all(rows, 'exp', 0, 0, tiled=True) for rows in mine]]
    unnamed x14 -> x18, local copies, waits for them, and re-layouts: 2.64 us -> 4.54 us
  transfers between devices with their start and end apart: 17 -> 18, of which waited for: 9 -> 8; matrix products, arithmetic and copies ran while one was open for 1% -> 1% of each run, Pallas kernels for 13% -> 23%
where the time goes in v1:
time: 151 us
  waiting for transfers between devices  62.4 us (41%)
  starting transfers between devices  42.4 us (28%)
  Pallas kernels  38.1 us (25%)
  local copies, waits for them, and re-layouts  4.54 us (3%)
  other arithmetic  2.26 us (1%)
    pallas_call x2, Pallas kernels, on_device(): pl.pallas_call(functools.partial(ffn_kernel, chunk * experts, seq_count),...  29.1 us
    ppermute x2, waiting for transfers between devices, on_device(): summed = summed + lax.ppermute(pieces[other], 'seq', pairs).astype(F32)  13.6 us
    all_to_all x2, waiting for transfers between devices, on_device(): back = [lax.all_to_all(rows, 'exp', 0, 0, tiled=True) for rows in mine]  13.4 us
    ppermute x1, waiting for transfers between devices, on_device(): lax.ppermute(sums, 'exp', [(i, i ^ group) for i in range(exp_count)])  13.1 us
    all_to_all x2, waiting for transfers between devices, on_device(): recv.append(lax.all_to_all(rows, 'exp', 0, 0, tiled=True))  12.9 us
    all_to_all x2, starting transfers between devices, on_device(): recv.append(lax.all_to_all(rows, 'exp', 0, 0, tiled=True))  11.2 us
    all_to_all x2, starting transfers between devices, on_device(): back = [lax.all_to_all(rows, 'exp', 0, 0, tiled=True) for rows in mine]  10.7 us
    ppermute x7, starting transfers between devices, on_device(): lax.ppermute(rows, 'exp', [(i, i ^ other) for i in range(exp_count)])  8.2 us
  transfers between devices with their start and end apart: 18, of which 8 were waited for; matrix products, arithmetic and copies ran while one was open for 1% of the time, Pallas kernels for 23%

profile of v1, /device:TPU:0, one launch (start us, length us, event | category | flops | bytes accessed | tf_op | source)
XLA Modules:
  0.0 150.6 jit_solution(2320927542748854700)
XLA Ops:
  3.2 1.7 %prep.1 = (bf16[16,4,4096]{2,1,0:T(4,128)(2,1)}, bf16[16,4,4096]{2,1,0:T(4,128)(2,1)}) custom-call(bf16[64,4096]{1,0:T(8,128)(2,1)S(1)} %copy-done.4, f32[1,4096]{1,0:T(1,128)S(1)} %bitcast.3, s32[64,2]{1,0:T(8,128)S(1)} %copy.12.ids_ref), custom_call_target="tpu_custom_call" | custom-call | flops 1000 | bytes 1000 | tf_op jit(solution)/shard_map/prep/pallas_call | solution.py:246
  4.9 7.4 %all-to-all-start = ((bf16[16,4,4096]{2,1,0:T(4,128)(2,1)}), bf16[16,4,4096]{2,1,0:T(4,128)(2,1)S(1)}, u32[]{:S(2)}, u32[]{:S(2)}) async-start(bf16[16,4,4096]{2,1,0:T(4,128)(2,1)} %get-tuple-element.25), calls=%async_computation | async-start | bytes 1048576 | tf_op jit(solution)/shard_map/all_to_all | solution.py:285
  14.3 2.9 %collective-permute-start = (bf16[16,2048]{1,0:T(8,128)(2,1)S(1)}, bf16[16,2048]{1,0:T(8,128)(2,1)S(1)}, u32[]{:S(2)}, u32[]{:S(2)}) collective-permute-start(bf16[16,2048]{1,0:T(8,128)(2,1)S(1)} %sums.1), channel_id=1, source_target_pairs={{0,8},{1,9},{2,10},{3,11},{4,12},{5,13},{6,14},{7,15},{8,0},{9,1},... | collective-permute-start | bytes 196616 | tf_op jit(solution)/shard_map/ppermute | solution.py:266
  17.2 13.1 %collective-permute-done = bf16[16,2048]{1,0:T(8,128)(2,1)S(1)} collective-permute-done((bf16[16,2048]{1,0:T(8,128)(2,1)S(1)}, bf16[16,2048]{1,0:T(8,128)(2,1)S(1)}, u32[]{:S(2)}, u32[]{:S(2)}) %collective-permute-start) | collective-permute-done | bytes 65568 | tf_op jit(solution)/shard_map/ppermute | solution.py:266
  30.3 1.6 %collective-permute-start.1 = (bf16[32,2048]{1,0:T(8,128)(2,1)S(1)}, bf16[32,2048]{1,0:T(8,128)(2,1)S(1)}, u32[]{:S(2)}, u32[]{:S(2)}) collective-permute-start(bf16[32,2048]{1,0:T(8,128)(2,1)S(1)} %pad_maximum_fusion.refs_0_), channel_id=1, source_target_pairs={{0,16},{16,0},{1,17},{17,1},{2,18},{18,2},{3,19},{19,3},{4,20},{20... | collective-permute-start | bytes 393224 | tf_op jit(solution)/shard_map/ppermute | solution.py:270
  31.9 3.5 %collective-permute-done.1.refs_1_ = bf16[32,2048]{1,0:T(8,128)(2,1)S(1)} collective-permute-done((bf16[32,2048]{1,0:T(8,128)(2,1)S(1)}, bf16[32,2048]{1,0:T(8,128)(2,1)S(1)}, u32[]{:S(2)}, u32[]{:S(2)}) %collective-permute-start.1) | collective-permute-done | bytes 131104 | tf_op jit(solution)/shard_map/ppermute | solution.py:270
  35.4 3.8 %all-to-all-start.1 = ((bf16[16,4,4096]{2,1,0:T(4,128)(2,1)}), bf16[16,4,4096]{2,1,0:T(4,128)(2,1)S(1)}, u32[]{:S(2)}, u32[]{:S(2)}) async-start(bf16[16,4,4096]{2,1,0:T(4,128)(2,1)} %get-tuple-element.29), calls=%async_computation.1 | async-start | bytes 1048576 | tf_op jit(solution)/shard_map/all_to_all | solution.py:285
  39.3 1.6 %collective-permute-start.2 = (bf16[16,4,4096]{2,1,0:T(4,128)(2,1)S(1)}, bf16[16,4,4096]{2,1,0:T(4,128)(2,1)S(1)}, u32[]{:S(2)}, u32[]{:S(2)}) collective-permute-start(bf16[16,4,4096]{2,1,0:T(4,128)(2,1)S(1)} %all-to-all-done.refs_0_), channel_id=1, source_target_pairs={{0,16},{16,0},{1,17},{17,1},{2,18},{18,2},{3,19},{19,3},{4,20},{20... | collective-permute-start | bytes 1572872 | tf_op jit(solution)/shard_map/ppermute | solution.py:297
  40.8 12.9 %all-to-all-done.1.refs_0_ = bf16[16,4,4096]{2,1,0:T(4,128)(2,1)S(1)} async-done(((bf16[16,4,4096]{2,1,0:T(4,128)(2,1)}), bf16[16,4,4096]{2,1,0:T(4,128)(2,1)S(1)}, u32[]{:S(2)}, u32[]{:S(2)}) %all-to-all-start.1) | async-done | bytes 524320 | tf_op jit(solution)/shard_map/all_to_all | solution.py:285
  53.7 1.5 %collective-permute-start.3 = (bf16[16,4,4096]{2,1,0:T(4,128)(2,1)S(1)}, bf16[16,4,4096]{2,1,0:T(4,128)(2,1)S(1)}, u32[]{:S(2)}, u32[]{:S(2)}) collective-permute-start(bf16[16,4,4096]{2,1,0:T(4,128)(2,1)S(1)} %all-to-all-done.1.refs_0_), channel_id=1, source_target_pairs={{0,16},{16,0},{1,17},{17,1},{2,18},{18,2},{3,19},{19,3},{4,20},{20... | collective-permute-start | bytes 1572872 | tf_op jit(solution)/shard_map/ppermute | solution.py:297
  55.2 14.7 %experts.2 = (bf16[16,4,4096]{2,1,0:T(4,128)(2,1)S(1)}, bf16[16,4,4096]{2,1,0:T(4,128)(2,1)S(1)}) custom-call(bf16[16,4,4096]{2,1,0:T(4,128)(2,1)S(1)} %all-to-all-done.refs_0_, bf16[16,4,4096]{2,1,0:T(4,128)(2,1)S(1)} %collective-permute-done.2.refs_1_, bf16[4,704,4096]{2,1,0:T(8,128)(2,1)} %refs_2_.3, bf16[4,704,4096]{2,1,0:T(8,128)(2,1)} %refs_3_.3, ...), custom_call_target="tpu_custom_call" | custom-call | flops 1000 | bytes 1000 | tf_op jit(solution)/shard_map/experts/pallas_call | solution.py:299
  70.5 14.4 %experts.3 = (bf16[16,4,4096]{2,1,0:T(4,128)(2,1)S(1)}, bf16[16,4,4096]{2,1,0:T(4,128)(2,1)S(1)}) custom-call(bf16[16,4,4096]{2,1,0:T(4,128)(2,1)S(1)} %all-to-all-done.1.refs_0_, bf16[16,4,4096]{2,1,0:T(4,128)(2,1)S(1)} %collective-permute-done.3.refs_1_, bf16[4,704,4096]{2,1,0:T(8,128)(2,1)} %refs_2_.3, bf16[4,704,4096]{2,1,0:T(8,128)(2,1)} %refs_3_.3, ...), custom_call_target="tpu_custom_call" | custom-call | flops 1000 | bytes 1000 | tf_op jit(solution)/shard_map/experts/pallas_call | solution.py:299
  86.1 5.0 %all-to-all-start.3 = ((bf16[16,4,4096]{2,1,0:T(4,128)(2,1)}), bf16[16,4,4096]{2,1,0:T(4,128)(2,1)S(1)}, u32[]{:S(2)}, u32[]{:S(2)}) async-start(bf16[16,4,4096]{2,1,0:T(4,128)(2,1)} %add_convert_fusion.1), calls=%async_computation.3 | async-start | bytes 1048576 | tf_op jit(solution)/shard_map/all_to_all | solution.py:348
  92.2 13.4 %all-to-all-done.3.refs_0_ = bf16[16,4,4096]{2,1,0:T(4,128)(2,1)S(1)} async-done(((bf16[16,4,4096]{2,1,0:T(4,128)(2,1)}), bf16[16,4,4096]{2,1,0:T(4,128)(2,1)S(1)}, u32[]{:S(2)}, u32[]{:S(2)}) %all-to-all-start.3) | async-done | bytes 524320 | tf_op jit(solution)/shard_map/all_to_all | solution.py:348
  105.6 3.6 %all-to-all-start.2 = ((bf16[8,256,256]{2,1,0:T(8,128)(2,1)}), bf16[8,256,256]{2,1,0:T(8,128)(2,1)S(1)}, u32[]{:S(2)}, u32[]{:S(2)}) async-start(bf16[8,256,256]{2,1,0:T(8,128)(2,1)} %pack.1), calls=%async_computation.2 | async-start | bytes 2097152 | tf_op jit(solution)/shard_map/all_to_all | solution.py:288
  109.8 13.6 %collective-permute-done.12 = bf16[16,4,4096]{2,1,0:T(4,128)(2,1)S(1)} collective-permute-done((bf16[16,4,4096]{2,1,0:T(4,128)(2,1)S(1)}, bf16[16,4,4096]{2,1,0:T(4,128)(2,1)S(1)}, u32[]{:S(2)}, u32[]{:S(2)}) %collective-permute-start.12) | collective-permute-done | bytes 524320 | tf_op jit(solution)/shard_map/ppermute | solution.py:319
  124.5 5.7 %all-to-all-start.4 = ((bf16[16,4,4096]{2,1,0:T(4,128)(2,1)}), bf16[16,4,4096]{2,1,0:T(4,128)(2,1)S(1)}, u32[]{:S(2)}, u32[]{:S(2)}) async-start(bf16[16,4,4096]{2,1,0:T(4,128)(2,1)} %add_convert_fusion), calls=%async_computation.4 | async-start | bytes 1048576 | tf_op jit(solution)/shard_map/all_to_all | solution.py:348
  130.2 3.2 %attend.1 = (bf16[64,256]{1,0:T(8,128)(2,1)S(1)}, bf16[64,256]{1,0:T(8,128)(2,1)S(1)}, bf16[64,256]{1,0:T(8,128)(2,1)S(1)}, bf16[64,256]{1,0:T(8,128)(2,1)S(1)},...) custom-call(s32[2]{0:T(128)S(1)} %pad_add_fusion.at_ref, ...), custom_call_target="tpu_custom_call" | custom-call | flops 1000 | bytes 1000 | tf_op jit(solution)/shard_map/attend/pallas_call | solution.py:322
  133.4 2.9 %collective-permute-start.10 = (bf16[64,256]{1,0:T(8,128)(2,1)S(1)}, bf16[64,256]{1,0:T(8,128)(2,1)S(1)}, u32[]{:S(2)}, u32[]{:S(2)}) collective-permute-start(bf16[64,256]{1,0:T(8,128)(2,1)S(1)} %get-tuple-element.44), channel_id=1, source_target_pairs={{0,6},{1,7},{2,4},{3,5},{4,2},{5,3},{6,0},{7,1},{8,14},{9,15},{10,... | collective-permute-start | bytes 98312 | tf_op jit(solution)/shard_map/ppermute | solution.py:335
  136.6 1.9 %collective-permute-start.6 = (bf16[64,256]{1,0:T(8,128)(2,1)S(1)}, bf16[64,256]{1,0:T(8,128)(2,1)S(1)}, u32[]{:S(2)}, u32[]{:S(2)}) collective-permute-start(bf16[64,256]{1,0:T(8,128)(2,1)S(1)} %get-tuple-element.40), channel_id=1, source_target_pairs={{0,2},{1,3},{2,0},{3,1},{4,6},{5,7},{6,4},{7,5},{8,10},{9,11},{10,... | collective-permute-start | bytes 98312 | tf_op jit(solution)/shard_map/ppermute | solution.py:335
  138.4 2.7 %collective-permute-done.10.refs_6_ = bf16[64,256]{1,0:T(8,128)(2,1)S(1)} collective-permute-done((bf16[64,256]{1,0:T(8,128)(2,1)S(1)}, bf16[64,256]{1,0:T(8,128)(2,1)S(1)}, u32[]{:S(2)}, u32[]{:S(2)}) %collective-permute-start.10) | collective-permute-done | bytes 32800 | tf_op jit(solution)/shard_map/ppermute | solution.py:335
  141.1 3.2 %collective-permute-start.8 = (bf16[64,256]{1,0:T(8,128)(2,1)S(1)}, bf16[64,256]{1,0:T(8,128)(2,1)S(1)}, u32[]{:S(2)}, u32[]{:S(2)}) collective-permute-start(bf16[64,256]{1,0:T(8,128)(2,1)S(1)} %get-tuple-element.42), channel_id=1, source_target_pairs={{0,4},{1,5},{2,6},{3,7},{4,0},{5,1},{6,2},{7,3},{8,12},{9,13},{10,... | collective-permute-start | bytes 98312 | tf_op jit(solution)/shard_map/ppermute | solution.py:335
  144.5 1.8 %collective-permute-done.8.refs_4_ = bf16[64,256]{1,0:T(8,128)(2,1)S(1)} collective-permute-done((bf16[64,256]{1,0:T(8,128)(2,1)S(1)}, bf16[64,256]{1,0:T(8,128)(2,1)S(1)}, u32[]{:S(2)}, u32[]{:S(2)}) %collective-permute-start.8) | collective-permute-done | bytes 32800 | tf_op jit(solution)/shard_map/ppermute | solution.py:335
  148.9 1.6 %mix.1 = bf16[64,4096]{1,0:T(8,128)(2,1)} custom-call(s32[64,2]{1,0:T(8,128)S(1)} %copy.12.ids_ref, f32[64,2]{1,0:T(8,128)S(1)} %copy.14.weight_ref, bf16[16,4,4096]{2,1,0:T(4,128)(2,1)S(1)} %all-to-all-done.3.refs_0_, bf16[16,4,4096]{2,1,0:T(4,128)(2,1)S(1)} %all-to-all-done.4.refs_1_), custom_call_target="tpu_custom_call" | custom-call | flops 1000 | bytes 1000 | tf_op jit(solution)/shard_map/mix/pallas_call | solution.py:349
  (42 shorter events, 12.3 us)
Async XLA Ops:
  1.4 1.0 copy-start.4
  4.9 27.1 %all-to-all-start = ((bf16[16,4,4096]{2,1,0:T(4,128)(2,1)}), bf16[16,4,4096]{2,1,0:T(4,128)(2,1)S(1)}, u32[]{:S(2)}, u32[]{:S(2)}) async-start(bf16[16,4,4096]{2,1,0:T(4,128)(2,1)} %get-tuple-element.25), calls=%async_computation | async-start | bytes 1048576 | tf_op jit(solution)/shard_map/all_to_all | solution.py:285
  12.2 1.0 copy-start
  14.3 16.0 %collective-permute-start = (bf16[16,2048]{1,0:T(8,128)(2,1)S(1)}, bf16[16,2048]{1,0:T(8,128)(2,1)S(1)}, u32[]{:S(2)}, u32[]{:S(2)}) collective-permute-start(bf16[16,2048]{1,0:T(8,128)(2,1)S(1)} %sums.1), channel_id=1, source_target_pairs={{0,8},{1,9},{2,10},{3,11},{4,12},{5,13},{6,14},{7,15},{8,0},{9,1},... | collective-permute-start | bytes 196616 | tf_op jit(solution)/shard_map/ppermute | solution.py:266
  30.3 5.1 %collective-permute-start.1 = (bf16[32,2048]{1,0:T(8,128)(2,1)S(1)}, bf16[32,2048]{1,0:T(8,128)(2,1)S(1)}, u32[]{:S(2)}, u32[]{:S(2)}) collective-permute-start(bf16[32,2048]{1,0:T(8,128)(2,1)S(1)} %pad_maximum_fusion.refs_0_), channel_id=1, source_target_pairs={{0,16},{16,0},{1,17},{17,1},{2,18},{18,2},{3,19},{19,3},{4,20},{20... | collective-permute-start | bytes 393224 | tf_op jit(solution)/shard_map/ppermute | solution.py:270
  35.4 18.3 %all-to-all-start.1 = ((bf16[16,4,4096]{2,1,0:T(4,128)(2,1)}), bf16[16,4,4096]{2,1,0:T(4,128)(2,1)S(1)}, u32[]{:S(2)}, u32[]{:S(2)}) async-start(bf16[16,4,4096]{2,1,0:T(4,128)(2,1)} %get-tuple-element.29), calls=%async_computation.1 | async-start | bytes 1048576 | tf_op jit(solution)/shard_map/all_to_all | solution.py:285
  39.3 16.0 %collective-permute-start.2 = (bf16[16,4,4096]{2,1,0:T(4,128)(2,1)S(1)}, bf16[16,4,4096]{2,1,0:T(4,128)(2,1)S(1)}, u32[]{:S(2)}, u32[]{:S(2)}) collective-permute-start(bf16[16,4,4096]{2,1,0:T(4,128)(2,1)S(1)} %all-to-all-done.refs_0_), channel_id=1, source_target_pairs={{0,16},{16,0},{1,17},{17,1},{2,18},{18,2},{3,19},{19,3},{4,20},{20... | collective-permute-start | bytes 1572872 | tf_op jit(solution)/shard_map/ppermute | solution.py:297
  53.7 16.8 %collective-permute-start.3 = (bf16[16,4,4096]{2,1,0:T(4,128)(2,1)S(1)}, bf16[16,4,4096]{2,1,0:T(4,128)(2,1)S(1)}, u32[]{:S(2)}, u32[]{:S(2)}) collective-permute-start(bf16[16,4,4096]{2,1,0:T(4,128)(2,1)S(1)} %all-to-all-done.1.refs_0_), channel_id=1, source_target_pairs={{0,16},{16,0},{1,17},{17,1},{2,18},{18,2},{3,19},{19,3},{4,20},{20... | collective-permute-start | bytes 1572872 | tf_op jit(solution)/shard_map/ppermute | solution.py:297
  69.9 21.2 %copy-start.1 = (bf16[64,2048]{1,0:T(8,128)(2,1)S(1)}, bf16[64,2048]{1,0:T(8,128)(2,1)}, u32[]{:S(2)}) copy-start(bf16[64,2048]{1,0:T(8,128)(2,1)} %k_ref.2) | copy-start | bytes 786436
  69.9 21.2 %copy-start.3 = (bf16[64,2048]{1,0:T(8,128)(2,1)S(1)}, bf16[64,2048]{1,0:T(8,128)(2,1)}, u32[]{:S(2)}) copy-start(bf16[64,2048]{1,0:T(8,128)(2,1)} %v_ref.3) | copy-start | bytes 786436
  69.9 21.2 %copy-start.5 = (bf16[64,2048]{1,0:T(8,128)(2,1)S(1)}, bf16[64,2048]{1,0:T(8,128)(2,1)}, u32[]{:S(2)}) copy-start(bf16[64,2048]{1,0:T(8,128)(2,1)} %q_ref.1) | copy-start | bytes 786436
  70.0 74.4 %copy-start.7 = (f32[64,2]{0,1:T(2,128)S(1)}, f32[64,2]{0,1:T(2,128)}, u32[]{:S(2)}) copy-start(f32[64,2]{0,1:T(2,128)} %param.16) | copy-start | bytes 1540
  70.0 15.0 %collective-permute-start.4 = (bf16[16,4,4096]{2,1,0:T(4,128)(2,1)S(1)}, bf16[16,4,4096]{2,1,0:T(4,128)(2,1)S(1)}, u32[]{:S(2)}, u32[]{:S(2)}) collective-permute-start(bf16[16,4,4096]{2,1,0:T(4,128)(2,1)S(1)} %get-tuple-element.36), channel_id=1, source_target_pairs={{0,16},{16,0},{1,17},{17,1},{2,18},{18,2},{3,19},{19,3},{4,20},{20... | collective-permute-start | bytes 1572872 | tf_op jit(solution)/shard_map/ppermute | solution.py:319
  86.1 19.5 %all-to-all-start.3 = ((bf16[16,4,4096]{2,1,0:T(4,128)(2,1)}), bf16[16,4,4096]{2,1,0:T(4,128)(2,1)S(1)}, u32[]{:S(2)}, u32[]{:S(2)}) async-start(bf16[16,4,4096]{2,1,0:T(4,128)(2,1)} %add_convert_fusion.1), calls=%async_computation.3 | async-start | bytes 1048576 | tf_op jit(solution)/shard_map/all_to_all | solution.py:348
  105.6 18.9 %all-to-all-start.2 = ((bf16[8,256,256]{2,1,0:T(8,128)(2,1)}), bf16[8,256,256]{2,1,0:T(8,128)(2,1)S(1)}, u32[]{:S(2)}, u32[]{:S(2)}) async-start(bf16[8,256,256]{2,1,0:T(8,128)(2,1)} %pack.1), calls=%async_computation.2 | async-start | bytes 2097152 | tf_op jit(solution)/shard_map/all_to_all | solution.py:288
  109.1 14.2 %collective-permute-start.12 = (bf16[16,4,4096]{2,1,0:T(4,128)(2,1)S(1)}, bf16[16,4,4096]{2,1,0:T(4,128)(2,1)S(1)}, u32[]{:S(2)}, u32[]{:S(2)}) collective-permute-start(bf16[16,4,4096]{2,1,0:T(4,128)(2,1)S(1)} %get-tuple-element.47), channel_id=1, source_target_pairs={{0,16},{16,0},{1,17},{17,1},{2,18},{18,2},{3,19},{19,3},{4,20},{20... | collective-permute-start | bytes 1572872 | tf_op jit(solution)/shard_map/ppermute | solution.py:319
  124.5 24.5 %all-to-all-start.4 = ((bf16[16,4,4096]{2,1,0:T(4,128)(2,1)}), bf16[16,4,4096]{2,1,0:T(4,128)(2,1)S(1)}, u32[]{:S(2)}, u32[]{:S(2)}) async-start(bf16[16,4,4096]{2,1,0:T(4,128)(2,1)} %add_convert_fusion), calls=%async_computation.4 | async-start | bytes 1048576 | tf_op jit(solution)/shard_map/all_to_all | solution.py:348
  133.4 7.7 %collective-permute-start.10 = (bf16[64,256]{1,0:T(8,128)(2,1)S(1)}, bf16[64,256]{1,0:T(8,128)(2,1)S(1)}, u32[]{:S(2)}, u32[]{:S(2)}) collective-permute-start(bf16[64,256]{1,0:T(8,128)(2,1)S(1)} %get-tuple-element.44), channel_id=1, source_target_pairs={{0,6},{1,7},{2,4},{3,5},{4,2},{5,3},{6,0},{7,1},{8,14},{9,15},{10,... | collective-permute-start | bytes 98312 | tf_op jit(solution)/shard_map/ppermute | solution.py:335
  136.3 8.0 %collective-permute-start.11 = (bf16[64,256]{1,0:T(8,128)(2,1)S(1)}, bf16[64,256]{1,0:T(8,128)(2,1)S(1)}, u32[]{:S(2)}, u32[]{:S(2)}) collective-permute-start(bf16[64,256]{1,0:T(8,128)(2,1)S(1)} %get-tuple-element.45), channel_id=1, source_target_pairs={{0,7},{1,6},{2,5},{3,4},{4,3},{5,2},{6,1},{7,0},{8,15},{9,14},{10,... | collective-permute-start | bytes 98312 | tf_op jit(solution)/shard_map/ppermute | solution.py:335
  136.3 8.1 %collective-permute-start.5 = (bf16[64,256]{1,0:T(8,128)(2,1)S(1)}, bf16[64,256]{1,0:T(8,128)(2,1)S(1)}, u32[]{:S(2)}, u32[]{:S(2)}) collective-permute-start(bf16[64,256]{1,0:T(8,128)(2,1)S(1)} %get-tuple-element.39), channel_id=1, source_target_pairs={{0,1},{1,0},{2,3},{3,2},{4,5},{5,4},{6,7},{7,6},{8,9},{9,8},{10,11... | collective-permute-start | bytes 98312 | tf_op jit(solution)/shard_map/ppermute | solution.py:335
  136.6 7.9 %collective-permute-start.6 = (bf16[64,256]{1,0:T(8,128)(2,1)S(1)}, bf16[64,256]{1,0:T(8,128)(2,1)S(1)}, u32[]{:S(2)}, u32[]{:S(2)}) collective-permute-start(bf16[64,256]{1,0:T(8,128)(2,1)S(1)} %get-tuple-element.40), channel_id=1, source_target_pairs={{0,2},{1,3},{2,0},{3,1},{4,6},{5,7},{6,4},{7,5},{8,10},{9,11},{10,... | collective-permute-start | bytes 98312 | tf_op jit(solution)/shard_map/ppermute | solution.py:335
  138.4 6.0 %collective-permute-start.7 = (bf16[64,256]{1,0:T(8,128)(2,1)S(1)}, bf16[64,256]{1,0:T(8,128)(2,1)S(1)}, u32[]{:S(2)}, u32[]{:S(2)}) collective-permute-start(bf16[64,256]{1,0:T(8,128)(2,1)S(1)} %get-tuple-element.41), channel_id=1, source_target_pairs={{0,3},{1,2},{2,1},{3,0},{4,7},{5,6},{6,5},{7,4},{8,11},{9,10},{10,... | collective-permute-start | bytes 98312 | tf_op jit(solution)/shard_map/ppermute | solution.py:335
  141.1 5.1 %collective-permute-start.8 = (bf16[64,256]{1,0:T(8,128)(2,1)S(1)}, bf16[64,256]{1,0:T(8,128)(2,1)S(1)}, u32[]{:S(2)}, u32[]{:S(2)}) collective-permute-start(bf16[64,256]{1,0:T(8,128)(2,1)S(1)} %get-tuple-element.42), channel_id=1, source_target_pairs={{0,4},{1,5},{2,6},{3,7},{4,0},{5,1},{6,2},{7,3},{8,12},{9,13},{10,... | collective-permute-start | bytes 98312 | tf_op jit(solution)/shard_map/ppermute | solution.py:335
  144.3 3.3 %collective-permute-start.9 = (bf16[64,256]{1,0:T(8,128)(2,1)S(1)}, bf16[64,256]{1,0:T(8,128)(2,1)S(1)}, u32[]{:S(2)}, u32[]{:S(2)}) collective-permute-start(bf16[64,256]{1,0:T(8,128)(2,1)S(1)} %get-tuple-element.43), channel_id=1, source_target_pairs={{0,5},{1,4},{2,7},{3,6},{4,1},{5,0},{6,3},{7,2},{8,13},{9,12},{10,... | collective-permute-start | bytes 98312 | tf_op jit(solution)/shard_map/ppermute | solution.py:335
  (2 other events, 1.7 us)

commit v2 on v1

--- a/solution.py
+++ b/solution.py
@@ -281,7 +281,7 @@
     recv = []
     for rows in send:
         if recv:
-            rows = after(after(rows, recv[-1]), parts)
+            rows = after(rows, recv[-1])
         recv.append(lax.all_to_all(rows, "exp", 0, 0, tiled=True))
     packed = after(packed, recv[-1])
     halves = [[half * group + j for j in range(group)] for half in range(SEG_DEV)]
@@ -291,7 +291,7 @@
     position = jnp.stack([segment, place]).astype(jnp.int32)
     done, mine = [], []
     for chunk in range(chunks):
-        planes = [after(recv[chunk], recv[-1])]
+        planes = [after(after(recv[chunk], recv[-1]), parts)]
         for other in range(1, seq_count):
             pairs = [(i, i ^ other) for i in range(seq_count)]
             planes.append(lax.ppermute(recv[chunk], "seq", pairs))
@@ -313,7 +313,7 @@
         )(*planes, gate_proj, up_proj, down_proj)
         done.append(pieces)
     for chunk, pieces in enumerate(done):
-        summed = after(pieces[0], done[-1][0]).astype(F32)
+        summed = after(after(pieces[0], done[-1][0]), got).astype(F32)
         for other in range(1, seq_count):
             pairs = [(i, i ^ other) for i in range(seq_count)]
             summed = summed + lax.ppermute(pieces[other], "seq", pairs).astype(F32)
@@ -345,6 +345,7 @@
         name="place",
     )(position, *heads)
 
+    mine[-1] = after(mine[-1], head_out[0])
     back = [lax.all_to_all(rows, "exp", 0, 0, tiled=True) for rows in mine]
     expert_mix = pl.pallas_call(
         mix_kernel,

time: 151 us -> 150 us (level)
  blocking collectives: 0 us -> 21.6 us
  waiting for transfers between devices: 62.4 us -> 46.1 us
  starting transfers between devices: 42.4 us -> 31.4 us
  other arithmetic: 2.26 us -> 4.36 us
  Pallas kernels: 38.1 us -> 39.7 us
    all_to_all x0 -> x1, blocking collectives: none -> 21.6 us  [on_device(): recv.append(lax.all_to_all(rows, 'exp', 0, 0, tiled=True))]
    all_to_all x2 -> x1, waiting for transfers between devices: 12.9 us -> 0.01 us  [on_device(): recv.append(lax.all_to_all(rows, 'exp', 0, 0, tiled=True))]
    ppermute x2, waiting for transfers between devices: 0.01 us -> 12.7 us  [on_device(): planes.append(lax.ppermute(recv[chunk], 'seq', pairs))]
    ppermute x2, waiting for transfers between devices: 13.6 us -> 2.49 us  [on_device(): summed = summed + lax.ppermute(pieces[other], 'seq', pairs).astype(F32)]
    all_to_all x2 -> x1, starting transfers between devices: 11.2 us -> 4.1 us  [on_device(): recv.append(lax.all_to_all(rows, 'exp', 0, 0, tiled=True))]
    all_to_all x2, waiting for transfers between devices: 13.4 us -> 6.55 us  [on_device(): back = [lax.all_to_all(rows, 'exp', 0, 0, tiled=True) for rows in mine]]
    all_to_all x2, starting transfers between devices: 10.7 us -> 8.5 us  [on_device(): back = [lax.all_to_all(rows, 'exp', 0, 0, tiled=True) for rows in mine]]
    convert_element_type x2, other arithmetic: 2.17 us -> 4.28 us  [on_device(): mine.append(summed.astype(BF16))]
  transfers between devices with their start and end apart: 18 -> 17, of which waited for: 8 -> 8; matrix products, arithmetic and copies ran while one was open for 1% -> 3% of each run, Pallas kernels for 23% -> 24%
where the time goes in v2:
time: 150 us; the launch traced here: 149 us
  waiting for transfers between devices  46.1 us (31%)
  Pallas kernels  39.7 us (26%)
  starting transfers between devices  31.4 us (21%)
  blocking collectives  21.6 us (14%)
  local copies, waits for them, and re-layouts  5.47 us (4%)
  other arithmetic  4.36 us (3%)
    pallas_call x2, Pallas kernels, on_device(): pl.pallas_call(functools.partial(ffn_kernel, chunk * experts, seq_count),...  30.8 us
    all_to_all x1, blocking collectives, on_device(): recv.append(lax.all_to_all(rows, 'exp', 0, 0, tiled=True))  21.6 us
    ppermute x1, waiting for transfers between devices, on_device(): lax.ppermute(sums, 'exp', [(i, i ^ group) for i in range(exp_count)])  13.1 us
    ppermute x2, waiting for transfers between devices, on_device(): planes.append(lax.ppermute(recv[chunk], 'seq', pairs))  12.7 us
    all_to_all x2, starting transfers between devices, on_device(): back = [lax.all_to_all(rows, 'exp', 0, 0, tiled=True) for rows in mine]  8.5 us
    ppermute x7, waiting for transfers between devices, on_device(): lax.ppermute(rows, 'exp', [(i, i ^ other) for i in range(exp_count)])  7.7 us
    all_to_all x2, waiting for transfers between devices, on_device(): back = [lax.all_to_all(rows, 'exp', 0, 0, tiled=True) for rows in mine]  6.55 us
    ppermute x7, starting transfers between devices, on_device(): lax.ppermute(rows, 'exp', [(i, i ^ other) for i in range(exp_count)])  6.49 us
  transfers between devices with their start and end apart: 17, of which 8 were waited for; matrix products, arithmetic and copies ran while one was open for 3% of the time, Pallas kernels for 24%

profile of v2, /device:TPU:0, one launch (start us, length us, event | category | flops | bytes accessed | tf_op | source)
XLA Modules:
  0.0 149.3 jit_solution(4394358470762691923)
XLA Ops:
  4.7 21.6 %all_to_all.25.refs_0_ = bf16[16,4,4096]{2,1,0:T(4,128)(2,1)S(1)} all-to-all(bf16[16,4,4096]{2,1,0:T(4,128)(2,1)S(1)} %get-tuple-element.29), channel_id=1, replica_groups=mesh['seq'=2,'exp'=16] {'exp'}, dimensions={0} | all-to-all | bytes 1048576 | tf_op jit(solution)/shard_map/all_to_all | solution.py:285
  26.3 4.1 %all-to-all-start.1 = ((bf16[16,4,4096]{2,1,0:T(4,128)(2,1)}), bf16[16,4,4096]{2,1,0:T(4,128)(2,1)S(1)}, u32[]{:S(2)}, u32[]{:S(2)}) async-start(bf16[16,4,4096]{2,1,0:T(4,128)(2,1)} %get-tuple-element.32), calls=%async_computation.1 | async-start | bytes 1048576 | tf_op jit(solution)/shard_map/all_to_all | solution.py:285
  32.5 2.9 %collective-permute-start = (bf16[16,2048]{1,0:T(8,128)(2,1)S(1)}, bf16[16,2048]{1,0:T(8,128)(2,1)S(1)}, u32[]{:S(2)}, u32[]{:S(2)}) collective-permute-start(bf16[16,2048]{1,0:T(8,128)(2,1)S(1)} %sums.1), channel_id=1, source_target_pairs={{0,8},{1,9},{2,10},{3,11},{4,12},{5,13},{6,14},{7,15},{8,0},{9,1},... | collective-permute-start | bytes 196616 | tf_op jit(solution)/shard_map/ppermute | solution.py:266
  35.4 13.1 %collective-permute-done = bf16[16,2048]{1,0:T(8,128)(2,1)S(1)} collective-permute-done((bf16[16,2048]{1,0:T(8,128)(2,1)S(1)}, bf16[16,2048]{1,0:T(8,128)(2,1)S(1)}, u32[]{:S(2)}, u32[]{:S(2)}) %collective-permute-start) | collective-permute-done | bytes 65568 | tf_op jit(solution)/shard_map/ppermute | solution.py:266
  48.5 1.6 %collective-permute-start.1 = (bf16[32,2048]{1,0:T(8,128)(2,1)S(1)}, bf16[32,2048]{1,0:T(8,128)(2,1)S(1)}, u32[]{:S(2)}, u32[]{:S(2)}) collective-permute-start(bf16[32,2048]{1,0:T(8,128)(2,1)S(1)} %pad_maximum_fusion.refs_0_), channel_id=1, source_target_pairs={{0,16},{16,0},{1,17},{17,1},{2,18},{18,2},{3,19},{19,3},{4,20},{20... | collective-permute-start | bytes 393224 | tf_op jit(solution)/shard_map/ppermute | solution.py:270
  50.1 3.5 %collective-permute-done.1.refs_1_ = bf16[32,2048]{1,0:T(8,128)(2,1)S(1)} collective-permute-done((bf16[32,2048]{1,0:T(8,128)(2,1)S(1)}, bf16[32,2048]{1,0:T(8,128)(2,1)S(1)}, u32[]{:S(2)}, u32[]{:S(2)}) %collective-permute-start.1) | collective-permute-done | bytes 131104 | tf_op jit(solution)/shard_map/ppermute | solution.py:270
  55.6 3.6 %all-to-all-start.2 = ((bf16[8,256,256]{2,1,0:T(8,128)(2,1)}), bf16[8,256,256]{2,1,0:T(8,128)(2,1)S(1)}, u32[]{:S(2)}, u32[]{:S(2)}) async-start(bf16[8,256,256]{2,1,0:T(8,128)(2,1)} %pack.1), calls=%async_computation.2 | async-start | bytes 2097152 | tf_op jit(solution)/shard_map/all_to_all | solution.py:288
  59.2 1.6 %collective-permute-start.2 = (bf16[16,4,4096]{2,1,0:T(4,128)(2,1)S(1)}, bf16[16,4,4096]{2,1,0:T(4,128)(2,1)S(1)}, u32[]{:S(2)}, u32[]{:S(2)}) collective-permute-start(bf16[16,4,4096]{2,1,0:T(4,128)(2,1)S(1)} %all_to_all.25.refs_0_), channel_id=1, source_target_pairs={{0,16},{16,0},{1,17},{17,1},{2,18},{18,2},{3,19},{19,3},{4,20},{20... | collective-permute-start | bytes 1572872 | tf_op jit(solution)/shard_map/ppermute | solution.py:297
  61.3 12.7 %collective-permute-done.2.refs_1_ = bf16[16,4,4096]{2,1,0:T(4,128)(2,1)S(1)} collective-permute-done((bf16[16,4,4096]{2,1,0:T(4,128)(2,1)S(1)}, bf16[16,4,4096]{2,1,0:T(4,128)(2,1)S(1)}, u32[]{:S(2)}, u32[]{:S(2)}) %collective-permute-start.2) | collective-permute-done | bytes 524320 | tf_op jit(solution)/shard_map/ppermute | solution.py:297
  74.0 15.4 %experts.2 = (bf16[16,4,4096]{2,1,0:T(4,128)(2,1)S(1)}, bf16[16,4,4096]{2,1,0:T(4,128)(2,1)}) custom-call(bf16[16,4,4096]{2,1,0:T(4,128)(2,1)S(1)} %all_to_all.25.refs_0_, bf16[16,4,4096]{2,1,0:T(4,128)(2,1)S(1)} %collective-permute-done.2.refs_1_, bf16[4,704,4096]{2,1,0:T(8,128)(2,1)} %refs_2_.3, bf16[4,704,4096]{2,1,0:T(8,128)(2,1)} %refs_3_.3, ...), custom_call_target="tpu_custom_call" | custom-call | flops 1000 | bytes 1000 | tf_op jit(solution)/shard_map/experts/pallas_call | solution.py:299
  91.1 15.3 %experts.3 = (bf16[16,4,4096]{2,1,0:T(4,128)(2,1)S(1)}, bf16[16,4,4096]{2,1,0:T(4,128)(2,1)}) custom-call(bf16[16,4,4096]{2,1,0:T(4,128)(2,1)S(1)} %all-to-all-done.1.refs_0_, bf16[16,4,4096]{2,1,0:T(4,128)(2,1)S(1)} %collective-permute-done.3.refs_1_, bf16[4,704,4096]{2,1,0:T(8,128)(2,1)} %refs_2_.3, bf16[4,704,4096]{2,1,0:T(8,128)(2,1)} %refs_3_.3, ...), custom_call_target="tpu_custom_call" | custom-call | flops 1000 | bytes 1000 | tf_op jit(solution)/shard_map/experts/pallas_call | solution.py:299
  107.0 2.1 %add_convert_fusion.1 = bf16[16,4,4096]{2,1,0:T(4,128)(2,1)} fusion(bf16[16,4,4096]{2,1,0:T(4,128)(2,1)} %collective-permute-done.4, bf16[16,4,4096]{2,1,0:T(4,128)(2,1)S(1)} %get-tuple-element.41), kind=kLoop, calls=%fused_computation.1 | loop fusion | flops 1048576 | bytes 1572864 | tf_op jit(solution)/shard_map/convert_element_type | solution.py:320
  109.1 4.4 %all-to-all-start.3 = ((bf16[16,4,4096]{2,1,0:T(4,128)(2,1)}), bf16[16,4,4096]{2,1,0:T(4,128)(2,1)S(1)}, u32[]{:S(2)}, u32[]{:S(2)}) async-start(bf16[16,4,4096]{2,1,0:T(4,128)(2,1)} %add_convert_fusion.1), calls=%async_computation.3 | async-start | bytes 1048576 | tf_op jit(solution)/shard_map/all_to_all | solution.py:349
  113.6 3.2 %attend.1 = (bf16[64,256]{1,0:T(8,128)(2,1)S(1)}, bf16[64,256]{1,0:T(8,128)(2,1)S(1)}, bf16[64,256]{1,0:T(8,128)(2,1)S(1)}, bf16[64,256]{1,0:T(8,128)(2,1)S(1)},...) custom-call(s32[2]{0:T(128)S(1)} %pad_add_fusion.at_ref, ...), custom_call_target="tpu_custom_call" | custom-call | flops 1000 | bytes 1000 | tf_op jit(solution)/shard_map/attend/pallas_call | solution.py:322
  116.8 2.5 %collective-permute-done.12 = bf16[16,4,4096]{2,1,0:T(4,128)(2,1)} collective-permute-done((bf16[16,4,4096]{2,1,0:T(4,128)(2,1)}, bf16[16,4,4096]{2,1,0:T(4,128)(2,1)}, u32[]{:S(2)}, u32[]{:S(2)}) %collective-permute-start.12) | collective-permute-done | bytes 524320 | tf_op jit(solution)/shard_map/ppermute | solution.py:319
  119.3 2.2 %add_convert_fusion = bf16[16,4,4096]{2,1,0:T(4,128)(2,1)} fusion(bf16[16,4,4096]{2,1,0:T(4,128)(2,1)} %collective-permute-done.12, bf16[16,4,4096]{2,1,0:T(4,128)(2,1)S(1)} %get-tuple-element.53), kind=kLoop, calls=%fused_computation | loop fusion | flops 1048576 | bytes 1572864 | tf_op jit(solution)/shard_map/convert_element_type | solution.py:320
  121.4 6.5 %all-to-all-done.3.refs_0_ = bf16[16,4,4096]{2,1,0:T(4,128)(2,1)S(1)} async-done(((bf16[16,4,4096]{2,1,0:T(4,128)(2,1)}), bf16[16,4,4096]{2,1,0:T(4,128)(2,1)S(1)}, u32[]{:S(2)}, u32[]{:S(2)}) %all-to-all-start.3) | async-done | bytes 524320 | tf_op jit(solution)/shard_map/all_to_all | solution.py:349
  128.0 4.1 %all-to-all-start.4 = ((bf16[16,4,4096]{2,1,0:T(4,128)(2,1)}), bf16[16,4,4096]{2,1,0:T(4,128)(2,1)S(1)}, u32[]{:S(2)}, u32[]{:S(2)}) async-start(bf16[16,4,4096]{2,1,0:T(4,128)(2,1)} %add_convert_fusion), calls=%async_computation.4 | async-start | bytes 1048576 | tf_op jit(solution)/shard_map/all_to_all | solution.py:349
  132.5 1.7 %collective-permute-start.6 = (bf16[64,256]{1,0:T(8,128)(2,1)S(1)}, bf16[64,256]{1,0:T(8,128)(2,1)S(1)}, u32[]{:S(2)}, u32[]{:S(2)}) collective-permute-start(bf16[64,256]{1,0:T(8,128)(2,1)S(1)} %get-tuple-element.46), channel_id=1, source_target_pairs={{0,2},{1,3},{2,0},{3,1},{4,6},{5,7},{6,4},{7,5},{8,10},{9,11},{10,... | collective-permute-start | bytes 98312 | tf_op jit(solution)/shard_map/ppermute | solution.py:335
  134.2 1.7 %collective-permute-start.8 = (bf16[64,256]{1,0:T(8,128)(2,1)S(1)}, bf16[64,256]{1,0:T(8,128)(2,1)S(1)}, u32[]{:S(2)}, u32[]{:S(2)}) collective-permute-start(bf16[64,256]{1,0:T(8,128)(2,1)S(1)} %get-tuple-element.48), channel_id=1, source_target_pairs={{0,4},{1,5},{2,6},{3,7},{4,0},{5,1},{6,2},{7,3},{8,12},{9,13},{10,... | collective-permute-start | bytes 98312 | tf_op jit(solution)/shard_map/ppermute | solution.py:335
  136.0 2.6 %collective-permute-start.10 = (bf16[64,256]{1,0:T(8,128)(2,1)S(1)}, bf16[64,256]{1,0:T(8,128)(2,1)S(1)}, u32[]{:S(2)}, u32[]{:S(2)}) collective-permute-start(bf16[64,256]{1,0:T(8,128)(2,1)S(1)} %get-tuple-element.50), channel_id=1, source_target_pairs={{0,6},{1,7},{2,4},{3,5},{4,2},{5,3},{6,0},{7,1},{8,14},{9,15},{10,... | collective-permute-start | bytes 98312 | tf_op jit(solution)/shard_map/ppermute | solution.py:335
  139.4 4.1 %collective-permute-done.8.refs_4_ = bf16[64,256]{1,0:T(8,128)(2,1)S(1)} collective-permute-done((bf16[64,256]{1,0:T(8,128)(2,1)S(1)}, bf16[64,256]{1,0:T(8,128)(2,1)S(1)}, u32[]{:S(2)}, u32[]{:S(2)}) %collective-permute-start.8) | collective-permute-done | bytes 32800 | tf_op jit(solution)/shard_map/ppermute | solution.py:335
  143.5 2.9 %collective-permute-done.10.refs_6_ = bf16[64,256]{1,0:T(8,128)(2,1)S(1)} collective-permute-done((bf16[64,256]{1,0:T(8,128)(2,1)S(1)}, bf16[64,256]{1,0:T(8,128)(2,1)S(1)}, u32[]{:S(2)}, u32[]{:S(2)}) %collective-permute-start.10) | collective-permute-done | bytes 32800 | tf_op jit(solution)/shard_map/ppermute | solution.py:335
  147.7 1.6 %mix.1 = bf16[64,4096]{1,0:T(8,128)(2,1)} custom-call(s32[64,2]{1,0:T(8,128)S(1)} %copy.12.ids_ref, f32[64,2]{1,0:T(8,128)S(1)} %copy.14.weight_ref, bf16[16,4,4096]{2,1,0:T(4,128)(2,1)S(1)} %all-to-all-done.3.refs_0_, bf16[16,4,4096]{2,1,0:T(4,128)(2,1)S(1)} %all-to-all-done.4.refs_1_), custom_call_target="tpu_custom_call" | custom-call | flops 1000 | bytes 1000 | tf_op jit(solution)/shard_map/mix/pallas_call | solution.py:350
  (37 shorter events, 13.5 us)
Async XLA Ops:
  1.4 1.0 copy-start.2
  2.4 0.7 copy-start.4
  26.3 29.3 %all-to-all-start.1 = ((bf16[16,4,4096]{2,1,0:T(4,128)(2,1)}), bf16[16,4,4096]{2,1,0:T(4,128)(2,1)S(1)}, u32[]{:S(2)}, u32[]{:S(2)}) async-start(bf16[16,4,4096]{2,1,0:T(4,128)(2,1)} %get-tuple-element.32), calls=%async_computation.1 | async-start | bytes 1048576 | tf_op jit(solution)/shard_map/all_to_all | solution.py:285
  30.4 1.0 copy-start
  31.4 0.9 copy-start.1
  32.5 16.0 %collective-permute-start = (bf16[16,2048]{1,0:T(8,128)(2,1)S(1)}, bf16[16,2048]{1,0:T(8,128)(2,1)S(1)}, u32[]{:S(2)}, u32[]{:S(2)}) collective-permute-start(bf16[16,2048]{1,0:T(8,128)(2,1)S(1)} %sums.1), channel_id=1, source_target_pairs={{0,8},{1,9},{2,10},{3,11},{4,12},{5,13},{6,14},{7,15},{8,0},{9,1},... | collective-permute-start | bytes 196616 | tf_op jit(solution)/shard_map/ppermute | solution.py:266
  48.5 5.1 %collective-permute-start.1 = (bf16[32,2048]{1,0:T(8,128)(2,1)S(1)}, bf16[32,2048]{1,0:T(8,128)(2,1)S(1)}, u32[]{:S(2)}, u32[]{:S(2)}) collective-permute-start(bf16[32,2048]{1,0:T(8,128)(2,1)S(1)} %pad_maximum_fusion.refs_0_), channel_id=1, source_target_pairs={{0,16},{16,0},{1,17},{17,1},{2,18},{18,2},{3,19},{19,3},{4,20},{20... | collective-permute-start | bytes 393224 | tf_op jit(solution)/shard_map/ppermute | solution.py:270
  53.6 1.0 copy-start.3
  55.6 51.3 %all-to-all-start.2 = ((bf16[8,256,256]{2,1,0:T(8,128)(2,1)}), bf16[8,256,256]{2,1,0:T(8,128)(2,1)S(1)}, u32[]{:S(2)}, u32[]{:S(2)}) async-start(bf16[8,256,256]{2,1,0:T(8,128)(2,1)} %pack.1), calls=%async_computation.2 | async-start | bytes 2097152 | tf_op jit(solution)/shard_map/all_to_all | solution.py:288
  59.2 14.8 %collective-permute-start.2 = (bf16[16,4,4096]{2,1,0:T(4,128)(2,1)S(1)}, bf16[16,4,4096]{2,1,0:T(4,128)(2,1)S(1)}, u32[]{:S(2)}, u32[]{:S(2)}) collective-permute-start(bf16[16,4,4096]{2,1,0:T(4,128)(2,1)S(1)} %all_to_all.25.refs_0_), channel_id=1, source_target_pairs={{0,16},{16,0},{1,17},{17,1},{2,18},{18,2},{3,19},{19,3},{4,20},{20... | collective-permute-start | bytes 1572872 | tf_op jit(solution)/shard_map/ppermute | solution.py:297
  60.8 30.3 %collective-permute-start.3 = (bf16[16,4,4096]{2,1,0:T(4,128)(2,1)S(1)}, bf16[16,4,4096]{2,1,0:T(4,128)(2,1)S(1)}, u32[]{:S(2)}, u32[]{:S(2)}) collective-permute-start(bf16[16,4,4096]{2,1,0:T(4,128)(2,1)S(1)} %all-to-all-done.1.refs_0_), channel_id=1, source_target_pairs={{0,16},{16,0},{1,17},{17,1},{2,18},{18,2},{3,19},{19,3},{4,20},{20... | collective-permute-start | bytes 1572872 | tf_op jit(solution)/shard_map/ppermute | solution.py:297
  89.5 17.5 %collective-permute-start.4 = (bf16[16,4,4096]{2,1,0:T(4,128)(2,1)}, bf16[16,4,4096]{2,1,0:T(4,128)(2,1)}, u32[]{:S(2)}, u32[]{:S(2)}) collective-permute-start(bf16[16,4,4096]{2,1,0:T(4,128)(2,1)} %get-tuple-element.42), channel_id=1, source_target_pairs={{0,16},{16,0},{1,17},{17,1},{2,18},{18,2},{3,19},{19,3},{4,20},{20... | collective-permute-start | bytes 1572872 | tf_op jit(solution)/shard_map/ppermute | solution.py:319
  91.1 48.2 %copy-start.5 = (f32[64,2]{0,1:T(2,128)S(1)}, f32[64,2]{0,1:T(2,128)}, u32[]{:S(2)}) copy-start(f32[64,2]{0,1:T(2,128)} %param.16) | copy-start | bytes 1540
  106.4 12.9 %collective-permute-start.12 = (bf16[16,4,4096]{2,1,0:T(4,128)(2,1)}, bf16[16,4,4096]{2,1,0:T(4,128)(2,1)}, u32[]{:S(2)}, u32[]{:S(2)}) collective-permute-start(bf16[16,4,4096]{2,1,0:T(4,128)(2,1)} %get-tuple-element.54), channel_id=1, source_target_pairs={{0,16},{16,0},{1,17},{17,1},{2,18},{18,2},{3,19},{19,3},{4,20},{20... | collective-permute-start | bytes 1572872 | tf_op jit(solution)/shard_map/ppermute | solution.py:319
  109.1 18.9 %all-to-all-start.3 = ((bf16[16,4,4096]{2,1,0:T(4,128)(2,1)}), bf16[16,4,4096]{2,1,0:T(4,128)(2,1)S(1)}, u32[]{:S(2)}, u32[]{:S(2)}) async-start(bf16[16,4,4096]{2,1,0:T(4,128)(2,1)} %add_convert_fusion.1), calls=%async_computation.3 | async-start | bytes 1048576 | tf_op jit(solution)/shard_map/all_to_all | solution.py:349
  128.0 19.7 %all-to-all-start.4 = ((bf16[16,4,4096]{2,1,0:T(4,128)(2,1)}), bf16[16,4,4096]{2,1,0:T(4,128)(2,1)S(1)}, u32[]{:S(2)}, u32[]{:S(2)}) async-start(bf16[16,4,4096]{2,1,0:T(4,128)(2,1)} %add_convert_fusion), calls=%async_computation.4 | async-start | bytes 1048576 | tf_op jit(solution)/shard_map/all_to_all | solution.py:349
  132.1 3.9 %collective-permute-start.5 = (bf16[64,256]{1,0:T(8,128)(2,1)S(1)}, bf16[64,256]{1,0:T(8,128)(2,1)S(1)}, u32[]{:S(2)}, u32[]{:S(2)}) collective-permute-start(bf16[64,256]{1,0:T(8,128)(2,1)S(1)} %get-tuple-element.45), channel_id=1, source_target_pairs={{0,1},{1,0},{2,3},{3,2},{4,5},{5,4},{6,7},{7,6},{8,9},{9,8},{10,11... | collective-permute-start | bytes 98312 | tf_op jit(solution)/shard_map/ppermute | solution.py:335
  132.5 6.8 %collective-permute-start.6 = (bf16[64,256]{1,0:T(8,128)(2,1)S(1)}, bf16[64,256]{1,0:T(8,128)(2,1)S(1)}, u32[]{:S(2)}, u32[]{:S(2)}) collective-permute-start(bf16[64,256]{1,0:T(8,128)(2,1)S(1)} %get-tuple-element.46), channel_id=1, source_target_pairs={{0,2},{1,3},{2,0},{3,1},{4,6},{5,7},{6,4},{7,5},{8,10},{9,11},{10,... | collective-permute-start | bytes 98312 | tf_op jit(solution)/shard_map/ppermute | solution.py:335
  134.2 5.2 %collective-permute-start.7 = (bf16[64,256]{1,0:T(8,128)(2,1)S(1)}, bf16[64,256]{1,0:T(8,128)(2,1)S(1)}, u32[]{:S(2)}, u32[]{:S(2)}) collective-permute-start(bf16[64,256]{1,0:T(8,128)(2,1)S(1)} %get-tuple-element.47), channel_id=1, source_target_pairs={{0,3},{1,2},{2,1},{3,0},{4,7},{5,6},{6,5},{7,4},{8,11},{9,10},{10,... | collective-permute-start | bytes 98312 | tf_op jit(solution)/shard_map/ppermute | solution.py:335
  134.2 9.3 %collective-permute-start.8 = (bf16[64,256]{1,0:T(8,128)(2,1)S(1)}, bf16[64,256]{1,0:T(8,128)(2,1)S(1)}, u32[]{:S(2)}, u32[]{:S(2)}) collective-permute-start(bf16[64,256]{1,0:T(8,128)(2,1)S(1)} %get-tuple-element.48), channel_id=1, source_target_pairs={{0,4},{1,5},{2,6},{3,7},{4,0},{5,1},{6,2},{7,3},{8,12},{9,13},{10,... | collective-permute-start | bytes 98312 | tf_op jit(solution)/shard_map/ppermute | solution.py:335
  135.9 7.6 %collective-permute-start.9 = (bf16[64,256]{1,0:T(8,128)(2,1)S(1)}, bf16[64,256]{1,0:T(8,128)(2,1)S(1)}, u32[]{:S(2)}, u32[]{:S(2)}) collective-permute-start(bf16[64,256]{1,0:T(8,128)(2,1)S(1)} %get-tuple-element.49), channel_id=1, source_target_pairs={{0,5},{1,4},{2,7},{3,6},{4,1},{5,0},{6,3},{7,2},{8,13},{9,12},{10,... | collective-permute-start | bytes 98312 | tf_op jit(solution)/shard_map/ppermute | solution.py:335
  136.0 10.4 %collective-permute-start.10 = (bf16[64,256]{1,0:T(8,128)(2,1)S(1)}, bf16[64,256]{1,0:T(8,128)(2,1)S(1)}, u32[]{:S(2)}, u32[]{:S(2)}) collective-permute-start(bf16[64,256]{1,0:T(8,128)(2,1)S(1)} %get-tuple-element.50), channel_id=1, source_target_pairs={{0,6},{1,7},{2,4},{3,5},{4,2},{5,3},{6,0},{7,1},{8,14},{9,15},{10,... | collective-permute-start | bytes 98312 | tf_op jit(solution)/shard_map/ppermute | solution.py:335
  139.3 7.1 %collective-permute-start.11 = (bf16[64,256]{1,0:T(8,128)(2,1)S(1)}, bf16[64,256]{1,0:T(8,128)(2,1)S(1)}, u32[]{:S(2)}, u32[]{:S(2)}) collective-permute-start(bf16[64,256]{1,0:T(8,128)(2,1)S(1)} %get-tuple-element.51), channel_id=1, source_target_pairs={{0,7},{1,6},{2,5},{3,4},{4,3},{5,2},{6,1},{7,0},{8,15},{9,14},{10,... | collective-permute-start | bytes 98312 | tf_op jit(solution)/shard_map/ppermute | solution.py:335

commit v3 on v2

--- a/solution.py
+++ b/solution.py
@@ -253,6 +253,9 @@
         name="prep",
     )(tokens, norm_gain.reshape(1, -1), expert_ids)
 
+    def device(segment, j):
+        return (segment // SEG_DEV) * exp_count + (segment % SEG_DEV) * group + j
+
     block = seg_len // SUMS
     sums = pl.pallas_call(
         functools.partial(sums_kernel, block),
@@ -263,16 +266,18 @@
         cost_estimate=LITTLE,
         name="sums",
     )(after(attn_keys, send[0]), attn_values)
-    halved = lax.ppermute(sums, "exp", [(i, i ^ group) for i in range(exp_count)])
-    sums = jnp.concatenate([sums, halved], axis=0)
     parts = [sums]
-    for other in range(1, seq_count):
-        parts.append(lax.ppermute(sums, "seq", [(i, i ^ other) for i in range(seq_count)]))
+    for other in range(1, segs):
+        pairs = []
+        for segment in range(segs):
+            for j in range(group):
+                pairs.append((device(segment, j), device(segment ^ other, j)))
+        parts.append(lax.ppermute(sums, ("seq", "exp"), pairs))
     packed_rows = 3 * local_tokens + segs * 2 * local_tokens // block
     packed = pl.pallas_call(
         pack_kernel,
         out_shape=shape((group, packed_rows, width)),
-        in_specs=[VMEM] * (3 + seq_count),
+        in_specs=[VMEM] * (3 + segs),
         out_specs=VMEM,
         compiler_params=params(32),
         cost_estimate=LITTLE,
@@ -281,7 +286,7 @@
     recv = []
     for rows in send:
         if recv:
-            rows = after(rows, recv[-1])
+            rows = after(after(rows, recv[-1]), sums)
         recv.append(lax.all_to_all(rows, "exp", 0, 0, tiled=True))
     packed = after(packed, recv[-1])
     halves = [[half * group + j for j in range(group)] for half in range(SEG_DEV)]
@@ -291,7 +296,7 @@
     position = jnp.stack([segment, place]).astype(jnp.int32)
     done, mine = [], []
     for chunk in range(chunks):
-        planes = [after(after(recv[chunk], recv[-1]), parts)]
+        planes = [after(recv[chunk], recv[-1])]
         for other in range(1, seq_count):
             pairs = [(i, i ^ other) for i in range(seq_count)]
             planes.append(lax.ppermute(recv[chunk], "seq", pairs))

time: 150 us -> 151 us (level)
  blocking collectives: 21.6 us -> 0 us
  waiting for transfers between devices: 46.1 us -> 59.3 us
  starting transfers between devices: 31.4 us -> 38.6 us
  local copies, waits for them, and re-layouts: 5.47 us -> 7.37 us
    all_to_all x1 -> x0, blocking collectives: 21.6 us -> none  [on_device(): recv.append(lax.all_to_all(rows, 'exp', 0, 0, tiled=True))]
    all_to_all x1 -> x2, waiting for transfers between devices: 0.01 us -> 12.4 us  [on_device(): recv.append(lax.all_to_all(rows, 'exp', 0, 0, tiled=True))]
    all_to_all x1 -> x2, starting transfers between devices: 4.1 us -> 11.5 us  [on_device(): recv.append(lax.all_to_all(rows, 'exp', 0, 0, tiled=True))]
    unnamed x14 -> x18, local copies, waits for them, and re-layouts: 5.47 us -> 7.37 us
    ppermute x2 -> x3, waiting for transfers between devices: 16.6 us -> 17.4 us  [on_device(): parts.append(lax.ppermute(sums, ('seq', 'exp'), pairs))]
    ppermute x2 -> x3, starting transfers between devices: 4.47 us -> 4.45 us  [on_device(): parts.append(lax.ppermute(sums, ('seq', 'exp'), pairs))]
  transfers between devices with their start and end apart: 17 -> 19, of which waited for: 8 -> 9; matrix products, arithmetic and copies ran while one was open for 3% -> 3% of each run, Pallas kernels for 24% -> 24%
where the time goes in v3:
time: 151 us; the launch traced here: 150 us
  waiting for transfers between devices  59.3 us (39%)
  Pallas kernels  39.8 us (26%)
  starting transfers between devices  38.6 us (26%)
  local copies, waits for them, and re-layouts  7.37 us (5%)
  other arithmetic  4.31 us (3%)
    pallas_call x2, Pallas kernels, on_device(): pl.pallas_call(functools.partial(ffn_kernel, chunk * experts, seq_count),...  30.8 us
    ppermute x3, waiting for transfers between devices, on_device(): parts.append(lax.ppermute(sums, ('seq', 'exp'), pairs))  17.4 us
    ppermute x2, waiting for transfers between devices, on_device(): planes.append(lax.ppermute(recv[chunk], 'seq', pairs))  12.7 us
    all_to_all x2, waiting for transfers between devices, on_device(): recv.append(lax.all_to_all(rows, 'exp', 0, 0, tiled=True))  12.4 us
    all_to_all x2, starting transfers between devices, on_device(): recv.append(lax.all_to_all(rows, 'exp', 0, 0, tiled=True))  11.5 us
    all_to_all x2, starting transfers between devices, on_device(): back = [lax.all_to_all(rows, 'exp', 0, 0, tiled=True) for rows in mine]  8.43 us
    ppermute x7, waiting for transfers between devices, on_device(): lax.ppermute(rows, 'exp', [(i, i ^ other) for i in range(exp_count)])  7.7 us
    all_to_all x2, waiting for transfers between devices, on_device(): back = [lax.all_to_all(rows, 'exp', 0, 0, tiled=True) for rows in mine]  7.51 us
  transfers between devices with their start and end apart: 19, of which 9 were waited for; matrix products, arithmetic and copies ran while one was open for 3% of the time, Pallas kernels for 24%

profile of v3, /device:TPU:0, one launch (start us, length us, event | category | flops | bytes accessed | tf_op | source)
XLA Modules:
  0.0 150.1 jit_solution(13041130357604214823)
XLA Ops:
  3.2 1.7 %prep.1 = (bf16[16,4,4096]{2,1,0:T(4,128)(2,1)}, bf16[16,4,4096]{2,1,0:T(4,128)(2,1)}) custom-call(bf16[64,4096]{1,0:T(8,128)(2,1)S(1)} %copy-done.4, f32[1,4096]{1,0:T(1,128)S(1)} %bitcast.3, s32[64,2]{1,0:T(8,128)S(1)} %copy.12.ids_ref), custom_call_target="tpu_custom_call" | custom-call | flops 1000 | bytes 1000 | tf_op jit(solution)/shard_map/prep/pallas_call | solution.py:246
  4.8 7.4 %all-to-all-start = ((bf16[16,4,4096]{2,1,0:T(4,128)(2,1)}), bf16[16,4,4096]{2,1,0:T(4,128)(2,1)S(1)}, u32[]{:S(2)}, u32[]{:S(2)}) async-start(bf16[16,4,4096]{2,1,0:T(4,128)(2,1)} %get-tuple-element.28), calls=%async_computation | async-start | bytes 1048576 | tf_op jit(solution)/shard_map/all_to_all | solution.py:290
  14.3 12.4 %all-to-all-done.refs_0_ = bf16[16,4,4096]{2,1,0:T(4,128)(2,1)S(1)} async-done(((bf16[16,4,4096]{2,1,0:T(4,128)(2,1)}), bf16[16,4,4096]{2,1,0:T(4,128)(2,1)S(1)}, u32[]{:S(2)}, u32[]{:S(2)}) %all-to-all-start) | async-done | bytes 524320 | tf_op jit(solution)/shard_map/all_to_all | solution.py:290
  26.7 4.1 %all-to-all-start.1 = ((bf16[16,4,4096]{2,1,0:T(4,128)(2,1)}), bf16[16,4,4096]{2,1,0:T(4,128)(2,1)S(1)}, u32[]{:S(2)}, u32[]{:S(2)}) async-start(bf16[16,4,4096]{2,1,0:T(4,128)(2,1)} %get-tuple-element.32), calls=%async_computation.1 | async-start | bytes 1048576 | tf_op jit(solution)/shard_map/all_to_all | solution.py:290
  30.8 2.8 %collective-permute-start = (bf16[16,2048]{1,0:T(8,128)(2,1)S(1)}, bf16[16,2048]{1,0:T(8,128)(2,1)S(1)}, u32[]{:S(2)}, u32[]{:S(2)}) collective-permute-start(bf16[16,2048]{1,0:T(8,128)(2,1)S(1)} %sums.1.refs_0_), channel_id=1, source_target_pairs={{0,8},{1,9},{2,10},{3,11},{4,12},{5,13},{6,14},{7,15},{8,0},{9,1},... | collective-permute-start | bytes 196616 | tf_op jit(solution)/shard_map/ppermute | solution.py:275
  35.2 15.5 %collective-permute-done.refs_1_ = bf16[16,2048]{1,0:T(8,128)(2,1)S(1)} collective-permute-done((bf16[16,2048]{1,0:T(8,128)(2,1)S(1)}, bf16[16,2048]{1,0:T(8,128)(2,1)S(1)}, u32[]{:S(2)}, u32[]{:S(2)}) %collective-permute-start) | collective-permute-done | bytes 65568 | tf_op jit(solution)/shard_map/ppermute | solution.py:275
  50.8 1.9 %collective-permute-done.2.refs_3_ = bf16[16,2048]{1,0:T(8,128)(2,1)S(1)} collective-permute-done((bf16[16,2048]{1,0:T(8,128)(2,1)S(1)}, bf16[16,2048]{1,0:T(8,128)(2,1)S(1)}, u32[]{:S(2)}, u32[]{:S(2)}) %collective-permute-start.2) | collective-permute-done | bytes 65568 | tf_op jit(solution)/shard_map/ppermute | solution.py:275
  56.6 3.6 %all-to-all-start.2 = ((bf16[8,256,256]{2,1,0:T(8,128)(2,1)}), bf16[8,256,256]{2,1,0:T(8,128)(2,1)S(1)}, u32[]{:S(2)}, u32[]{:S(2)}) async-start(bf16[8,256,256]{2,1,0:T(8,128)(2,1)} %pack.1), calls=%async_computation.2 | async-start | bytes 2097152 | tf_op jit(solution)/shard_map/all_to_all | solution.py:293
  62.2 12.7 %collective-permute-done.3.refs_1_ = bf16[16,4,4096]{2,1,0:T(4,128)(2,1)S(1)} collective-permute-done((bf16[16,4,4096]{2,1,0:T(4,128)(2,1)S(1)}, bf16[16,4,4096]{2,1,0:T(4,128)(2,1)S(1)}, u32[]{:S(2)}, u32[]{:S(2)}) %collective-permute-start.3) | collective-permute-done | bytes 524320 | tf_op jit(solution)/shard_map/ppermute | solution.py:302
  74.9 15.4 %experts.2 = (bf16[16,4,4096]{2,1,0:T(4,128)(2,1)S(1)}, bf16[16,4,4096]{2,1,0:T(4,128)(2,1)}) custom-call(bf16[16,4,4096]{2,1,0:T(4,128)(2,1)S(1)} %all-to-all-done.refs_0_, bf16[16,4,4096]{2,1,0:T(4,128)(2,1)S(1)} %collective-permute-done.3.refs_1_, bf16[4,704,4096]{2,1,0:T(8,128)(2,1)} %refs_2_.3, bf16[4,704,4096]{2,1,0:T(8,128)(2,1)} %refs_3_.3, ...), custom_call_target="tpu_custom_call" | custom-call | flops 1000 | bytes 1000 | tf_op jit(solution)/shard_map/experts/pallas_call | solution.py:304
  91.0 15.3 %experts.3 = (bf16[16,4,4096]{2,1,0:T(4,128)(2,1)S(1)}, bf16[16,4,4096]{2,1,0:T(4,128)(2,1)}) custom-call(bf16[16,4,4096]{2,1,0:T(4,128)(2,1)S(1)} %all-to-all-done.1.refs_0_, bf16[16,4,4096]{2,1,0:T(4,128)(2,1)S(1)} %collective-permute-done.4.refs_1_, bf16[4,704,4096]{2,1,0:T(8,128)(2,1)} %refs_2_.3, bf16[4,704,4096]{2,1,0:T(8,128)(2,1)} %refs_3_.3, ...), custom_call_target="tpu_custom_call" | custom-call | flops 1000 | bytes 1000 | tf_op jit(solution)/shard_map/experts/pallas_call | solution.py:304
  106.3 1.6 %collective-permute-start.13 = (bf16[16,4,4096]{2,1,0:T(4,128)(2,1)}, bf16[16,4,4096]{2,1,0:T(4,128)(2,1)}, u32[]{:S(2)}, u32[]{:S(2)}) collective-permute-start(bf16[16,4,4096]{2,1,0:T(4,128)(2,1)} %get-tuple-element.52), channel_id=1, source_target_pairs={{0,16},{16,0},{1,17},{17,1},{2,18},{18,2},{3,19},{19,3},{4,20},{20... | collective-permute-start | bytes 1572872 | tf_op jit(solution)/shard_map/ppermute | solution.py:324
  107.9 2.1 %add_convert_fusion.1 = bf16[16,4,4096]{2,1,0:T(4,128)(2,1)} fusion(bf16[16,4,4096]{2,1,0:T(4,128)(2,1)} %collective-permute-done.5, bf16[16,4,4096]{2,1,0:T(4,128)(2,1)S(1)} %get-tuple-element.39), kind=kLoop, calls=%fused_computation.1 | loop fusion | flops 1048576 | bytes 1572864 | tf_op jit(solution)/shard_map/convert_element_type | solution.py:325
  110.0 4.3 %all-to-all-start.3 = ((bf16[16,4,4096]{2,1,0:T(4,128)(2,1)}), bf16[16,4,4096]{2,1,0:T(4,128)(2,1)S(1)}, u32[]{:S(2)}, u32[]{:S(2)}) async-start(bf16[16,4,4096]{2,1,0:T(4,128)(2,1)} %add_convert_fusion.1), calls=%async_computation.3 | async-start | bytes 1048576 | tf_op jit(solution)/shard_map/all_to_all | solution.py:354
  114.4 3.2 %attend.1 = (bf16[64,256]{1,0:T(8,128)(2,1)S(1)}, bf16[64,256]{1,0:T(8,128)(2,1)S(1)}, bf16[64,256]{1,0:T(8,128)(2,1)S(1)}, bf16[64,256]{1,0:T(8,128)(2,1)S(1)},...) custom-call(s32[2]{0:T(128)S(1)} %pad_add_fusion.at_ref, ...), custom_call_target="tpu_custom_call" | custom-call | flops 1000 | bytes 1000 | tf_op jit(solution)/shard_map/attend/pallas_call | solution.py:327
  119.2 2.1 %add_convert_fusion = bf16[16,4,4096]{2,1,0:T(4,128)(2,1)} fusion(bf16[16,4,4096]{2,1,0:T(4,128)(2,1)} %collective-permute-done.13, bf16[16,4,4096]{2,1,0:T(4,128)(2,1)S(1)} %get-tuple-element.51), kind=kLoop, calls=%fused_computation | loop fusion | flops 1048576 | bytes 1572864 | tf_op jit(solution)/shard_map/convert_element_type | solution.py:325
  121.3 7.5 %all-to-all-done.3.refs_0_ = bf16[16,4,4096]{2,1,0:T(4,128)(2,1)S(1)} async-done(((bf16[16,4,4096]{2,1,0:T(4,128)(2,1)}), bf16[16,4,4096]{2,1,0:T(4,128)(2,1)S(1)}, u32[]{:S(2)}, u32[]{:S(2)}) %all-to-all-start.3) | async-done | bytes 524320 | tf_op jit(solution)/shard_map/all_to_all | solution.py:354
  128.8 4.1 %all-to-all-start.4 = ((bf16[16,4,4096]{2,1,0:T(4,128)(2,1)}), bf16[16,4,4096]{2,1,0:T(4,128)(2,1)S(1)}, u32[]{:S(2)}, u32[]{:S(2)}) async-start(bf16[16,4,4096]{2,1,0:T(4,128)(2,1)} %add_convert_fusion), calls=%async_computation.4 | async-start | bytes 1048576 | tf_op jit(solution)/shard_map/all_to_all | solution.py:354
  133.3 1.7 %collective-permute-start.7 = (bf16[64,256]{1,0:T(8,128)(2,1)S(1)}, bf16[64,256]{1,0:T(8,128)(2,1)S(1)}, u32[]{:S(2)}, u32[]{:S(2)}) collective-permute-start(bf16[64,256]{1,0:T(8,128)(2,1)S(1)} %get-tuple-element.44), channel_id=1, source_target_pairs={{0,2},{1,3},{2,0},{3,1},{4,6},{5,7},{6,4},{7,5},{8,10},{9,11},{10,... | collective-permute-start | bytes 98312 | tf_op jit(solution)/shard_map/ppermute | solution.py:340
  135.0 1.7 %collective-permute-start.9 = (bf16[64,256]{1,0:T(8,128)(2,1)S(1)}, bf16[64,256]{1,0:T(8,128)(2,1)S(1)}, u32[]{:S(2)}, u32[]{:S(2)}) collective-permute-start(bf16[64,256]{1,0:T(8,128)(2,1)S(1)} %get-tuple-element.46), channel_id=1, source_target_pairs={{0,4},{1,5},{2,6},{3,7},{4,0},{5,1},{6,2},{7,3},{8,12},{9,13},{10,... | collective-permute-start | bytes 98312 | tf_op jit(solution)/shard_map/ppermute | solution.py:340
  136.8 2.6 %collective-permute-start.11 = (bf16[64,256]{1,0:T(8,128)(2,1)S(1)}, bf16[64,256]{1,0:T(8,128)(2,1)S(1)}, u32[]{:S(2)}, u32[]{:S(2)}) collective-permute-start(bf16[64,256]{1,0:T(8,128)(2,1)S(1)} %get-tuple-element.48), channel_id=1, source_target_pairs={{0,6},{1,7},{2,4},{3,5},{4,2},{5,3},{6,0},{7,1},{8,14},{9,15},{10,... | collective-permute-start | bytes 98312 | tf_op jit(solution)/shard_map/ppermute | solution.py:340
  140.2 4.1 %collective-permute-done.9.refs_4_ = bf16[64,256]{1,0:T(8,128)(2,1)S(1)} collective-permute-done((bf16[64,256]{1,0:T(8,128)(2,1)S(1)}, bf16[64,256]{1,0:T(8,128)(2,1)S(1)}, u32[]{:S(2)}, u32[]{:S(2)}) %collective-permute-start.9) | collective-permute-done | bytes 32800 | tf_op jit(solution)/shard_map/ppermute | solution.py:340
  144.3 2.9 %collective-permute-done.11.refs_6_ = bf16[64,256]{1,0:T(8,128)(2,1)S(1)} collective-permute-done((bf16[64,256]{1,0:T(8,128)(2,1)S(1)}, bf16[64,256]{1,0:T(8,128)(2,1)S(1)}, u32[]{:S(2)}, u32[]{:S(2)}) %collective-permute-start.11) | collective-permute-done | bytes 32800 | tf_op jit(solution)/shard_map/ppermute | solution.py:340
  148.5 1.6 %mix.1 = bf16[64,4096]{1,0:T(8,128)(2,1)} custom-call(s32[64,2]{1,0:T(8,128)S(1)} %copy.12.ids_ref, f32[64,2]{1,0:T(8,128)S(1)} %copy.14.weight_ref, bf16[16,4,4096]{2,1,0:T(4,128)(2,1)S(1)} %all-to-all-done.3.refs_0_, bf16[16,4,4096]{2,1,0:T(4,128)(2,1)S(1)} %all-to-all-done.4.refs_1_), custom_call_target="tpu_custom_call" | custom-call | flops 1000 | bytes 1000 | tf_op jit(solution)/shard_map/mix/pallas_call | solution.py:355
  (43 shorter events, 17.0 us)
Async XLA Ops:
  1.4 1.0 copy-start.4
  4.8 21.8 %all-to-all-start = ((bf16[16,4,4096]{2,1,0:T(4,128)(2,1)}), bf16[16,4,4096]{2,1,0:T(4,128)(2,1)S(1)}, u32[]{:S(2)}, u32[]{:S(2)}) async-start(bf16[16,4,4096]{2,1,0:T(4,128)(2,1)} %get-tuple-element.28), calls=%async_computation | async-start | bytes 1048576 | tf_op jit(solution)/shard_map/all_to_all | solution.py:290
  12.2 1.0 copy-start
  13.2 0.9 copy-start.2
  26.7 29.9 %all-to-all-start.1 = ((bf16[16,4,4096]{2,1,0:T(4,128)(2,1)}), bf16[16,4,4096]{2,1,0:T(4,128)(2,1)S(1)}, u32[]{:S(2)}, u32[]{:S(2)}) async-start(bf16[16,4,4096]{2,1,0:T(4,128)(2,1)} %get-tuple-element.32), calls=%async_computation.1 | async-start | bytes 1048576 | tf_op jit(solution)/shard_map/all_to_all | solution.py:290
  30.8 20.0 %collective-permute-start = (bf16[16,2048]{1,0:T(8,128)(2,1)S(1)}, bf16[16,2048]{1,0:T(8,128)(2,1)S(1)}, u32[]{:S(2)}, u32[]{:S(2)}) collective-permute-start(bf16[16,2048]{1,0:T(8,128)(2,1)S(1)} %sums.1.refs_0_), channel_id=1, source_target_pairs={{0,8},{1,9},{2,10},{3,11},{4,12},{5,13},{6,14},{7,15},{8,0},{9,1},... | collective-permute-start | bytes 196616 | tf_op jit(solution)/shard_map/ppermute | solution.py:275
  33.6 17.1 %collective-permute-start.1 = (bf16[16,2048]{1,0:T(8,128)(2,1)S(1)}, bf16[16,2048]{1,0:T(8,128)(2,1)S(1)}, u32[]{:S(2)}, u32[]{:S(2)}) collective-permute-start(bf16[16,2048]{1,0:T(8,128)(2,1)S(1)} %sums.1.refs_0_), channel_id=1, source_target_pairs={{0,16},{1,17},{2,18},{3,19},{4,20},{5,21},{6,22},{7,23},{8,24},{9,... | collective-permute-start | bytes 196616 | tf_op jit(solution)/shard_map/ppermute | solution.py:275
  35.1 17.5 %collective-permute-start.2 = (bf16[16,2048]{1,0:T(8,128)(2,1)S(1)}, bf16[16,2048]{1,0:T(8,128)(2,1)S(1)}, u32[]{:S(2)}, u32[]{:S(2)}) collective-permute-start(bf16[16,2048]{1,0:T(8,128)(2,1)S(1)} %sums.1.refs_0_), channel_id=1, source_target_pairs={{0,24},{1,25},{2,26},{3,27},{4,28},{5,29},{6,30},{7,31},{8,16},{9,... | collective-permute-start | bytes 196616 | tf_op jit(solution)/shard_map/ppermute | solution.py:275
  52.6 1.0 copy-start.1
  56.6 51.3 %all-to-all-start.2 = ((bf16[8,256,256]{2,1,0:T(8,128)(2,1)}), bf16[8,256,256]{2,1,0:T(8,128)(2,1)S(1)}, u32[]{:S(2)}, u32[]{:S(2)}) async-start(bf16[8,256,256]{2,1,0:T(8,128)(2,1)} %pack.1), calls=%async_computation.2 | async-start | bytes 2097152 | tf_op jit(solution)/shard_map/all_to_all | solution.py:293
  60.1 14.8 %collective-permute-start.3 = (bf16[16,4,4096]{2,1,0:T(4,128)(2,1)S(1)}, bf16[16,4,4096]{2,1,0:T(4,128)(2,1)S(1)}, u32[]{:S(2)}, u32[]{:S(2)}) collective-permute-start(bf16[16,4,4096]{2,1,0:T(4,128)(2,1)S(1)} %all-to-all-done.refs_0_), channel_id=1, source_target_pairs={{0,16},{16,0},{1,17},{17,1},{2,18},{18,2},{3,19},{19,3},{4,20},{20... | collective-permute-start | bytes 1572872 | tf_op jit(solution)/shard_map/ppermute | solution.py:302
  60.7 30.3 %collective-permute-start.4 = (bf16[16,4,4096]{2,1,0:T(4,128)(2,1)S(1)}, bf16[16,4,4096]{2,1,0:T(4,128)(2,1)S(1)}, u32[]{:S(2)}, u32[]{:S(2)}) collective-permute-start(bf16[16,4,4096]{2,1,0:T(4,128)(2,1)S(1)} %all-to-all-done.1.refs_0_), channel_id=1, source_target_pairs={{0,16},{16,0},{1,17},{17,1},{2,18},{18,2},{3,19},{19,3},{4,20},{20... | collective-permute-start | bytes 1572872 | tf_op jit(solution)/shard_map/ppermute | solution.py:302
  90.4 17.5 %collective-permute-start.5 = (bf16[16,4,4096]{2,1,0:T(4,128)(2,1)}, bf16[16,4,4096]{2,1,0:T(4,128)(2,1)}, u32[]{:S(2)}, u32[]{:S(2)}) collective-permute-start(bf16[16,4,4096]{2,1,0:T(4,128)(2,1)} %get-tuple-element.40), channel_id=1, source_target_pairs={{0,16},{16,0},{1,17},{17,1},{2,18},{18,2},{3,19},{19,3},{4,20},{20... | collective-permute-start | bytes 1572872 | tf_op jit(solution)/shard_map/ppermute | solution.py:324
  91.0 49.2 %copy-start.7 = (f32[64,2]{0,1:T(2,128)S(1)}, f32[64,2]{0,1:T(2,128)}, u32[]{:S(2)}) copy-start(f32[64,2]{0,1:T(2,128)} %param.16) | copy-start | bytes 1540
  106.3 12.9 %collective-permute-start.13 = (bf16[16,4,4096]{2,1,0:T(4,128)(2,1)}, bf16[16,4,4096]{2,1,0:T(4,128)(2,1)}, u32[]{:S(2)}, u32[]{:S(2)}) collective-permute-start(bf16[16,4,4096]{2,1,0:T(4,128)(2,1)} %get-tuple-element.52), channel_id=1, source_target_pairs={{0,16},{16,0},{1,17},{17,1},{2,18},{18,2},{3,19},{19,3},{4,20},{20... | collective-permute-start | bytes 1572872 | tf_op jit(solution)/shard_map/ppermute | solution.py:324
  110.0 18.8 %all-to-all-start.3 = ((bf16[16,4,4096]{2,1,0:T(4,128)(2,1)}), bf16[16,4,4096]{2,1,0:T(4,128)(2,1)S(1)}, u32[]{:S(2)}, u32[]{:S(2)}) async-start(bf16[16,4,4096]{2,1,0:T(4,128)(2,1)} %add_convert_fusion.1), calls=%async_computation.3 | async-start | bytes 1048576 | tf_op jit(solution)/shard_map/all_to_all | solution.py:354
  128.8 19.7 %all-to-all-start.4 = ((bf16[16,4,4096]{2,1,0:T(4,128)(2,1)}), bf16[16,4,4096]{2,1,0:T(4,128)(2,1)S(1)}, u32[]{:S(2)}, u32[]{:S(2)}) async-start(bf16[16,4,4096]{2,1,0:T(4,128)(2,1)} %add_convert_fusion), calls=%async_computation.4 | async-start | bytes 1048576 | tf_op jit(solution)/shard_map/all_to_all | solution.py:354
  132.9 3.9 %collective-permute-start.6 = (bf16[64,256]{1,0:T(8,128)(2,1)S(1)}, bf16[64,256]{1,0:T(8,128)(2,1)S(1)}, u32[]{:S(2)}, u32[]{:S(2)}) collective-permute-start(bf16[64,256]{1,0:T(8,128)(2,1)S(1)} %get-tuple-element.43), channel_id=1, source_target_pairs={{0,1},{1,0},{2,3},{3,2},{4,5},{5,4},{6,7},{7,6},{8,9},{9,8},{10,11... | collective-permute-start | bytes 98312 | tf_op jit(solution)/shard_map/ppermute | solution.py:340
  133.3 6.8 %collective-permute-start.7 = (bf16[64,256]{1,0:T(8,128)(2,1)S(1)}, bf16[64,256]{1,0:T(8,128)(2,1)S(1)}, u32[]{:S(2)}, u32[]{:S(2)}) collective-permute-start(bf16[64,256]{1,0:T(8,128)(2,1)S(1)} %get-tuple-element.44), channel_id=1, source_target_pairs={{0,2},{1,3},{2,0},{3,1},{4,6},{5,7},{6,4},{7,5},{8,10},{9,11},{10,... | collective-permute-start | bytes 98312 | tf_op jit(solution)/shard_map/ppermute | solution.py:340
  135.0 5.2 %collective-permute-start.8 = (bf16[64,256]{1,0:T(8,128)(2,1)S(1)}, bf16[64,256]{1,0:T(8,128)(2,1)S(1)}, u32[]{:S(2)}, u32[]{:S(2)}) collective-permute-start(bf16[64,256]{1,0:T(8,128)(2,1)S(1)} %get-tuple-element.45), channel_id=1, source_target_pairs={{0,3},{1,2},{2,1},{3,0},{4,7},{5,6},{6,5},{7,4},{8,11},{9,10},{10,... | collective-permute-start | bytes 98312 | tf_op jit(solution)/shard_map/ppermute | solution.py:340
  135.0 9.3 %collective-permute-start.9 = (bf16[64,256]{1,0:T(8,128)(2,1)S(1)}, bf16[64,256]{1,0:T(8,128)(2,1)S(1)}, u32[]{:S(2)}, u32[]{:S(2)}) collective-permute-start(bf16[64,256]{1,0:T(8,128)(2,1)S(1)} %get-tuple-element.46), channel_id=1, source_target_pairs={{0,4},{1,5},{2,6},{3,7},{4,0},{5,1},{6,2},{7,3},{8,12},{9,13},{10,... | collective-permute-start | bytes 98312 | tf_op jit(solution)/shard_map/ppermute | solution.py:340
  136.7 7.6 %collective-permute-start.10 = (bf16[64,256]{1,0:T(8,128)(2,1)S(1)}, bf16[64,256]{1,0:T(8,128)(2,1)S(1)}, u32[]{:S(2)}, u32[]{:S(2)}) collective-permute-start(bf16[64,256]{1,0:T(8,128)(2,1)S(1)} %get-tuple-element.47), channel_id=1, source_target_pairs={{0,5},{1,4},{2,7},{3,6},{4,1},{5,0},{6,3},{7,2},{8,13},{9,12},{10,... | collective-permute-start | bytes 98312 | tf_op jit(solution)/shard_map/ppermute | solution.py:340
  136.8 10.4 %collective-permute-start.11 = (bf16[64,256]{1,0:T(8,128)(2,1)S(1)}, bf16[64,256]{1,0:T(8,128)(2,1)S(1)}, u32[]{:S(2)}, u32[]{:S(2)}) collective-permute-start(bf16[64,256]{1,0:T(8,128)(2,1)S(1)} %get-tuple-element.48), channel_id=1, source_target_pairs={{0,6},{1,7},{2,4},{3,5},{4,2},{5,3},{6,0},{7,1},{8,14},{9,15},{10,... | collective-permute-start | bytes 98312 | tf_op jit(solution)/shard_map/ppermute | solution.py:340
  140.1 7.1 %collective-permute-start.12 = (bf16[64,256]{1,0:T(8,128)(2,1)S(1)}, bf16[64,256]{1,0:T(8,128)(2,1)S(1)}, u32[]{:S(2)}, u32[]{:S(2)}) collective-permute-start(bf16[64,256]{1,0:T(8,128)(2,1)S(1)} %get-tuple-element.49), channel_id=1, source_target_pairs={{0,7},{1,6},{2,5},{3,4},{4,3},{5,2},{6,1},{7,0},{8,15},{9,14},{10,... | collective-permute-start | bytes 98312 | tf_op jit(solution)/shard_map/ppermute | solution.py:340
  (3 other events, 2.6 us)

commit v4 on v3

--- a/solution.py
+++ b/solution.py
@@ -30,61 +30,81 @@
     return pltpu.CompilerParams(vmem_limit_bytes=mib * 2**20)
 
 
-def as_row(column):
-    n = column.shape[0]
+def as_column(row):
+    n = row.shape[1]
     eye = lax.broadcasted_iota(jnp.int32, (n, n), 0) == lax.broadcasted_iota(jnp.int32, (n, n), 1)
-    return jnp.sum(jnp.where(eye, column, 0), axis=0, keepdims=True)
+    return jnp.sum(jnp.where(eye, row, jnp.zeros((), row.dtype)), axis=1, keepdims=True)
 
 
 def slots(ids):
-    n = ids.shape[0]
-    columns = [ids[:, 0:1], ids[:, 1:2]]
-    rows = [as_row(column) for column in columns]
-    earlier = lax.broadcasted_iota(jnp.int32, (n, n), 1) < lax.broadcasted_iota(jnp.int32, (n, n), 0)
+    n = ids.shape[1]
+    rows = [ids[0:1], ids[1:2]]
+    columns = [as_column(row) for row in rows]
+    earlier = lax.broadcasted_iota(jnp.int32, (n, n), 0) < lax.broadcasted_iota(jnp.int32, (n, n), 1)
     found = []
-    for column in columns:
-        same = (rows[0] == column) | (rows[1] == column)
-        before = jnp.sum(jnp.where(same & earlier, 1, 0), axis=1, keepdims=True)
-        found.append(column * CAP + before)
+    for row in rows:
+        same = (columns[0] == row) | (columns[1] == row)
+        before = jnp.sum(jnp.where(same & earlier, 1, 0), axis=0, keepdims=True)
+        found.append(row * CAP + before)
     return found
 
 
-def prep_kernel(tok_ref, gain_ref, ids_ref, *out_refs):
+def prep_kernel(block, tok_hbm, gain_ref, ids_ref, k_hbm, v_hbm, *refs):
+    out_refs, sum_ref, (tok_ref, k_ref, v_ref, sem) = refs[:-5], refs[-5], refs[-4:]
+    copies = [
+        pltpu.make_async_copy(frm, to, sem.at[at])
+        for at, (frm, to) in enumerate(((tok_hbm, tok_ref), (k_hbm, k_ref), (v_hbm, v_ref)))
+    ]
+    for copy in copies:
+        copy.start()
     n = tok_ref.shape[0]
+    first, second = slots(ids_ref[...])
+    place = lax.broadcasted_iota(jnp.int32, (EXPERTS * CAP, n), 0)
+    pick = jnp.where((place == first) | (place == second), 1.0, 0.0).astype(BF16)
+    copies[0].wait()
     values = tok_ref[...].astype(F32)
     inv_rms = lax.rsqrt(jnp.mean(values * values, axis=-1, keepdims=True) + EPS)
     normed = (values * inv_rms * gain_ref[...]).astype(BF16)
-    first, second = [as_row(column) for column in slots(ids_ref[...])]
-    place = lax.broadcasted_iota(jnp.int32, (EXPERTS * CAP, n), 0)
-    pick = jnp.where((place == first) | (place == second), 1.0, 0.0).astype(BF16)
     rows = jnp.dot(pick, normed, preferred_element_type=F32)
     dests, step = out_refs[0].shape[0], out_refs[0].shape[1]
     for dest in range(dests):
         for chunk, out_ref in enumerate(out_refs):
             lower = (dest * len(out_refs) + chunk) * step
             out_ref[dest] = rows[lower : lower + step].astype(BF16)
-
-
-def sums_kernel(block, k_ref, v_ref, out_ref):
-    total, _ = k_ref.shape
-    count = total // block
-    row = lax.broadcasted_iota(jnp.int32, (count, total), 0)
-    column = lax.broadcasted_iota(jnp.int32, (count, total), 1)
+    count = n // block
+    row = lax.broadcasted_iota(jnp.int32, (count, n), 0)
+    column = lax.broadcasted_iota(jnp.int32, (count, n), 1)
     member = jnp.where(column // block == row, 1.0, 0.0).astype(BF16)
     for which, ref in enumerate((k_ref, v_ref)):
+        copies[which + 1].wait()
         summed = jnp.dot(member, ref[...], preferred_element_type=F32) * (1.0 / math.sqrt(block))
-        out_ref[which * count : (which + 1) * count] = summed.astype(BF16)
-
-
-def pack_kernel(q_ref, k_ref, v_ref, *refs):
-    sum_refs, out_ref = refs[:-1], refs[-1]
+        sum_ref[which * count : (which + 1) * count] = summed.astype(BF16)
+
+
+def pack_kernel(q_hbm, k_hbm, v_hbm, *refs):
+    sum_refs, out_ref, sem = refs[:-2], refs[-2], refs[-1]
     dests, _, width = out_ref.shape
+    tokens = q_hbm.shape[0]
+    copies = []
     for dest in range(dests):
-        lower = 0
-        for ref in (q_ref, k_ref, v_ref, *sum_refs):
+        for which, ref in enumerate((q_hbm, k_hbm, v_hbm)):
+            copies.append(
+                pltpu.make_async_copy(
+                    ref.at[:, pl.ds(dest * width, width)],
+                    out_ref.at[dest, pl.ds(which * tokens, tokens)],
+                    sem.at[dest * 3 + which],
+                )
+            )
+    for copy in copies:
+        copy.start()
+    for dest in range(dests):
+        lower = 3 * tokens
+        for ref in sum_refs:
             upper = lower + ref.shape[0]
             out_ref[dest, lower:upper] = ref[:, dest * width : (dest + 1) * width]
             lower = upper
+    for copy in copies:
+        copy.wait()
 
 
 def attend_kernel(query_rows, tokens, segs, at_ref, recv_ref, *refs):
@@ -200,12 +220,12 @@
             lower = (dest * len(in_refs) + chunk) * step
             y_ref[lower : lower + step] = ref[dest].astype(F32)
     rows = y_ref[...].astype(BF16)
-    n = ids_ref.shape[0]
+    n = ids_ref.shape[1]
     place = lax.broadcasted_iota(jnp.int32, (n, EXPERTS * CAP), 1)
     total = None
-    for k, column in enumerate(slots(ids_ref[...])):
-        pick = jnp.where(place == column, 1.0, 0.0).astype(BF16)
-        part = weight_ref[:, k : k + 1] * jnp.dot(pick, rows, preferred_element_type=F32)
+    for k, row in enumerate(slots(ids_ref[...])):
+        pick = jnp.where(place == as_column(row), 1.0, 0.0).astype(BF16)
+        part = as_column(weight_ref[k : k + 1]) * jnp.dot(pick, rows, preferred_element_type=F32)
         total = part if total is None else total + part
     out_ref[...] = total.astype(BF16)
 
@@ -243,29 +263,27 @@
     att = queries.shape[1]
     width = att // group
 
-    send = pl.pallas_call(
-        prep_kernel,
-        out_shape=[shape((exp_count, step, features))] * chunks,
-        in_specs=[VMEM] * 3,
-        out_specs=[VMEM] * chunks,
-        compiler_params=params(32),
+    block = seg_len // SUMS
+    *send, sums = pl.pallas_call(
+        functools.partial(prep_kernel, block),
+        out_shape=[shape((exp_count, step, features))] * chunks
+        + [shape((2 * local_tokens // block, att))],
+        in_specs=[ANY, VMEM, VMEM, ANY, ANY],
+        out_specs=[VMEM] * (chunks + 1),
+        scratch_shapes=[
+            pltpu.VMEM((local_tokens, features), BF16),
+            pltpu.VMEM((local_tokens, att), BF16),
+            pltpu.VMEM((local_tokens, att), BF16),
+            pltpu.SemaphoreType.DMA((3,)),
+        ],
+        compiler_params=params(56),
         cost_estimate=LITTLE,
         name="prep",
-    )(tokens, norm_gain.reshape(1, -1), expert_ids)
+    )(tokens, norm_gain.reshape(1, -1), expert_ids.T, attn_keys, attn_values)
 
     def device(segment, j):
         return (segment // SEG_DEV) * exp_count + (segment % SEG_DEV) * group + j
 
-    block = seg_len // SUMS
-    sums = pl.pallas_call(
-        functools.partial(sums_kernel, block),
-        out_shape=shape((2 * local_tokens // block, att)),
-        in_specs=[VMEM] * 2,
-        out_specs=VMEM,
-        compiler_params=params(32),
-        cost_estimate=LITTLE,
-        name="sums",
-    )(after(attn_keys, send[0]), attn_values)
     parts = [sums]
     for other in range(1, segs):
         pairs = []
@@ -277,29 +295,30 @@
     packed = pl.pallas_call(
         pack_kernel,
         out_shape=shape((group, packed_rows, width)),
-        in_specs=[VMEM] * (3 + segs),
+        in_specs=[ANY] * 3 + [VMEM] * segs,
         out_specs=VMEM,
-        compiler_params=params(32),
+        scratch_shapes=[pltpu.SemaphoreType.DMA((3 * group,))],
+        compiler_params=params(56),
         cost_estimate=LITTLE,
         name="pack",
     )(queries, attn_keys, attn_values, *parts)
-    recv = []
-    for rows in send:
-        if recv:
-            rows = after(after(rows, recv[-1]), sums)
-        recv.append(lax.all_to_all(rows, "exp", 0, 0, tiled=True))
-    packed = after(packed, recv[-1])
-    halves = [[half * group + j for j in range(group)] for half in range(SEG_DEV)]
-    got = lax.all_to_all(packed, "exp", 0, 0, axis_index_groups=halves, tiled=True)
+    recv = [lax.all_to_all(send[0], "exp", 0, 0, tiled=True)]
+    recv[0] = after(recv[0], parts)
+    for rows in send[1:]:
+        recv.append(lax.all_to_all(after(rows, recv[-1]), "exp", 0, 0, tiled=True))
+    arrived = []
+    for rows in recv:
+        planes = [rows]
+        for other in range(1, seq_count):
+            pairs = [(i, i ^ other) for i in range(seq_count)]
+            planes.append(lax.ppermute(rows, "seq", pairs))
+        arrived.append(planes)
     segment = lax.axis_index("seq") * SEG_DEV + lax.axis_index("exp") // group
     place = lax.axis_index("exp") % group
     position = jnp.stack([segment, place]).astype(jnp.int32)
     done, mine = [], []
     for chunk in range(chunks):
-        planes = [after(recv[chunk], recv[-1])]
-        for other in range(1, seq_count):
-            pairs = [(i, i ^ other) for i in range(seq_count)]
-            planes.append(lax.ppermute(recv[chunk], "seq", pairs))
+        planes = [after(arrived[chunk][0], recv[-1])] + arrived[chunk][1:]
         total = seq_count * exp_count * step
         pieces = pl.pallas_call(
             functools.partial(ffn_kernel, chunk * experts, seq_count),
@@ -317,6 +336,9 @@
             name="experts",
         )(*planes, gate_proj, up_proj, down_proj)
         done.append(pieces)
+    packed = after(packed, done[0][0])
+    halves = [[half * group + j for j in range(group)] for half in range(SEG_DEV)]
+    got = lax.all_to_all(packed, "exp", 0, 0, axis_index_groups=halves, tiled=True)
     for chunk, pieces in enumerate(done):
         summed = after(after(pieces[0], done[-1][0]), got).astype(F32)
         for other in range(1, seq_count):
@@ -350,7 +372,7 @@
         name="place",
     )(position, *heads)
 
-    mine[-1] = after(mine[-1], head_out[0])
+    mine[-1] = after(mine[-1], heads[1:4])
     back = [lax.all_to_all(rows, "exp", 0, 0, tiled=True) for rows in mine]
     expert_mix = pl.pallas_call(
         mix_kernel,
@@ -361,7 +383,7 @@
         compiler_params=params(32),
         cost_estimate=LITTLE,
         name="mix",
-    )(expert_ids, route_weights, *back)
+    )(expert_ids.T, route_weights.T, *back)
     return (attention, expert_mix)
 
 

time: 151 us -> 146 us (0.967)
  local copies, waits for them, and re-layouts: 7.37 us -> 0.02 us
  Pallas kernels: 39.8 us -> 43.6 us
    unnamed x18 -> x10, local copies, waits for them, and re-layouts: 7.37 us -> 0.02 us
    ppermute x7, waiting for transfers between devices: 7.7 us -> 12.2 us  [on_device(): lax.ppermute(rows, 'exp', [(i, i ^ other) for i in range(exp_count)])]
    pallas_call x1, Pallas kernels: 1.06 us -> 3.21 us  [on_device(): pl.pallas_call(pack_kernel, out_shape=shape((group, packed_rows, width)),...]
    all_to_all x2, waiting for transfers between devices: 7.51 us -> 5.36 us  [on_device(): back = [lax.all_to_all(rows, 'exp', 0, 0, tiled=True) for rows in mine]]
    all_to_all x2, waiting for transfers between devices: 12.4 us -> 10.7 us  [the longest x1 10.7 us: on_device(): recv.append(lax.all_to_all(after(rows, recv[-1]), 'exp', 0, 0, tiled=True))]
    pallas_call x2 -> x1, Pallas kernels: 1.87 us -> 3.55 us  [on_device(): pl.pallas_call(functools.partial(prep_kernel, block), out_shape=[shape((e...]
    all_to_all x2, starting transfers between devices: 8.43 us -> 10 us  [on_device(): back = [lax.all_to_all(rows, 'exp', 0, 0, tiled=True) for rows in mine]]
    ppermute x2, waiting for transfers between devices: 1.56 us -> 0.01 us  [on_device(): summed = summed + lax.ppermute(pieces[other], 'seq', pairs).astype(F32)]
  transfers between devices with their start and end apart: 19 -> 19, of which waited for: 9 -> 10; matrix products, arithmetic and copies ran while one was open for 3% -> 2% of each run, Pallas kernels for 24% -> 16%
where the time goes in v4:
time: 146 us; the launch traced here: 145 us
  waiting for transfers between devices  58.3 us (40%)
  Pallas kernels  43.6 us (30%)
  starting transfers between devices  39.3 us (27%)
  other arithmetic  3.3 us (2%)
    pallas_call x2, Pallas kernels, on_device(): pl.pallas_call(functools.partial(ffn_kernel, chunk * experts, seq_count),...  30.6 us
    ppermute x3, waiting for transfers between devices, on_device(): parts.append(lax.ppermute(sums, ('seq', 'exp'), pairs))  17.4 us
    ppermute x2, waiting for transfers between devices, on_device(): planes.append(lax.ppermute(rows, 'seq', pairs))  12.7 us
    ppermute x7, waiting for transfers between devices, on_device(): lax.ppermute(rows, 'exp', [(i, i ^ other) for i in range(exp_count)])  12.2 us
    all_to_all x1, waiting for transfers between devices, on_device(): recv.append(lax.all_to_all(after(rows, recv[-1]), 'exp', 0, 0, tiled=True))  10.7 us
    all_to_all x2, starting transfers between devices, on_device(): back = [lax.all_to_all(rows, 'exp', 0, 0, tiled=True) for rows in mine]  10 us
    all_to_all x1, starting transfers between devices, on_device(): recv = [lax.all_to_all(send[0], 'exp', 0, 0, tiled=True)]  7.36 us
    ppermute x7, starting transfers between devices, on_device(): lax.ppermute(rows, 'exp', [(i, i ^ other) for i in range(exp_count)])  6.79 us
  transfers between devices with their start and end apart: 19, of which 10 were waited for; matrix products, arithmetic and copies ran while one was open for 2% of the time, Pallas kernels for 16%

profile of v4, /device:TPU:0, one launch (start us, length us, event | category | flops | bytes accessed | tf_op | source)
XLA Modules:
  0.0 145.3 jit_solution(9040100342407238128)
XLA Ops:
  0.6 3.5 %prep.1 = (bf16[16,4,4096]{2,1,0:T(4,128)(2,1)}, bf16[16,4,4096]{2,1,0:T(4,128)(2,1)}, bf16[16,2048]{1,0:T(8,128)(2,1)}) custom-call(bf16[64,4096]{1,0:T(8,128)(2,1)} %tok_hbm.1, f32[1,4096]{1,0:T(1,128)} %bitcast.8, s32[2,64]{1,0:T(2,128)} %bitcast.5, bf16[64,2048]{1,0:T(8,128)(2,1)} %k_hbm.3, bf16[64,2048]{1,0:T(8,128)(2,1)} %v_hbm.3), custom_call_target="tpu_custom_call" | custom-call | flops 1000 | bytes 1000 | tf_op jit(solution)/shard_map/prep/pallas_call | solution.py:267
  4.2 7.4 %all-to-all-start = ((bf16[16,4,4096]{2,1,0:T(4,128)(2,1)}), bf16[16,4,4096]{2,1,0:T(4,128)(2,1)S(1)}, u32[]{:S(2)}, u32[]{:S(2)}) async-start(bf16[16,4,4096]{2,1,0:T(4,128)(2,1)} %get-tuple-element.29), calls=%async_computation | async-start | bytes 1048576 | tf_op jit(solution)/shard_map/all_to_all | solution.py:305
  11.6 2.8 %collective-permute-start = (bf16[16,2048]{1,0:T(8,128)(2,1)}, bf16[16,2048]{1,0:T(8,128)(2,1)S(1)}, u32[]{:S(2)}, u32[]{:S(2)}) collective-permute-start(bf16[16,2048]{1,0:T(8,128)(2,1)} %get-tuple-element.28.refs_0_), channel_id=1, source_target_pairs={{0,8},{1,9},{2,10},{3,11},{4,12},{5,13},{6,14},{7,15},{8,0},{9,1},... | collective-permute-start | bytes 196616 | tf_op jit(solution)/shard_map/ppermute | solution.py:293
  14.4 1.5 %collective-permute-start.1 = (bf16[16,2048]{1,0:T(8,128)(2,1)}, bf16[16,2048]{1,0:T(8,128)(2,1)S(1)}, u32[]{:S(2)}, u32[]{:S(2)}) collective-permute-start(bf16[16,2048]{1,0:T(8,128)(2,1)} %get-tuple-element.28.refs_0_), channel_id=1, source_target_pairs={{0,16},{1,17},{2,18},{3,19},{4,20},{5,21},{6,22},{7,23},{8,24},{9,... | collective-permute-start | bytes 196616 | tf_op jit(solution)/shard_map/ppermute | solution.py:293
  16.0 15.5 %collective-permute-done.refs_1_ = bf16[16,2048]{1,0:T(8,128)(2,1)S(1)} collective-permute-done((bf16[16,2048]{1,0:T(8,128)(2,1)}, bf16[16,2048]{1,0:T(8,128)(2,1)S(1)}, u32[]{:S(2)}, u32[]{:S(2)}) %collective-permute-start) | collective-permute-done | bytes 65568 | tf_op jit(solution)/shard_map/ppermute | solution.py:293
  31.5 1.9 %collective-permute-done.2.refs_3_ = bf16[16,2048]{1,0:T(8,128)(2,1)S(1)} collective-permute-done((bf16[16,2048]{1,0:T(8,128)(2,1)}, bf16[16,2048]{1,0:T(8,128)(2,1)S(1)}, u32[]{:S(2)}, u32[]{:S(2)}) %collective-permute-start.2) | collective-permute-done | bytes 65568 | tf_op jit(solution)/shard_map/ppermute | solution.py:293
  33.4 3.7 %all-to-all-start.1 = ((bf16[16,4,4096]{2,1,0:T(4,128)(2,1)}), bf16[16,4,4096]{2,1,0:T(4,128)(2,1)S(1)}, u32[]{:S(2)}, u32[]{:S(2)}) async-start(bf16[16,4,4096]{2,1,0:T(4,128)(2,1)} %get-tuple-element.32), calls=%async_computation.1 | async-start | bytes 1048576 | tf_op jit(solution)/shard_map/all_to_all | solution.py:308
  37.7 3.2 %pack.1 = bf16[8,256,256]{2,1,0:T(8,128)(2,1)} custom-call(bf16[64,2048]{1,0:T(8,128)(2,1)} %q_hbm.1, bf16[64,2048]{1,0:T(8,128)(2,1)} %k_hbm.3, bf16[64,2048]{1,0:T(8,128)(2,1)} %v_hbm.3, bf16[16,2048]{1,0:T(8,128)(2,1)} %get-tuple-element.28.refs_0_, bf16[16,2048]{1,0:T(8,128)(2,1)} %copy-done.2, bf16[16,2048]{1,0:T(8,128)(2,1)} %copy-done.3, ...), custom_call_target="tpu_custom_call" | custom-call | flops 1000 | bytes 1000 | tf_op jit(solution)/shard_map/pack/pallas_call | solution.py:295
  40.9 10.7 %all-to-all-done.1.refs_0_ = bf16[16,4,4096]{2,1,0:T(4,128)(2,1)S(1)} async-done(((bf16[16,4,4096]{2,1,0:T(4,128)(2,1)}), bf16[16,4,4096]{2,1,0:T(4,128)(2,1)S(1)}, u32[]{:S(2)}, u32[]{:S(2)}) %all-to-all-start.1) | async-done | bytes 524320 | tf_op jit(solution)/shard_map/all_to_all | solution.py:308
  51.6 15.4 %experts.2 = (bf16[16,4,4096]{2,1,0:T(4,128)(2,1)S(1)}, bf16[16,4,4096]{2,1,0:T(4,128)(2,1)}) custom-call(bf16[16,4,4096]{2,1,0:T(4,128)(2,1)S(1)} %all-to-all-done.refs_0_, bf16[16,4,4096]{2,1,0:T(4,128)(2,1)S(1)} %collective-permute-done.3.refs_1_, bf16[4,704,4096]{2,1,0:T(8,128)(2,1)} %refs_2_.3, bf16[4,704,4096]{2,1,0:T(8,128)(2,1)} %refs_3_.3, ...), custom_call_target="tpu_custom_call" | custom-call | flops 1000 | bytes 1000 | tf_op jit(solution)/shard_map/experts/pallas_call | solution.py:323
  67.1 3.7 %all-to-all-start.2 = ((bf16[8,256,256]{2,1,0:T(8,128)(2,1)}), bf16[8,256,256]{2,1,0:T(8,128)(2,1)S(1)}, u32[]{:S(2)}, u32[]{:S(2)}) async-start(bf16[8,256,256]{2,1,0:T(8,128)(2,1)} %pack.1), calls=%async_computation.2 | async-start | bytes 2097152 | tf_op jit(solution)/shard_map/all_to_all | solution.py:341
  72.9 12.7 %collective-permute-done.4.refs_1_ = bf16[16,4,4096]{2,1,0:T(4,128)(2,1)S(1)} collective-permute-done((bf16[16,4,4096]{2,1,0:T(4,128)(2,1)S(1)}, bf16[16,4,4096]{2,1,0:T(4,128)(2,1)S(1)}, u32[]{:S(2)}, u32[]{:S(2)}) %collective-permute-start.4) | collective-permute-done | bytes 524320 | tf_op jit(solution)/shard_map/ppermute | solution.py:314
  85.6 15.1 %experts.3 = (bf16[16,4,4096]{2,1,0:T(4,128)(2,1)S(1)}, bf16[16,4,4096]{2,1,0:T(4,128)(2,1)}) custom-call(bf16[16,4,4096]{2,1,0:T(4,128)(2,1)S(1)} %all-to-all-done.1.refs_0_, bf16[16,4,4096]{2,1,0:T(4,128)(2,1)S(1)} %collective-permute-done.4.refs_1_, bf16[4,704,4096]{2,1,0:T(8,128)(2,1)} %refs_2_.3, bf16[4,704,4096]{2,1,0:T(8,128)(2,1)} %refs_3_.3, ...), custom_call_target="tpu_custom_call" | custom-call | flops 1000 | bytes 1000 | tf_op jit(solution)/shard_map/experts/pallas_call | solution.py:323
  101.4 2.1 %add_convert_fusion.1 = bf16[16,4,4096]{2,1,0:T(4,128)(2,1)} fusion(bf16[16,4,4096]{2,1,0:T(4,128)(2,1)} %collective-permute-done.5, bf16[16,4,4096]{2,1,0:T(4,128)(2,1)S(1)} %get-tuple-element.39), kind=kLoop, calls=%fused_computation.1 | loop fusion | flops 1048576 | bytes 1572864 | tf_op jit(solution)/shard_map/convert_element_type | solution.py:347
  103.5 5.9 %all-to-all-start.3 = ((bf16[16,4,4096]{2,1,0:T(4,128)(2,1)}), bf16[16,4,4096]{2,1,0:T(4,128)(2,1)S(1)}, u32[]{:S(2)}, u32[]{:S(2)}) async-start(bf16[16,4,4096]{2,1,0:T(4,128)(2,1)} %add_convert_fusion.1), calls=%async_computation.3 | async-start | bytes 1048576 | tf_op jit(solution)/shard_map/all_to_all | solution.py:376
  109.5 3.3 %attend.1 = (bf16[64,256]{1,0:T(8,128)(2,1)S(1)}, bf16[64,256]{1,0:T(8,128)(2,1)S(1)}, bf16[64,256]{1,0:T(8,128)(2,1)S(1)}, bf16[64,256]{1,0:T(8,128)(2,1)S(1)},...) custom-call(s32[2]{0:T(128)S(1)} %pad_add_fusion.at_ref, ...), custom_call_target="tpu_custom_call" | custom-call | flops 1000 | bytes 1000 | tf_op jit(solution)/shard_map/attend/pallas_call | solution.py:349
  113.3 1.7 %collective-permute-start.7 = (bf16[64,256]{1,0:T(8,128)(2,1)S(1)}, bf16[64,256]{1,0:T(8,128)(2,1)S(1)}, u32[]{:S(2)}, u32[]{:S(2)}) collective-permute-start(bf16[64,256]{1,0:T(8,128)(2,1)S(1)} %get-tuple-element.44), channel_id=1, source_target_pairs={{0,2},{1,3},{2,0},{3,1},{4,6},{5,7},{6,4},{7,5},{8,10},{9,11},{10,... | collective-permute-start | bytes 98312 | tf_op jit(solution)/shard_map/ppermute | solution.py:362
  118.5 5.4 %all-to-all-done.3.refs_0_ = bf16[16,4,4096]{2,1,0:T(4,128)(2,1)S(1)} async-done(((bf16[16,4,4096]{2,1,0:T(4,128)(2,1)}), bf16[16,4,4096]{2,1,0:T(4,128)(2,1)S(1)}, u32[]{:S(2)}, u32[]{:S(2)}) %all-to-all-start.3) | async-done | bytes 524320 | tf_op jit(solution)/shard_map/all_to_all | solution.py:376
  123.9 4.1 %all-to-all-start.4 = ((bf16[16,4,4096]{2,1,0:T(4,128)(2,1)}), bf16[16,4,4096]{2,1,0:T(4,128)(2,1)S(1)}, u32[]{:S(2)}, u32[]{:S(2)}) async-start(bf16[16,4,4096]{2,1,0:T(4,128)(2,1)} %add_convert_fusion), calls=%async_computation.4 | async-start | bytes 1048576 | tf_op jit(solution)/shard_map/all_to_all | solution.py:376
  128.0 1.7 %collective-permute-start.10 = (bf16[64,256]{1,0:T(8,128)(2,1)S(1)}, bf16[64,256]{1,0:T(8,128)(2,1)S(1)}, u32[]{:S(2)}, u32[]{:S(2)}) collective-permute-start(bf16[64,256]{1,0:T(8,128)(2,1)S(1)} %get-tuple-element.47), channel_id=1, source_target_pairs={{0,5},{1,4},{2,7},{3,6},{4,1},{5,0},{6,3},{7,2},{8,13},{9,12},{10,... | collective-permute-start | bytes 98312 | tf_op jit(solution)/shard_map/ppermute | solution.py:362
  132.6 5.8 %collective-permute-done.10.refs_5_ = bf16[64,256]{1,0:T(8,128)(2,1)S(1)} collective-permute-done((bf16[64,256]{1,0:T(8,128)(2,1)S(1)}, bf16[64,256]{1,0:T(8,128)(2,1)S(1)}, u32[]{:S(2)}, u32[]{:S(2)}) %collective-permute-start.10) | collective-permute-done | bytes 32800 | tf_op jit(solution)/shard_map/ppermute | solution.py:362
  138.4 2.0 %collective-permute-done.11.refs_6_ = bf16[64,256]{1,0:T(8,128)(2,1)S(1)} collective-permute-done((bf16[64,256]{1,0:T(8,128)(2,1)S(1)}, bf16[64,256]{1,0:T(8,128)(2,1)S(1)}, u32[]{:S(2)}, u32[]{:S(2)}) %collective-permute-start.11) | collective-permute-done | bytes 32800 | tf_op jit(solution)/shard_map/ppermute | solution.py:362
  140.4 1.9 %collective-permute-done.9.refs_4_ = bf16[64,256]{1,0:T(8,128)(2,1)S(1)} collective-permute-done((bf16[64,256]{1,0:T(8,128)(2,1)S(1)}, bf16[64,256]{1,0:T(8,128)(2,1)S(1)}, u32[]{:S(2)}, u32[]{:S(2)}) %collective-permute-start.9) | collective-permute-done | bytes 32800 | tf_op jit(solution)/shard_map/ppermute | solution.py:362
  143.6 1.6 %mix.1 = bf16[64,4096]{1,0:T(8,128)(2,1)} custom-call(s32[2,64]{1,0:T(2,128)S(1)} %bitcast.6, f32[2,64]{1,0:T(2,128)S(1)} %bitcast.7, bf16[16,4,4096]{2,1,0:T(4,128)(2,1)S(1)} %all-to-all-done.3.refs_0_, bf16[16,4,4096]{2,1,0:T(4,128)(2,1)S(1)} %all-to-all-done.4.refs_1_), custom_call_target="tpu_custom_call" | custom-call | flops 1000 | bytes 1000 | tf_op jit(solution)/shard_map/mix/pallas_call | solution.py:377
  (34 shorter events, 11.7 us)
Async XLA Ops:
  4.2 29.2 %all-to-all-start = ((bf16[16,4,4096]{2,1,0:T(4,128)(2,1)}), bf16[16,4,4096]{2,1,0:T(4,128)(2,1)S(1)}, u32[]{:S(2)}, u32[]{:S(2)}) async-start(bf16[16,4,4096]{2,1,0:T(4,128)(2,1)} %get-tuple-element.29), calls=%async_computation | async-start | bytes 1048576 | tf_op jit(solution)/shard_map/all_to_all | solution.py:305
  11.6 20.0 %collective-permute-start = (bf16[16,2048]{1,0:T(8,128)(2,1)}, bf16[16,2048]{1,0:T(8,128)(2,1)S(1)}, u32[]{:S(2)}, u32[]{:S(2)}) collective-permute-start(bf16[16,2048]{1,0:T(8,128)(2,1)} %get-tuple-element.28.refs_0_), channel_id=1, source_target_pairs={{0,8},{1,9},{2,10},{3,11},{4,12},{5,13},{6,14},{7,15},{8,0},{9,1},... | collective-permute-start | bytes 196616 | tf_op jit(solution)/shard_map/ppermute | solution.py:293
  14.4 17.1 %collective-permute-start.1 = (bf16[16,2048]{1,0:T(8,128)(2,1)}, bf16[16,2048]{1,0:T(8,128)(2,1)S(1)}, u32[]{:S(2)}, u32[]{:S(2)}) collective-permute-start(bf16[16,2048]{1,0:T(8,128)(2,1)} %get-tuple-element.28.refs_0_), channel_id=1, source_target_pairs={{0,16},{1,17},{2,18},{3,19},{4,20},{5,21},{6,22},{7,23},{8,24},{9,... | collective-permute-start | bytes 196616 | tf_op jit(solution)/shard_map/ppermute | solution.py:293
  15.9 17.5 %collective-permute-start.2 = (bf16[16,2048]{1,0:T(8,128)(2,1)}, bf16[16,2048]{1,0:T(8,128)(2,1)S(1)}, u32[]{:S(2)}, u32[]{:S(2)}) collective-permute-start(bf16[16,2048]{1,0:T(8,128)(2,1)} %get-tuple-element.28.refs_0_), channel_id=1, source_target_pairs={{0,24},{1,25},{2,26},{3,27},{4,28},{5,29},{6,30},{7,31},{8,16},{9,... | collective-permute-start | bytes 196616 | tf_op jit(solution)/shard_map/ppermute | solution.py:293
  31.5 6.2 %copy-start.2 = (bf16[16,2048]{1,0:T(8,128)(2,1)}, bf16[16,2048]{1,0:T(8,128)(2,1)S(1)}, u32[]{:S(2)}) copy-start(bf16[16,2048]{1,0:T(8,128)(2,1)S(1)} %collective-permute-done.refs_1_) | copy-start | bytes 196612
  31.5 6.2 %copy-start.3 = (bf16[16,2048]{1,0:T(8,128)(2,1)}, bf16[16,2048]{1,0:T(8,128)(2,1)S(1)}, u32[]{:S(2)}) copy-start(bf16[16,2048]{1,0:T(8,128)(2,1)S(1)} %collective-permute-done.1.refs_2_) | copy-start | bytes 196612
  33.4 4.3 %copy-start.4 = (bf16[16,2048]{1,0:T(8,128)(2,1)}, bf16[16,2048]{1,0:T(8,128)(2,1)S(1)}, u32[]{:S(2)}) copy-start(bf16[16,2048]{1,0:T(8,128)(2,1)S(1)} %collective-permute-done.2.refs_3_) | copy-start | bytes 196612
  33.4 18.2 %all-to-all-start.1 = ((bf16[16,4,4096]{2,1,0:T(4,128)(2,1)}), bf16[16,4,4096]{2,1,0:T(4,128)(2,1)S(1)}, u32[]{:S(2)}, u32[]{:S(2)}) async-start(bf16[16,4,4096]{2,1,0:T(4,128)(2,1)} %get-tuple-element.32), calls=%async_computation.1 | async-start | bytes 1048576 | tf_op jit(solution)/shard_map/all_to_all | solution.py:308
  37.1 14.5 %collective-permute-start.3 = (bf16[16,4,4096]{2,1,0:T(4,128)(2,1)S(1)}, bf16[16,4,4096]{2,1,0:T(4,128)(2,1)S(1)}, u32[]{:S(2)}, u32[]{:S(2)}) collective-permute-start(bf16[16,4,4096]{2,1,0:T(4,128)(2,1)S(1)} %all-to-all-done.refs_0_), channel_id=1, source_target_pairs={{0,16},{16,0},{1,17},{17,1},{2,18},{18,2},{3,19},{19,3},{4,20},{20... | collective-permute-start | bytes 1572872 | tf_op jit(solution)/shard_map/ppermute | solution.py:314
  67.1 34.3 %all-to-all-start.2 = ((bf16[8,256,256]{2,1,0:T(8,128)(2,1)}), bf16[8,256,256]{2,1,0:T(8,128)(2,1)S(1)}, u32[]{:S(2)}, u32[]{:S(2)}) async-start(bf16[8,256,256]{2,1,0:T(8,128)(2,1)} %pack.1), calls=%async_computation.2 | async-start | bytes 2097152 | tf_op jit(solution)/shard_map/all_to_all | solution.py:341
  70.8 14.8 %collective-permute-start.4 = (bf16[16,4,4096]{2,1,0:T(4,128)(2,1)S(1)}, bf16[16,4,4096]{2,1,0:T(4,128)(2,1)S(1)}, u32[]{:S(2)}, u32[]{:S(2)}) collective-permute-start(bf16[16,4,4096]{2,1,0:T(4,128)(2,1)S(1)} %all-to-all-done.1.refs_0_), channel_id=1, source_target_pairs={{0,16},{16,0},{1,17},{17,1},{2,18},{18,2},{3,19},{19,3},{4,20},{20... | collective-permute-start | bytes 1572872 | tf_op jit(solution)/shard_map/ppermute | solution.py:314
  71.4 30.0 %collective-permute-start.5 = (bf16[16,4,4096]{2,1,0:T(4,128)(2,1)}, bf16[16,4,4096]{2,1,0:T(4,128)(2,1)}, u32[]{:S(2)}, u32[]{:S(2)}) collective-permute-start(bf16[16,4,4096]{2,1,0:T(4,128)(2,1)} %get-tuple-element.40), channel_id=1, source_target_pairs={{0,16},{16,0},{1,17},{17,1},{2,18},{18,2},{3,19},{19,3},{4,20},{20... | collective-permute-start | bytes 1572872 | tf_op jit(solution)/shard_map/ppermute | solution.py:346
  72.9 70.7 %copy-start = (s32[64,2]{0,1:T(2,128)S(1)}, s32[64,2]{0,1:T(2,128)}, u32[]{:S(2)}) copy-start(s32[64,2]{0,1:T(2,128)} %param.15) | copy-start | bytes 1540
  72.9 70.7 %copy-start.1 = (f32[64,2]{0,1:T(2,128)S(1)}, f32[64,2]{0,1:T(2,128)}, u32[]{:S(2)}) copy-start(f32[64,2]{0,1:T(2,128)} %param.16) | copy-start | bytes 1540
  100.8 14.2 %collective-permute-start.13 = (bf16[16,4,4096]{2,1,0:T(4,128)(2,1)}, bf16[16,4,4096]{2,1,0:T(4,128)(2,1)S(1)}, u32[]{:S(2)}, u32[]{:S(2)}) collective-permute-start(bf16[16,4,4096]{2,1,0:T(4,128)(2,1)} %get-tuple-element.52), channel_id=1, source_target_pairs={{0,16},{16,0},{1,17},{17,1},{2,18},{18,2},{3,19},{19,3},{4,20},{20... | collective-permute-start | bytes 1572872 | tf_op jit(solution)/shard_map/ppermute | solution.py:346
  103.5 20.4 %all-to-all-start.3 = ((bf16[16,4,4096]{2,1,0:T(4,128)(2,1)}), bf16[16,4,4096]{2,1,0:T(4,128)(2,1)S(1)}, u32[]{:S(2)}, u32[]{:S(2)}) async-start(bf16[16,4,4096]{2,1,0:T(4,128)(2,1)} %add_convert_fusion.1), calls=%async_computation.3 | async-start | bytes 1048576 | tf_op jit(solution)/shard_map/all_to_all | solution.py:376
  112.9 3.3 %collective-permute-start.6 = (bf16[64,256]{1,0:T(8,128)(2,1)S(1)}, bf16[64,256]{1,0:T(8,128)(2,1)S(1)}, u32[]{:S(2)}, u32[]{:S(2)}) collective-permute-start(bf16[64,256]{1,0:T(8,128)(2,1)S(1)} %get-tuple-element.43), channel_id=1, source_target_pairs={{0,1},{1,0},{2,3},{3,2},{4,5},{5,4},{6,7},{7,6},{8,9},{9,8},{10,11... | collective-permute-start | bytes 98312 | tf_op jit(solution)/shard_map/ppermute | solution.py:362
  113.3 4.2 %collective-permute-start.7 = (bf16[64,256]{1,0:T(8,128)(2,1)S(1)}, bf16[64,256]{1,0:T(8,128)(2,1)S(1)}, u32[]{:S(2)}, u32[]{:S(2)}) collective-permute-start(bf16[64,256]{1,0:T(8,128)(2,1)S(1)} %get-tuple-element.44), channel_id=1, source_target_pairs={{0,2},{1,3},{2,0},{3,1},{4,6},{5,7},{6,4},{7,5},{8,10},{9,11},{10,... | collective-permute-start | bytes 98312 | tf_op jit(solution)/shard_map/ppermute | solution.py:362
  115.0 3.5 %collective-permute-start.8 = (bf16[64,256]{1,0:T(8,128)(2,1)S(1)}, bf16[64,256]{1,0:T(8,128)(2,1)S(1)}, u32[]{:S(2)}, u32[]{:S(2)}) collective-permute-start(bf16[64,256]{1,0:T(8,128)(2,1)S(1)} %get-tuple-element.45), channel_id=1, source_target_pairs={{0,3},{1,2},{2,1},{3,0},{4,7},{5,6},{6,5},{7,4},{8,11},{9,10},{10,... | collective-permute-start | bytes 98312 | tf_op jit(solution)/shard_map/ppermute | solution.py:362
  123.9 19.7 %all-to-all-start.4 = ((bf16[16,4,4096]{2,1,0:T(4,128)(2,1)}), bf16[16,4,4096]{2,1,0:T(4,128)(2,1)S(1)}, u32[]{:S(2)}, u32[]{:S(2)}) async-start(bf16[16,4,4096]{2,1,0:T(4,128)(2,1)} %add_convert_fusion), calls=%async_computation.4 | async-start | bytes 1048576 | tf_op jit(solution)/shard_map/all_to_all | solution.py:376
  128.0 10.4 %collective-permute-start.10 = (bf16[64,256]{1,0:T(8,128)(2,1)S(1)}, bf16[64,256]{1,0:T(8,128)(2,1)S(1)}, u32[]{:S(2)}, u32[]{:S(2)}) collective-permute-start(bf16[64,256]{1,0:T(8,128)(2,1)S(1)} %get-tuple-element.47), channel_id=1, source_target_pairs={{0,5},{1,4},{2,7},{3,6},{4,1},{5,0},{6,3},{7,2},{8,13},{9,12},{10,... | collective-permute-start | bytes 98312 | tf_op jit(solution)/shard_map/ppermute | solution.py:362
  129.7 10.7 %collective-permute-start.11 = (bf16[64,256]{1,0:T(8,128)(2,1)S(1)}, bf16[64,256]{1,0:T(8,128)(2,1)S(1)}, u32[]{:S(2)}, u32[]{:S(2)}) collective-permute-start(bf16[64,256]{1,0:T(8,128)(2,1)S(1)} %get-tuple-element.48), channel_id=1, source_target_pairs={{0,6},{1,7},{2,4},{3,5},{4,2},{5,3},{6,0},{7,1},{8,14},{9,15},{10,... | collective-permute-start | bytes 98312 | tf_op jit(solution)/shard_map/ppermute | solution.py:362
  131.2 9.3 %collective-permute-start.12 = (bf16[64,256]{1,0:T(8,128)(2,1)S(1)}, bf16[64,256]{1,0:T(8,128)(2,1)S(1)}, u32[]{:S(2)}, u32[]{:S(2)}) collective-permute-start(bf16[64,256]{1,0:T(8,128)(2,1)S(1)} %get-tuple-element.49), channel_id=1, source_target_pairs={{0,7},{1,6},{2,5},{3,4},{4,3},{5,2},{6,1},{7,0},{8,15},{9,14},{10,... | collective-permute-start | bytes 98312 | tf_op jit(solution)/shard_map/ppermute | solution.py:362
  132.3 10.1 %collective-permute-start.9 = (bf16[64,256]{1,0:T(8,128)(2,1)S(1)}, bf16[64,256]{1,0:T(8,128)(2,1)S(1)}, u32[]{:S(2)}, u32[]{:S(2)}) collective-permute-start(bf16[64,256]{1,0:T(8,128)(2,1)S(1)} %get-tuple-element.46), channel_id=1, source_target_pairs={{0,4},{1,5},{2,6},{3,7},{4,0},{5,1},{6,2},{7,3},{8,12},{9,13},{10,... | collective-permute-start | bytes 98312 | tf_op jit(solution)/shard_map/ppermute | solution.py:362

commit v5 on v4

--- a/solution.py
+++ b/solution.py
@@ -303,7 +303,6 @@
         name="pack",
     )(queries, attn_keys, attn_values, *parts)
     recv = [lax.all_to_all(send[0], "exp", 0, 0, tiled=True)]
-    recv[0] = after(recv[0], parts)
     for rows in send[1:]:
         recv.append(lax.all_to_all(after(rows, recv[-1]), "exp", 0, 0, tiled=True))
     arrived = []
@@ -318,7 +317,7 @@
     position = jnp.stack([segment, place]).astype(jnp.int32)
     done, mine = [], []
     for chunk in range(chunks):
-        planes = [after(arrived[chunk][0], recv[-1])] + arrived[chunk][1:]
+        planes = [after(after(arrived[chunk][0], recv[-1]), parts)] + arrived[chunk][1:]
         total = seq_count * exp_count * step
         pieces = pl.pallas_call(
             functools.partial(ffn_kernel, chunk * experts, seq_count),
@@ -332,11 +331,15 @@
                 pltpu.SemaphoreType.DMA((experts * 3,)),
             ],
             compiler_params=params(44),
-            cost_estimate=LITTLE,
+            cost_estimate=pl.CostEstimate(
+                flops=6 * total * hidden * features,
+                bytes_accessed=3 * experts * 3 * hidden * features * 2,
+                transcendentals=total * hidden,
+            ),
             name="experts",
         )(*planes, gate_proj, up_proj, down_proj)
         done.append(pieces)
-    packed = after(packed, done[0][0])
+    packed = after(packed, recv[-1])
     halves = [[half * group + j for j in range(group)] for half in range(SEG_DEV)]
     got = lax.all_to_all(packed, "exp", 0, 0, axis_index_groups=halves, tiled=True)
     for chunk, pieces in enumerate(done):

time: 146 us -> 151 us (1.034)
  blocking collectives: 0 us -> 21.8 us
  waiting for transfers between devices: 58.3 us -> 47.7 us
  starting transfers between devices: 39.3 us -> 31.6 us
    all_to_all x0 -> x1, blocking collectives: none -> 21.8 us  [on_device(): recv = [lax.all_to_all(send[0], 'exp', 0, 0, tiled=True)]]
    all_to_all x1, waiting for transfers between devices: 10.7 us -> 0.01 us  [on_device(): recv.append(lax.all_to_all(after(rows, recv[-1]), 'exp', 0, 0, tiled=True))]
    all_to_all x1 -> x0, starting transfers between devices: 7.36 us -> none  [on_device(): recv = [lax.all_to_all(send[0], 'exp', 0, 0, tiled=True)]]
    all_to_all x2, starting transfers between devices: 10 us -> 8.43 us  [on_device(): back = [lax.all_to_all(rows, 'exp', 0, 0, tiled=True) for rows in mine]]
  transfers between devices with their start and end apart: 19 -> 18, of which waited for: 10 -> 8; matrix products, arithmetic and copies ran while one was open for 2% -> 2% of each run, Pallas kernels for 16% -> 26%
where the time goes in v5:
time: 151 us; the launch traced here: 149 us
  waiting for transfers between devices  47.7 us (32%)
  Pallas kernels  43.6 us (29%)
  starting transfers between devices  31.6 us (21%)
  blocking collectives  21.8 us (14%)
  other arithmetic  3.32 us (2%)
    pallas_call x2, Pallas kernels, on_device(): pl.pallas_call(functools.partial(ffn_kernel, chunk * experts, seq_count),...  30.8 us
    all_to_all x1, blocking collectives, on_device(): recv = [lax.all_to_all(send[0], 'exp', 0, 0, tiled=True)]  21.8 us
    ppermute x3, waiting for transfers between devices, on_device(): parts.append(lax.ppermute(sums, ('seq', 'exp'), pairs))  17.4 us
    ppermute x2, waiting for transfers between devices, on_device(): planes.append(lax.ppermute(rows, 'seq', pairs))  12.7 us
    ppermute x7, waiting for transfers between devices, on_device(): lax.ppermute(rows, 'exp', [(i, i ^ other) for i in range(exp_count)])  12 us
    all_to_all x2, starting transfers between devices, on_device(): back = [lax.all_to_all(rows, 'exp', 0, 0, tiled=True) for rows in mine]  8.43 us
    ppermute x7, starting transfers between devices, on_device(): lax.ppermute(rows, 'exp', [(i, i ^ other) for i in range(exp_count)])  6.76 us
    all_to_all x2, waiting for transfers between devices, on_device(): back = [lax.all_to_all(rows, 'exp', 0, 0, tiled=True) for rows in mine]  5.59 us
  transfers between devices with their start and end apart: 18, of which 8 were waited for; matrix products, arithmetic and copies ran while one was open for 2% of the time, Pallas kernels for 26%

profile of v5, /device:TPU:0, one launch (start us, length us, event | category | flops | bytes accessed | tf_op | source)
XLA Modules:
  0.0 149.4 jit_solution(8883409795492478990)
XLA Ops:
  0.6 3.5 %prep.1 = (bf16[16,4,4096]{2,1,0:T(4,128)(2,1)}, bf16[16,4,4096]{2,1,0:T(4,128)(2,1)}, bf16[16,2048]{1,0:T(8,128)(2,1)}) custom-call(bf16[64,4096]{1,0:T(8,128)(2,1)} %tok_hbm.1, f32[1,4096]{1,0:T(1,128)} %bitcast.8, s32[2,64]{1,0:T(2,128)} %bitcast.5, bf16[64,2048]{1,0:T(8,128)(2,1)} %k_hbm.3, bf16[64,2048]{1,0:T(8,128)(2,1)} %v_hbm.3), custom_call_target="tpu_custom_call" | custom-call | flops 1000 | bytes 1000 | tf_op jit(solution)/shard_map/prep/pallas_call | solution.py:267
  4.2 21.8 %all_to_all.25.refs_0_ = bf16[16,4,4096]{2,1,0:T(4,128)(2,1)S(1)} all-to-all(bf16[16,4,4096]{2,1,0:T(4,128)(2,1)} %get-tuple-element.31), channel_id=1, replica_groups=mesh['seq'=2,'exp'=16] {'exp'}, dimensions={0} | all-to-all | bytes 1048576 | tf_op jit(solution)/shard_map/all_to_all | solution.py:305
  26.0 4.1 %all-to-all-start.1 = ((bf16[16,4,4096]{2,1,0:T(4,128)(2,1)}), bf16[16,4,4096]{2,1,0:T(4,128)(2,1)S(1)}, u32[]{:S(2)}, u32[]{:S(2)}) async-start(bf16[16,4,4096]{2,1,0:T(4,128)(2,1)} %get-tuple-element.32), calls=%async_computation.1 | async-start | bytes 1048576 | tf_op jit(solution)/shard_map/all_to_all | solution.py:307
  30.1 2.8 %collective-permute-start = (bf16[16,2048]{1,0:T(8,128)(2,1)}, bf16[16,2048]{1,0:T(8,128)(2,1)S(1)}, u32[]{:S(2)}, u32[]{:S(2)}) collective-permute-start(bf16[16,2048]{1,0:T(8,128)(2,1)} %get-tuple-element.29.refs_0_), channel_id=1, source_target_pairs={{0,8},{1,9},{2,10},{3,11},{4,12},{5,13},{6,14},{7,15},{8,0},{9,1},... | collective-permute-start | bytes 196616 | tf_op jit(solution)/shard_map/ppermute | solution.py:293
  32.9 1.5 %collective-permute-start.1 = (bf16[16,2048]{1,0:T(8,128)(2,1)}, bf16[16,2048]{1,0:T(8,128)(2,1)S(1)}, u32[]{:S(2)}, u32[]{:S(2)}) collective-permute-start(bf16[16,2048]{1,0:T(8,128)(2,1)} %get-tuple-element.29.refs_0_), channel_id=1, source_target_pairs={{0,16},{1,17},{2,18},{3,19},{4,20},{5,21},{6,22},{7,23},{8,24},{9,... | collective-permute-start | bytes 196616 | tf_op jit(solution)/shard_map/ppermute | solution.py:293
  34.6 15.5 %collective-permute-done.refs_1_ = bf16[16,2048]{1,0:T(8,128)(2,1)S(1)} collective-permute-done((bf16[16,2048]{1,0:T(8,128)(2,1)}, bf16[16,2048]{1,0:T(8,128)(2,1)S(1)}, u32[]{:S(2)}, u32[]{:S(2)}) %collective-permute-start) | collective-permute-done | bytes 65568 | tf_op jit(solution)/shard_map/ppermute | solution.py:293
  50.1 1.9 %collective-permute-done.2.refs_3_ = bf16[16,2048]{1,0:T(8,128)(2,1)S(1)} collective-permute-done((bf16[16,2048]{1,0:T(8,128)(2,1)}, bf16[16,2048]{1,0:T(8,128)(2,1)S(1)}, u32[]{:S(2)}, u32[]{:S(2)}) %collective-permute-start.2) | collective-permute-done | bytes 65568 | tf_op jit(solution)/shard_map/ppermute | solution.py:293
  52.6 3.2 %pack.1 = bf16[8,256,256]{2,1,0:T(8,128)(2,1)} custom-call(bf16[64,2048]{1,0:T(8,128)(2,1)} %q_hbm.1, bf16[64,2048]{1,0:T(8,128)(2,1)} %k_hbm.3, bf16[64,2048]{1,0:T(8,128)(2,1)} %v_hbm.3, bf16[16,2048]{1,0:T(8,128)(2,1)} %get-tuple-element.29.refs_0_, bf16[16,2048]{1,0:T(8,128)(2,1)} %copy-done.2, bf16[16,2048]{1,0:T(8,128)(2,1)} %copy-done.3, ...), custom_call_target="tpu_custom_call" | custom-call | flops 1000 | bytes 1000 | tf_op jit(solution)/shard_map/pack/pallas_call | solution.py:295
  55.9 3.6 %all-to-all-start.2 = ((bf16[8,256,256]{2,1,0:T(8,128)(2,1)}), bf16[8,256,256]{2,1,0:T(8,128)(2,1)S(1)}, u32[]{:S(2)}, u32[]{:S(2)}) async-start(bf16[8,256,256]{2,1,0:T(8,128)(2,1)} %pack.1), calls=%async_computation.2 | async-start | bytes 2097152 | tf_op jit(solution)/shard_map/all_to_all | solution.py:344
  61.5 12.7 %collective-permute-done.3.refs_1_ = bf16[16,4,4096]{2,1,0:T(4,128)(2,1)S(1)} collective-permute-done((bf16[16,4,4096]{2,1,0:T(4,128)(2,1)S(1)}, bf16[16,4,4096]{2,1,0:T(4,128)(2,1)S(1)}, u32[]{:S(2)}, u32[]{:S(2)}) %collective-permute-start.3) | collective-permute-done | bytes 524320 | tf_op jit(solution)/shard_map/ppermute | solution.py:313
  74.2 15.5 %experts.2 = (bf16[16,4,4096]{2,1,0:T(4,128)(2,1)S(1)}, bf16[16,4,4096]{2,1,0:T(4,128)(2,1)}) custom-call(bf16[16,4,4096]{2,1,0:T(4,128)(2,1)S(1)} %all_to_all.25.refs_0_, bf16[16,4,4096]{2,1,0:T(4,128)(2,1)S(1)} %collective-permute-done.3.refs_1_, bf16[4,704,4096]{2,1,0:T(8,128)(2,1)} %refs_2_.3, bf16[4,704,4096]{2,1,0:T(8,128)(2,1)} %refs_3_.3, ...), custom_call_target="tpu_custom_call" | custom-call | flops 2214592512 | bytes 103809024 | tf_op jit(solution)/shard_map/experts/pallas_call | solution.py:322
  90.3 15.3 %experts.3 = (bf16[16,4,4096]{2,1,0:T(4,128)(2,1)S(1)}, bf16[16,4,4096]{2,1,0:T(4,128)(2,1)}) custom-call(bf16[16,4,4096]{2,1,0:T(4,128)(2,1)S(1)} %all-to-all-done.1.refs_0_, bf16[16,4,4096]{2,1,0:T(4,128)(2,1)S(1)} %collective-permute-done.4.refs_1_, bf16[4,704,4096]{2,1,0:T(8,128)(2,1)} %refs_2_.3, bf16[4,704,4096]{2,1,0:T(8,128)(2,1)} %refs_3_.3, ...), custom_call_target="tpu_custom_call" | custom-call | flops 2214592512 | bytes 103809024 | tf_op jit(solution)/shard_map/experts/pallas_call | solution.py:322
  105.6 1.6 %collective-permute-start.13 = (bf16[16,4,4096]{2,1,0:T(4,128)(2,1)}, bf16[16,4,4096]{2,1,0:T(4,128)(2,1)S(1)}, u32[]{:S(2)}, u32[]{:S(2)}) collective-permute-start(bf16[16,4,4096]{2,1,0:T(4,128)(2,1)} %get-tuple-element.54), channel_id=1, source_target_pairs={{0,16},{16,0},{1,17},{17,1},{2,18},{18,2},{3,19},{19,3},{4,20},{20... | collective-permute-start | bytes 1572872 | tf_op jit(solution)/shard_map/ppermute | solution.py:349
  107.2 2.1 %add_convert_fusion.1 = bf16[16,4,4096]{2,1,0:T(4,128)(2,1)} fusion(bf16[16,4,4096]{2,1,0:T(4,128)(2,1)} %collective-permute-done.5, bf16[16,4,4096]{2,1,0:T(4,128)(2,1)S(1)} %get-tuple-element.41), kind=kLoop, calls=%fused_computation.1 | loop fusion | flops 1048576 | bytes 1572864 | tf_op jit(solution)/shard_map/convert_element_type | solution.py:350
  109.3 4.3 %all-to-all-start.3 = ((bf16[16,4,4096]{2,1,0:T(4,128)(2,1)}), bf16[16,4,4096]{2,1,0:T(4,128)(2,1)S(1)}, u32[]{:S(2)}, u32[]{:S(2)}) async-start(bf16[16,4,4096]{2,1,0:T(4,128)(2,1)} %add_convert_fusion.1), calls=%async_computation.3 | async-start | bytes 1048576 | tf_op jit(solution)/shard_map/all_to_all | solution.py:379
  113.7 3.2 %attend.1 = (bf16[64,256]{1,0:T(8,128)(2,1)S(1)}, bf16[64,256]{1,0:T(8,128)(2,1)S(1)}, bf16[64,256]{1,0:T(8,128)(2,1)S(1)}, bf16[64,256]{1,0:T(8,128)(2,1)S(1)},...) custom-call(s32[2]{0:T(128)S(1)} %pad_add_fusion.at_ref, ...), custom_call_target="tpu_custom_call" | custom-call | flops 1000 | bytes 1000 | tf_op jit(solution)/shard_map/attend/pallas_call | solution.py:352
  117.4 1.7 %collective-permute-start.7 = (bf16[64,256]{1,0:T(8,128)(2,1)S(1)}, bf16[64,256]{1,0:T(8,128)(2,1)S(1)}, u32[]{:S(2)}, u32[]{:S(2)}) collective-permute-start(bf16[64,256]{1,0:T(8,128)(2,1)S(1)} %get-tuple-element.46), channel_id=1, source_target_pairs={{0,2},{1,3},{2,0},{3,1},{4,6},{5,7},{6,4},{7,5},{8,10},{9,11},{10,... | collective-permute-start | bytes 98312 | tf_op jit(solution)/shard_map/ppermute | solution.py:365
  122.5 5.6 %all-to-all-done.3.refs_0_ = bf16[16,4,4096]{2,1,0:T(4,128)(2,1)S(1)} async-done(((bf16[16,4,4096]{2,1,0:T(4,128)(2,1)}), bf16[16,4,4096]{2,1,0:T(4,128)(2,1)S(1)}, u32[]{:S(2)}, u32[]{:S(2)}) %all-to-all-start.3) | async-done | bytes 524320 | tf_op jit(solution)/shard_map/all_to_all | solution.py:379
  128.1 4.1 %all-to-all-start.4 = ((bf16[16,4,4096]{2,1,0:T(4,128)(2,1)}), bf16[16,4,4096]{2,1,0:T(4,128)(2,1)S(1)}, u32[]{:S(2)}, u32[]{:S(2)}) async-start(bf16[16,4,4096]{2,1,0:T(4,128)(2,1)} %add_convert_fusion), calls=%async_computation.4 | async-start | bytes 1048576 | tf_op jit(solution)/shard_map/all_to_all | solution.py:379
  132.2 1.9 %collective-permute-start.9 = (bf16[64,256]{1,0:T(8,128)(2,1)S(1)}, bf16[64,256]{1,0:T(8,128)(2,1)S(1)}, u32[]{:S(2)}, u32[]{:S(2)}) collective-permute-start(bf16[64,256]{1,0:T(8,128)(2,1)S(1)} %get-tuple-element.48), channel_id=1, source_target_pairs={{0,4},{1,5},{2,6},{3,7},{4,0},{5,1},{6,2},{7,3},{8,12},{9,13},{10,... | collective-permute-start | bytes 98312 | tf_op jit(solution)/shard_map/ppermute | solution.py:365
  134.2 2.4 %collective-permute-start.11 = (bf16[64,256]{1,0:T(8,128)(2,1)S(1)}, bf16[64,256]{1,0:T(8,128)(2,1)S(1)}, u32[]{:S(2)}, u32[]{:S(2)}) collective-permute-start(bf16[64,256]{1,0:T(8,128)(2,1)S(1)} %get-tuple-element.50), channel_id=1, source_target_pairs={{0,6},{1,7},{2,4},{3,5},{4,2},{5,3},{6,0},{7,1},{8,14},{9,15},{10,... | collective-permute-start | bytes 98312 | tf_op jit(solution)/shard_map/ppermute | solution.py:365
  136.8 6.8 %collective-permute-done.9.refs_4_ = bf16[64,256]{1,0:T(8,128)(2,1)S(1)} collective-permute-done((bf16[64,256]{1,0:T(8,128)(2,1)S(1)}, bf16[64,256]{1,0:T(8,128)(2,1)S(1)}, u32[]{:S(2)}, u32[]{:S(2)}) %collective-permute-start.9) | collective-permute-done | bytes 32800 | tf_op jit(solution)/shard_map/ppermute | solution.py:365
  143.6 2.9 %collective-permute-done.11.refs_6_ = bf16[64,256]{1,0:T(8,128)(2,1)S(1)} collective-permute-done((bf16[64,256]{1,0:T(8,128)(2,1)S(1)}, bf16[64,256]{1,0:T(8,128)(2,1)S(1)}, u32[]{:S(2)}, u32[]{:S(2)}) %collective-permute-start.11) | collective-permute-done | bytes 32800 | tf_op jit(solution)/shard_map/ppermute | solution.py:365
  147.8 1.6 %mix.1 = bf16[64,4096]{1,0:T(8,128)(2,1)} custom-call(s32[2,64]{1,0:T(2,128)S(1)} %bitcast.6, f32[2,64]{1,0:T(2,128)S(1)} %bitcast.7, bf16[16,4,4096]{2,1,0:T(4,128)(2,1)S(1)} %all-to-all-done.3.refs_0_, bf16[16,4,4096]{2,1,0:T(4,128)(2,1)S(1)} %all-to-all-done.4.refs_1_), custom_call_target="tpu_custom_call" | custom-call | flops 1000 | bytes 1000 | tf_op jit(solution)/shard_map/mix/pallas_call | solution.py:380
  (33 shorter events, 9.0 us)
Async XLA Ops:
  26.0 29.8 %all-to-all-start.1 = ((bf16[16,4,4096]{2,1,0:T(4,128)(2,1)}), bf16[16,4,4096]{2,1,0:T(4,128)(2,1)S(1)}, u32[]{:S(2)}, u32[]{:S(2)}) async-start(bf16[16,4,4096]{2,1,0:T(4,128)(2,1)} %get-tuple-element.32), calls=%async_computation.1 | async-start | bytes 1048576 | tf_op jit(solution)/shard_map/all_to_all | solution.py:307
  30.1 20.0 %collective-permute-start = (bf16[16,2048]{1,0:T(8,128)(2,1)}, bf16[16,2048]{1,0:T(8,128)(2,1)S(1)}, u32[]{:S(2)}, u32[]{:S(2)}) collective-permute-start(bf16[16,2048]{1,0:T(8,128)(2,1)} %get-tuple-element.29.refs_0_), channel_id=1, source_target_pairs={{0,8},{1,9},{2,10},{3,11},{4,12},{5,13},{6,14},{7,15},{8,0},{9,1},... | collective-permute-start | bytes 196616 | tf_op jit(solution)/shard_map/ppermute | solution.py:293
  32.9 17.1 %collective-permute-start.1 = (bf16[16,2048]{1,0:T(8,128)(2,1)}, bf16[16,2048]{1,0:T(8,128)(2,1)S(1)}, u32[]{:S(2)}, u32[]{:S(2)}) collective-permute-start(bf16[16,2048]{1,0:T(8,128)(2,1)} %get-tuple-element.29.refs_0_), channel_id=1, source_target_pairs={{0,16},{1,17},{2,18},{3,19},{4,20},{5,21},{6,22},{7,23},{8,24},{9,... | collective-permute-start | bytes 196616 | tf_op jit(solution)/shard_map/ppermute | solution.py:293
  34.5 17.5 %collective-permute-start.2 = (bf16[16,2048]{1,0:T(8,128)(2,1)}, bf16[16,2048]{1,0:T(8,128)(2,1)S(1)}, u32[]{:S(2)}, u32[]{:S(2)}) collective-permute-start(bf16[16,2048]{1,0:T(8,128)(2,1)} %get-tuple-element.29.refs_0_), channel_id=1, source_target_pairs={{0,24},{1,25},{2,26},{3,27},{4,28},{5,29},{6,30},{7,31},{8,16},{9,... | collective-permute-start | bytes 196616 | tf_op jit(solution)/shard_map/ppermute | solution.py:293
  50.1 1.9 %copy-start.2 = (bf16[16,2048]{1,0:T(8,128)(2,1)}, bf16[16,2048]{1,0:T(8,128)(2,1)S(1)}, u32[]{:S(2)}) copy-start(bf16[16,2048]{1,0:T(8,128)(2,1)S(1)} %collective-permute-done.refs_1_) | copy-start | bytes 196612
  50.1 1.9 %copy-start.3 = (bf16[16,2048]{1,0:T(8,128)(2,1)}, bf16[16,2048]{1,0:T(8,128)(2,1)S(1)}, u32[]{:S(2)}) copy-start(bf16[16,2048]{1,0:T(8,128)(2,1)S(1)} %collective-permute-done.1.refs_2_) | copy-start | bytes 196612
  52.0 0.6 copy-start.4
  55.9 51.3 %all-to-all-start.2 = ((bf16[8,256,256]{2,1,0:T(8,128)(2,1)}), bf16[8,256,256]{2,1,0:T(8,128)(2,1)S(1)}, u32[]{:S(2)}, u32[]{:S(2)}) async-start(bf16[8,256,256]{2,1,0:T(8,128)(2,1)} %pack.1), calls=%async_computation.2 | async-start | bytes 2097152 | tf_op jit(solution)/shard_map/all_to_all | solution.py:344
  59.4 14.8 %collective-permute-start.3 = (bf16[16,4,4096]{2,1,0:T(4,128)(2,1)S(1)}, bf16[16,4,4096]{2,1,0:T(4,128)(2,1)S(1)}, u32[]{:S(2)}, u32[]{:S(2)}) collective-permute-start(bf16[16,4,4096]{2,1,0:T(4,128)(2,1)S(1)} %all_to_all.25.refs_0_), channel_id=1, source_target_pairs={{0,16},{16,0},{1,17},{17,1},{2,18},{18,2},{3,19},{19,3},{4,20},{20... | collective-permute-start | bytes 1572872 | tf_op jit(solution)/shard_map/ppermute | solution.py:313
  60.0 30.3 %collective-permute-start.4 = (bf16[16,4,4096]{2,1,0:T(4,128)(2,1)S(1)}, bf16[16,4,4096]{2,1,0:T(4,128)(2,1)S(1)}, u32[]{:S(2)}, u32[]{:S(2)}) collective-permute-start(bf16[16,4,4096]{2,1,0:T(4,128)(2,1)S(1)} %all-to-all-done.1.refs_0_), channel_id=1, source_target_pairs={{0,16},{16,0},{1,17},{17,1},{2,18},{18,2},{3,19},{19,3},{4,20},{20... | collective-permute-start | bytes 1572872 | tf_op jit(solution)/shard_map/ppermute | solution.py:313
  89.7 17.5 %collective-permute-start.5 = (bf16[16,4,4096]{2,1,0:T(4,128)(2,1)}, bf16[16,4,4096]{2,1,0:T(4,128)(2,1)}, u32[]{:S(2)}, u32[]{:S(2)}) collective-permute-start(bf16[16,4,4096]{2,1,0:T(4,128)(2,1)} %get-tuple-element.42), channel_id=1, source_target_pairs={{0,16},{16,0},{1,17},{17,1},{2,18},{18,2},{3,19},{19,3},{4,20},{20... | collective-permute-start | bytes 1572872 | tf_op jit(solution)/shard_map/ppermute | solution.py:349
  90.3 57.5 %copy-start = (s32[64,2]{0,1:T(2,128)S(1)}, s32[64,2]{0,1:T(2,128)}, u32[]{:S(2)}) copy-start(s32[64,2]{0,1:T(2,128)} %param.15) | copy-start | bytes 1540
  90.3 57.5 %copy-start.1 = (f32[64,2]{0,1:T(2,128)S(1)}, f32[64,2]{0,1:T(2,128)}, u32[]{:S(2)}) copy-start(f32[64,2]{0,1:T(2,128)} %param.16) | copy-start | bytes 1540
  105.6 13.5 %collective-permute-start.13 = (bf16[16,4,4096]{2,1,0:T(4,128)(2,1)}, bf16[16,4,4096]{2,1,0:T(4,128)(2,1)S(1)}, u32[]{:S(2)}, u32[]{:S(2)}) collective-permute-start(bf16[16,4,4096]{2,1,0:T(4,128)(2,1)} %get-tuple-element.54), channel_id=1, source_target_pairs={{0,16},{16,0},{1,17},{17,1},{2,18},{18,2},{3,19},{19,3},{4,20},{20... | collective-permute-start | bytes 1572872 | tf_op jit(solution)/shard_map/ppermute | solution.py:349
  109.3 18.8 %all-to-all-start.3 = ((bf16[16,4,4096]{2,1,0:T(4,128)(2,1)}), bf16[16,4,4096]{2,1,0:T(4,128)(2,1)S(1)}, u32[]{:S(2)}, u32[]{:S(2)}) async-start(bf16[16,4,4096]{2,1,0:T(4,128)(2,1)} %add_convert_fusion.1), calls=%async_computation.3 | async-start | bytes 1048576 | tf_op jit(solution)/shard_map/all_to_all | solution.py:379
  116.9 3.3 %collective-permute-start.6 = (bf16[64,256]{1,0:T(8,128)(2,1)S(1)}, bf16[64,256]{1,0:T(8,128)(2,1)S(1)}, u32[]{:S(2)}, u32[]{:S(2)}) collective-permute-start(bf16[64,256]{1,0:T(8,128)(2,1)S(1)} %get-tuple-element.45), channel_id=1, source_target_pairs={{0,1},{1,0},{2,3},{3,2},{4,5},{5,4},{6,7},{7,6},{8,9},{9,8},{10,11... | collective-permute-start | bytes 98312 | tf_op jit(solution)/shard_map/ppermute | solution.py:365
  117.4 4.1 %collective-permute-start.7 = (bf16[64,256]{1,0:T(8,128)(2,1)S(1)}, bf16[64,256]{1,0:T(8,128)(2,1)S(1)}, u32[]{:S(2)}, u32[]{:S(2)}) collective-permute-start(bf16[64,256]{1,0:T(8,128)(2,1)S(1)} %get-tuple-element.46), channel_id=1, source_target_pairs={{0,2},{1,3},{2,0},{3,1},{4,6},{5,7},{6,4},{7,5},{8,10},{9,11},{10,... | collective-permute-start | bytes 98312 | tf_op jit(solution)/shard_map/ppermute | solution.py:365
  119.1 3.4 %collective-permute-start.8 = (bf16[64,256]{1,0:T(8,128)(2,1)S(1)}, bf16[64,256]{1,0:T(8,128)(2,1)S(1)}, u32[]{:S(2)}, u32[]{:S(2)}) collective-permute-start(bf16[64,256]{1,0:T(8,128)(2,1)S(1)} %get-tuple-element.47), channel_id=1, source_target_pairs={{0,3},{1,2},{2,1},{3,0},{4,7},{5,6},{6,5},{7,4},{8,11},{9,10},{10,... | collective-permute-start | bytes 98312 | tf_op jit(solution)/shard_map/ppermute | solution.py:365
  128.1 19.7 %all-to-all-start.4 = ((bf16[16,4,4096]{2,1,0:T(4,128)(2,1)}), bf16[16,4,4096]{2,1,0:T(4,128)(2,1)S(1)}, u32[]{:S(2)}, u32[]{:S(2)}) async-start(bf16[16,4,4096]{2,1,0:T(4,128)(2,1)} %add_convert_fusion), calls=%async_computation.4 | async-start | bytes 1048576 | tf_op jit(solution)/shard_map/all_to_all | solution.py:379
  132.2 11.4 %collective-permute-start.9 = (bf16[64,256]{1,0:T(8,128)(2,1)S(1)}, bf16[64,256]{1,0:T(8,128)(2,1)S(1)}, u32[]{:S(2)}, u32[]{:S(2)}) collective-permute-start(bf16[64,256]{1,0:T(8,128)(2,1)S(1)} %get-tuple-element.48), channel_id=1, source_target_pairs={{0,4},{1,5},{2,6},{3,7},{4,0},{5,1},{6,2},{7,3},{8,12},{9,13},{10,... | collective-permute-start | bytes 98312 | tf_op jit(solution)/shard_map/ppermute | solution.py:365
  134.2 9.5 %collective-permute-start.10 = (bf16[64,256]{1,0:T(8,128)(2,1)S(1)}, bf16[64,256]{1,0:T(8,128)(2,1)S(1)}, u32[]{:S(2)}, u32[]{:S(2)}) collective-permute-start(bf16[64,256]{1,0:T(8,128)(2,1)S(1)} %get-tuple-element.49), channel_id=1, source_target_pairs={{0,5},{1,4},{2,7},{3,6},{4,1},{5,0},{6,3},{7,2},{8,13},{9,12},{10,... | collective-permute-start | bytes 98312 | tf_op jit(solution)/shard_map/ppermute | solution.py:365
  134.2 12.4 %collective-permute-start.11 = (bf16[64,256]{1,0:T(8,128)(2,1)S(1)}, bf16[64,256]{1,0:T(8,128)(2,1)S(1)}, u32[]{:S(2)}, u32[]{:S(2)}) collective-permute-start(bf16[64,256]{1,0:T(8,128)(2,1)S(1)} %get-tuple-element.50), channel_id=1, source_target_pairs={{0,6},{1,7},{2,4},{3,5},{4,2},{5,3},{6,0},{7,1},{8,14},{9,15},{10,... | collective-permute-start | bytes 98312 | tf_op jit(solution)/shard_map/ppermute | solution.py:365
  136.6 10.0 %collective-permute-start.12 = (bf16[64,256]{1,0:T(8,128)(2,1)S(1)}, bf16[64,256]{1,0:T(8,128)(2,1)S(1)}, u32[]{:S(2)}, u32[]{:S(2)}) collective-permute-start(bf16[64,256]{1,0:T(8,128)(2,1)S(1)} %get-tuple-element.51), channel_id=1, source_target_pairs={{0,7},{1,6},{2,5},{3,4},{4,3},{5,2},{6,1},{7,0},{8,15},{9,14},{10,... | collective-permute-start | bytes 98312 | tf_op jit(solution)/shard_map/ppermute | solution.py:365

commit v6 on v5

--- a/solution.py
+++ b/solution.py
@@ -14,6 +14,7 @@
 SEG_DEV = 2
 CAP = 2
 CHUNKS = 2
+FLIGHT = 2
 
 EPS = 1e-05
 NEG = -1e30
@@ -49,19 +50,15 @@
     return found
 
 
-def prep_kernel(block, tok_hbm, gain_ref, ids_ref, k_hbm, v_hbm, *refs):
-    out_refs, sum_ref, (tok_ref, k_ref, v_ref, sem) = refs[:-5], refs[-5], refs[-4:]
-    copies = [
-        pltpu.make_async_copy(frm, to, sem.at[at])
-        for at, (frm, to) in enumerate(((tok_hbm, tok_ref), (k_hbm, k_ref), (v_hbm, v_ref)))
-    ]
-    for copy in copies:
-        copy.start()
+def prep_kernel(tok_hbm, gain_ref, ids_ref, *refs):
+    out_refs, (tok_ref, sem) = refs[:-2], refs[-2:]
+    copy = pltpu.make_async_copy(tok_hbm, tok_ref, sem.at[0])
+    copy.start()
     n = tok_ref.shape[0]
     first, second = slots(ids_ref[...])
     place = lax.broadcasted_iota(jnp.int32, (EXPERTS * CAP, n), 0)
     pick = jnp.where((place == first) | (place == second), 1.0, 0.0).astype(BF16)
-    copies[0].wait()
+    copy.wait()
     values = tok_ref[...].astype(F32)
     inv_rms = lax.rsqrt(jnp.mean(values * values, axis=-1, keepdims=True) + EPS)
     normed = (values * inv_rms * gain_ref[...]).astype(BF16)
@@ -71,18 +68,22 @@
         for chunk, out_ref in enumerate(out_refs):
             lower = (dest * len(out_refs) + chunk) * step
             out_ref[dest] = rows[lower : lower + step].astype(BF16)
-    count = n // block
-    row = lax.broadcasted_iota(jnp.int32, (count, n), 0)
-    column = lax.broadcasted_iota(jnp.int32, (count, n), 1)
+
+
+def sums_kernel(block, recv_ref, out_ref):
+    sources, rows, width = recv_ref.shape
+    tokens = rows // 3
+    total = sources * tokens
+    row = lax.broadcasted_iota(jnp.int32, (SUMS, total), 0)
+    column = lax.broadcasted_iota(jnp.int32, (SUMS, total), 1)
     member = jnp.where(column // block == row, 1.0, 0.0).astype(BF16)
-    for which, ref in enumerate((k_ref, v_ref)):
-        copies[which + 1].wait()
-        summed = jnp.dot(member, ref[...], preferred_element_type=F32) * (1.0 / math.sqrt(block))
-        sum_ref[which * count : (which + 1) * count] = summed.astype(BF16)
-
-
-def pack_kernel(q_hbm, k_hbm, v_hbm, *refs):
-    sum_refs, out_ref, sem = refs[:-2], refs[-2], refs[-1]
+    for which in range(2):
+        values = recv_ref[:, (which + 1) * tokens : (which + 2) * tokens].reshape(total, width)
+        summed = jnp.dot(member, values, preferred_element_type=F32) * (1.0 / math.sqrt(block))
+        out_ref[which * SUMS : (which + 1) * SUMS] = summed.astype(BF16)
+
+
+def pack_kernel(q_hbm, k_hbm, v_hbm, out_ref, sem):
     dests, _, width = out_ref.shape
     tokens = q_hbm.shape[0]
     copies = []
@@ -97,31 +98,20 @@
             )
     for copy in copies:
         copy.start()
-    for dest in range(dests):
-        lower = 3 * tokens
-        for ref in sum_refs:
-            upper = lower + ref.shape[0]
-            out_ref[dest, lower:upper] = ref[:, dest * width : (dest + 1) * width]
-            lower = upper
     for copy in copies:
         copy.wait()
 
 
 def attend_kernel(query_rows, tokens, segs, at_ref, recv_ref, *refs):
-    out_refs, mixed_ref = refs[:-1], refs[-1]
+    sum_refs, out_refs, mixed_ref = refs[:segs], refs[segs:-1], refs[-1]
     sources, _, width = recv_ref.shape
     seg_len = sources * tokens
     query, key, value = (
         recv_ref[:, which * tokens : (which + 1) * tokens].reshape(seg_len, width) for which in range(3)
     )
     sum_total = segs * SUMS
-    per = SUMS // sources
-    sum_rows = [
-        recv_ref[:, 3 * tokens + at * per : 3 * tokens + (at + 1) * per].reshape(SUMS, width)
-        for at in range(2 * segs)
-    ]
-    sum_keys = jnp.concatenate(sum_rows[0::2], axis=0)
-    sum_values = jnp.concatenate(sum_rows[1::2], axis=0)
+    sum_keys = jnp.concatenate([ref[:SUMS] for ref in sum_refs], axis=0)
+    sum_values = jnp.concatenate([ref[SUMS:] for ref in sum_refs], axis=0)
     scale = 1.0 / math.sqrt(HDIM)
     segment = at_ref[0]
     lane = lax.broadcasted_iota(jnp.int32, (1, width), 1)
@@ -179,8 +169,16 @@
         for which, ref in enumerate((gate_ref, up_ref, down_ref)):
             at = expert * 3 + which
             copy = pltpu.make_async_copy(ref.at[base + expert], buf.at[at], sem.at[at])
-            copy.start()
             copies.append(copy)
+    for copy in copies[:FLIGHT]:
+        copy.start()
+
+    def weight(at):
+        copies[at].wait()
+        if at + FLIGHT < len(copies):
+            copies[at + FLIGHT].start()
+        return buf[at]
+
     total = planes * sources * step
     for plane in range(planes):
         for source in range(sources):
@@ -195,13 +193,10 @@
     nt = (((1,), (1,)), ((), ()))
     for expert in range(experts):
         rows = x_ref[expert * per : (expert + 1) * per]
-        copies[expert * 3].wait()
-        gate = lax.dot_general(rows, buf[expert * 3], nt, preferred_element_type=F32)
-        copies[expert * 3 + 1].wait()
-        up = lax.dot_general(rows, buf[expert * 3 + 1], nt, preferred_element_type=F32)
+        gate = lax.dot_general(rows, weight(expert * 3), nt, preferred_element_type=F32)
+        up = lax.dot_general(rows, weight(expert * 3 + 1), nt, preferred_element_type=F32)
         hidden = (gate / (1.0 + jnp.exp(-gate)) * up).astype(BF16)
-        copies[expert * 3 + 2].wait()
-        piece = jnp.dot(hidden, buf[expert * 3 + 2], preferred_element_type=F32)
+        piece = jnp.dot(hidden, weight(expert * 3 + 2), preferred_element_type=F32)
         x_ref[expert * per : (expert + 1) * per] = piece.astype(BF16)
     inverse = (to // step) * CAP + (to % step // CAP) * per + to % CAP
     unsort = jnp.where(frm == inverse, 1.0, 0.0).astype(BF16)
@@ -263,45 +258,30 @@
     att = queries.shape[1]
     width = att // group
 
-    block = seg_len // SUMS
-    *send, sums = pl.pallas_call(
-        functools.partial(prep_kernel, block),
-        out_shape=[shape((exp_count, step, features))] * chunks
-        + [shape((2 * local_tokens // block, att))],
-        in_specs=[ANY, VMEM, VMEM, ANY, ANY],
-        out_specs=[VMEM] * (chunks + 1),
-        scratch_shapes=[
-            pltpu.VMEM((local_tokens, features), BF16),
-            pltpu.VMEM((local_tokens, att), BF16),
-            pltpu.VMEM((local_tokens, att), BF16),
-            pltpu.SemaphoreType.DMA((3,)),
-        ],
+    send = pl.pallas_call(
+        prep_kernel,
+        out_shape=[shape((exp_count, step, features))] * chunks,
+        in_specs=[ANY, VMEM, VMEM],
+        out_specs=[VMEM] * chunks,
+        scratch_shapes=[pltpu.VMEM((local_tokens, features), BF16), pltpu.SemaphoreType.DMA((1,))],
         compiler_params=params(56),
         cost_estimate=LITTLE,
         name="prep",
-    )(tokens, norm_gain.reshape(1, -1), expert_ids.T, attn_keys, attn_values)
+    )(tokens, norm_gain.reshape(1, -1), expert_ids.T)
 
     def device(segment, j):
         return (segment // SEG_DEV) * exp_count + (segment % SEG_DEV) * group + j
 
-    parts = [sums]
-    for other in range(1, segs):
-        pairs = []
-        for segment in range(segs):
-            for j in range(group):
-                pairs.append((device(segment, j), device(segment ^ other, j)))
-        parts.append(lax.ppermute(sums, ("seq", "exp"), pairs))
-    packed_rows = 3 * local_tokens + segs * 2 * local_tokens // block
     packed = pl.pallas_call(
         pack_kernel,
-        out_shape=shape((group, packed_rows, width)),
-        in_specs=[ANY] * 3 + [VMEM] * segs,
+        out_shape=shape((group, 3 * local_tokens, width)),
+        in_specs=[ANY] * 3,
         out_specs=VMEM,
         scratch_shapes=[pltpu.SemaphoreType.DMA((3 * group,))],
         compiler_params=params(56),
         cost_estimate=LITTLE,
         name="pack",
-    )(queries, attn_keys, attn_values, *parts)
+    )(queries, attn_keys, attn_values)
     recv = [lax.all_to_all(send[0], "exp", 0, 0, tiled=True)]
     for rows in send[1:]:
         recv.append(lax.all_to_all(after(rows, recv[-1]), "exp", 0, 0, tiled=True))
@@ -317,7 +297,7 @@
     position = jnp.stack([segment, place]).astype(jnp.int32)
     done, mine = [], []
     for chunk in range(chunks):
-        planes = [after(after(arrived[chunk][0], recv[-1]), parts)] + arrived[chunk][1:]
+        planes = [after(arrived[chunk][0], recv[-1])] + arrived[chunk][1:]
         total = seq_count * exp_count * step
         pieces = pl.pallas_call(
             functools.partial(ffn_kernel, chunk * experts, seq_count),
@@ -339,7 +319,7 @@
             name="experts",
         )(*planes, gate_proj, up_proj, down_proj)
         done.append(pieces)
-    packed = after(packed, recv[-1])
+    packed = after(after(packed, recv[-1]), arrived[0])
     halves = [[half * group + j for j in range(group)] for half in range(SEG_DEV)]
     got = lax.all_to_all(packed, "exp", 0, 0, axis_index_groups=halves, tiled=True)
     for chunk, pieces in enumerate(done):
@@ -349,16 +329,32 @@
             summed = summed + lax.ppermute(pieces[other], "seq", pairs).astype(F32)
         mine.append(summed.astype(BF16))
     got = after(got, mine[0])
+    sums = pl.pallas_call(
+        functools.partial(sums_kernel, seg_len // SUMS),
+        out_shape=shape((2 * SUMS, width)),
+        in_specs=[VMEM],
+        out_specs=VMEM,
+        compiler_params=params(32),
+        cost_estimate=LITTLE,
+        name="sums",
+    )(got)
+    parts = [sums]
+    for other in range(1, segs):
+        pairs = []
+        for frm in range(segs):
+            for j in range(group):
+                pairs.append((device(frm, j), device(frm ^ other, j)))
+        parts.append(lax.ppermute(sums, ("seq", "exp"), pairs))
     head_out = pl.pallas_call(
         functools.partial(attend_kernel, min(256, seg_len), local_tokens, segs),
         out_shape=[shape((local_tokens, width))] * group,
-        in_specs=[SMEM, VMEM],
+        in_specs=[SMEM, VMEM] + [VMEM] * segs,
         out_specs=[VMEM] * group,
         scratch_shapes=[pltpu.VMEM((group, local_tokens, width), BF16)],
         compiler_params=params(48),
         cost_estimate=LITTLE,
         name="attend",
-    )(position, got)
+    )(position, got, *parts)
     heads = [
         rows
         if other == 0
@@ -375,7 +371,6 @@
         name="place",
     )(position, *heads)
 
-    mine[-1] = after(mine[-1], heads[1:4])
     back = [lax.all_to_all(rows, "exp", 0, 0, tiled=True) for rows in mine]
     expert_mix = pl.pallas_call(
         mix_kernel,

time: 151 us -> 159 us (1.053)
  waiting for transfers between devices: 47.7 us -> 56.1 us
  starting transfers between devices: 31.6 us -> 33.7 us
    all_to_all x1, waiting for transfers between devices: 0.01 us -> 10.7 us  [on_device(): recv.append(lax.all_to_all(after(rows, recv[-1]), 'exp', 0, 0, tiled=True))]
    ppermute x7, waiting for transfers between devices: 12 us -> 3.1 us  [on_device(): lax.ppermute(rows, 'exp', [(i, i ^ other) for i in range(exp_count)])]
    ppermute x2, waiting for transfers between devices: 0.01 us -> 4.58 us  [on_device(): summed = summed + lax.ppermute(pieces[other], 'seq', pairs).astype(F32)]
    all_to_all x2, waiting for transfers between devices: 5.59 us -> 8.81 us  [on_device(): back = [lax.all_to_all(rows, 'exp', 0, 0, tiled=True) for rows in mine]]
    pallas_call x2 -> x3, Pallas kernels: 6.77 us -> 5.76 us  [the longest x1 3.37 us: on_device(): pl.pallas_call(prep_kernel, out_shape=[shape((exp_count, step, features))...]
  transfers between devices with their start and end apart: 18 -> 18, of which waited for: 8 -> 7; matrix products, arithmetic and copies ran while one was open for 2% -> 2% of each run, Pallas kernels for 26% -> 24%
where the time goes in v6:
time: 159 us; the launch traced here: 158 us
  waiting for transfers between devices  56.1 us (35%)
  Pallas kernels  42.3 us (27%)
  starting transfers between devices  33.7 us (21%)
  blocking collectives  21.8 us (14%)
  other arithmetic  3.56 us (2%)
    pallas_call x2, Pallas kernels, on_device(): pl.pallas_call(functools.partial(ffn_kernel, chunk * experts, seq_count),...  30.3 us
    all_to_all x1, blocking collectives, on_device(): recv = [lax.all_to_all(send[0], 'exp', 0, 0, tiled=True)]  21.8 us
    ppermute x3, waiting for transfers between devices, on_device(): parts.append(lax.ppermute(sums, ('seq', 'exp'), pairs))  16.1 us
    ppermute x2, waiting for transfers between devices, on_device(): planes.append(lax.ppermute(rows, 'seq', pairs))  12.8 us
    all_to_all x1, waiting for transfers between devices, on_device(): recv.append(lax.all_to_all(after(rows, recv[-1]), 'exp', 0, 0, tiled=True))  10.7 us
    all_to_all x2, starting transfers between devices, on_device(): back = [lax.all_to_all(rows, 'exp', 0, 0, tiled=True) for rows in mine]  9.84 us
    all_to_all x2, waiting for transfers between devices, on_device(): back = [lax.all_to_all(rows, 'exp', 0, 0, tiled=True) for rows in mine]  8.81 us
    ppermute x7, starting transfers between devices, on_device(): lax.ppermute(rows, 'exp', [(i, i ^ other) for i in range(exp_count)])  6.34 us
  transfers between devices with their start and end apart: 18, of which 7 were waited for; matrix products, arithmetic and copies ran while one was open for 2% of the time, Pallas kernels for 24%

profile of v6, /device:TPU:0, one launch (start us, length us, event | category | flops | bytes accessed | tf_op | source)
XLA Modules:
  0.0 158.3 jit_solution(4846603463628281993)
XLA Ops:
  0.6 3.4 %prep.1 = (bf16[16,4,4096]{2,1,0:T(4,128)(2,1)}, bf16[16,4,4096]{2,1,0:T(4,128)(2,1)}) custom-call(bf16[64,4096]{1,0:T(8,128)(2,1)} %tok_hbm.1, f32[1,4096]{1,0:T(1,128)} %bitcast.8, s32[2,64]{1,0:T(2,128)} %bitcast.5), custom_call_target="tpu_custom_call" | custom-call | flops 1000 | bytes 1000 | tf_op jit(solution)/shard_map/prep/pallas_call | solution.py:261
  4.0 21.8 %all_to_all.25.refs_0_ = bf16[16,4,4096]{2,1,0:T(4,128)(2,1)S(1)} all-to-all(bf16[16,4,4096]{2,1,0:T(4,128)(2,1)} %get-tuple-element.27), channel_id=1, replica_groups=mesh['seq'=2,'exp'=16] {'exp'}, dimensions={0} | all-to-all | bytes 1048576 | tf_op jit(solution)/shard_map/all_to_all | solution.py:285
  25.8 4.1 %all-to-all-start.1 = ((bf16[16,4,4096]{2,1,0:T(4,128)(2,1)}), bf16[16,4,4096]{2,1,0:T(4,128)(2,1)S(1)}, u32[]{:S(2)}, u32[]{:S(2)}) async-start(bf16[16,4,4096]{2,1,0:T(4,128)(2,1)} %get-tuple-element.28), calls=%async_computation.1 | async-start | bytes 1048576 | tf_op jit(solution)/shard_map/all_to_all | solution.py:287
  30.0 1.6 %collective-permute-start = (bf16[16,4,4096]{2,1,0:T(4,128)(2,1)S(1)}, bf16[16,4,4096]{2,1,0:T(4,128)(2,1)S(1)}, u32[]{:S(2)}, u32[]{:S(2)}) collective-permute-start(bf16[16,4,4096]{2,1,0:T(4,128)(2,1)S(1)} %all_to_all.25.refs_0_), channel_id=1, source_target_pairs={{0,16},{16,0},{1,17},{17,1},{2,18},{18,2},{3,19},{19,3},{4,20},{20... | collective-permute-start | bytes 1572872 | tf_op jit(solution)/shard_map/ppermute | solution.py:293
  31.5 2.2 %pack.1 = bf16[8,192,256]{2,1,0:T(8,128)(2,1)} custom-call(bf16[64,2048]{1,0:T(8,128)(2,1)} %q_hbm.1, bf16[64,2048]{1,0:T(8,128)(2,1)} %k_hbm.1, bf16[64,2048]{1,0:T(8,128)(2,1)} %v_hbm.1), custom_call_target="tpu_custom_call" | custom-call | flops 1000 | bytes 1000 | tf_op jit(solution)/shard_map/pack/pallas_call | solution.py:275
  33.7 10.7 %all-to-all-done.1.refs_0_ = bf16[16,4,4096]{2,1,0:T(4,128)(2,1)S(1)} async-done(((bf16[16,4,4096]{2,1,0:T(4,128)(2,1)}), bf16[16,4,4096]{2,1,0:T(4,128)(2,1)S(1)}, u32[]{:S(2)}, u32[]{:S(2)}) %all-to-all-start.1) | async-done | bytes 524320 | tf_op jit(solution)/shard_map/all_to_all | solution.py:287
  44.4 3.6 %all-to-all-start.2 = ((bf16[8,192,256]{2,1,0:T(8,128)(2,1)}), bf16[8,192,256]{2,1,0:T(8,128)(2,1)S(1)}, u32[]{:S(2)}, u32[]{:S(2)}) async-start(bf16[8,192,256]{2,1,0:T(8,128)(2,1)} %pack.1), calls=%async_computation.2 | async-start | bytes 1572864 | tf_op jit(solution)/shard_map/all_to_all | solution.py:324
  48.0 1.6 collective-permute-start.1
  49.6 12.8 %collective-permute-done.1.refs_1_ = bf16[16,4,4096]{2,1,0:T(4,128)(2,1)S(1)} collective-permute-done((bf16[16,4,4096]{2,1,0:T(4,128)(2,1)S(1)}, bf16[16,4,4096]{2,1,0:T(4,128)(2,1)S(1)}, u32[]{:S(2)}, u32[]{:S(2)}) %collective-permute-start.1) | collective-permute-done | bytes 524320 | tf_op jit(solution)/shard_map/ppermute | solution.py:293
  62.4 15.5 %experts.3 = (bf16[16,4,4096]{2,1,0:T(4,128)(2,1)S(1)}, bf16[16,4,4096]{2,1,0:T(4,128)(2,1)}) custom-call(bf16[16,4,4096]{2,1,0:T(4,128)(2,1)S(1)} %all-to-all-done.1.refs_0_, bf16[16,4,4096]{2,1,0:T(4,128)(2,1)S(1)} %collective-permute-done.1.refs_1_, bf16[4,704,4096]{2,1,0:T(8,128)(2,1)} %refs_2_.3, bf16[4,704,4096]{2,1,0:T(8,128)(2,1)} %refs_3_.3, ...), custom_call_target="tpu_custom_call" | custom-call | flops 2214592512 | bytes 103809024 | tf_op jit(solution)/shard_map/experts/pallas_call | solution.py:302
  77.9 1.6 %collective-permute-start.13 = (bf16[16,4,4096]{2,1,0:T(4,128)(2,1)}, bf16[16,4,4096]{2,1,0:T(4,128)(2,1)}, u32[]{:S(2)}, u32[]{:S(2)}) collective-permute-start(bf16[16,4,4096]{2,1,0:T(4,128)(2,1)} %get-tuple-element.49), channel_id=1, source_target_pairs={{0,16},{16,0},{1,17},{17,1},{2,18},{18,2},{3,19},{19,3},{4,20},{20... | collective-permute-start | bytes 1572872 | tf_op jit(solution)/shard_map/ppermute | solution.py:329
  79.5 14.8 %experts.2 = (bf16[16,4,4096]{2,1,0:T(4,128)(2,1)S(1)}, bf16[16,4,4096]{2,1,0:T(4,128)(2,1)S(1)}) custom-call(bf16[16,4,4096]{2,1,0:T(4,128)(2,1)S(1)} %all_to_all.25.refs_0_, bf16[16,4,4096]{2,1,0:T(4,128)(2,1)S(1)} %collective-permute-done.refs_1_, bf16[4,704,4096]{2,1,0:T(8,128)(2,1)} %refs_2_.3, bf16[4,704,4096]{2,1,0:T(8,128)(2,1)} %refs_3_.3, ...), custom_call_target="tpu_custom_call" | custom-call | flops 2214592512 | bytes 103809024 | tf_op jit(solution)/shard_map/experts/pallas_call | solution.py:302
  94.9 2.4 %add_convert_fusion = bf16[16,4,4096]{2,1,0:T(4,128)(2,1)} fusion(bf16[16,4,4096]{2,1,0:T(4,128)(2,1)} %collective-permute-done.13, bf16[16,4,4096]{2,1,0:T(4,128)(2,1)S(1)} %get-tuple-element.48), kind=kLoop, calls=%fused_computation | loop fusion | flops 1048576 | bytes 1572864 | tf_op jit(solution)/shard_map/convert_element_type | solution.py:330
  97.3 5.7 %all-to-all-start.4 = ((bf16[16,4,4096]{2,1,0:T(4,128)(2,1)}), bf16[16,4,4096]{2,1,0:T(4,128)(2,1)S(1)}, u32[]{:S(2)}, u32[]{:S(2)}) async-start(bf16[16,4,4096]{2,1,0:T(4,128)(2,1)} %add_convert_fusion), calls=%async_computation.4 | async-start | bytes 1048576 | tf_op jit(solution)/shard_map/all_to_all | solution.py:374
  103.0 4.6 %collective-permute-done.2 = bf16[16,4,4096]{2,1,0:T(4,128)(2,1)S(1)} collective-permute-done((bf16[16,4,4096]{2,1,0:T(4,128)(2,1)S(1)}, bf16[16,4,4096]{2,1,0:T(4,128)(2,1)S(1)}, u32[]{:S(2)}, u32[]{:S(2)}) %collective-permute-start.2) | collective-permute-done | bytes 524320 | tf_op jit(solution)/shard_map/ppermute | solution.py:329
  108.7 8.8 %all-to-all-done.4.refs_1_ = bf16[16,4,4096]{2,1,0:T(4,128)(2,1)S(1)} async-done(((bf16[16,4,4096]{2,1,0:T(4,128)(2,1)}), bf16[16,4,4096]{2,1,0:T(4,128)(2,1)S(1)}, u32[]{:S(2)}, u32[]{:S(2)}) %all-to-all-start.4) | async-done | bytes 524320 | tf_op jit(solution)/shard_map/all_to_all | solution.py:374
  117.5 4.1 %all-to-all-start.3 = ((bf16[16,4,4096]{2,1,0:T(4,128)(2,1)}), bf16[16,4,4096]{2,1,0:T(4,128)(2,1)S(1)}, u32[]{:S(2)}, u32[]{:S(2)}) async-start(bf16[16,4,4096]{2,1,0:T(4,128)(2,1)} %add_convert_fusion.1), calls=%async_computation.3 | async-start | bytes 1048576 | tf_op jit(solution)/shard_map/all_to_all | solution.py:374
  121.8 3.8 %collective-permute-start.5 = (bf16[128,256]{1,0:T(8,128)(2,1)S(1)}, bf16[128,256]{1,0:T(8,128)(2,1)S(1)}, u32[]{:S(2)}, u32[]{:S(2)}) collective-permute-start(bf16[128,256]{1,0:T(8,128)(2,1)S(1)} %sums.1.refs_0_), channel_id=1, source_target_pairs={{0,24},{1,25},{2,26},{3,27},{4,28},{5,29},{6,30},{7,31},{8,16},{9,... | collective-permute-start | bytes 196616 | tf_op jit(solution)/shard_map/ppermute | solution.py:347
  126.4 16.1 %collective-permute-done.5.refs_3_ = bf16[128,256]{1,0:T(8,128)(2,1)S(1)} collective-permute-done((bf16[128,256]{1,0:T(8,128)(2,1)S(1)}, bf16[128,256]{1,0:T(8,128)(2,1)S(1)}, u32[]{:S(2)}, u32[]{:S(2)}) %collective-permute-start.5) | collective-permute-done | bytes 65568 | tf_op jit(solution)/shard_map/ppermute | solution.py:347
  142.5 3.4 %attend.1 = (bf16[64,256]{1,0:T(8,128)(2,1)S(1)}, bf16[64,256]{1,0:T(8,128)(2,1)S(1)}, bf16[64,256]{1,0:T(8,128)(2,1)S(1)}, bf16[64,256]{1,0:T(8,128)(2,1)S(1)},...) custom-call(s32[2]{0:T(128)S(1)} %pad_add_fusion.at_ref, ...), custom_call_target="tpu_custom_call" | custom-call | flops 1000 | bytes 1000 | tf_op jit(solution)/shard_map/attend/pallas_call | solution.py:348
  146.0 1.5 collective-permute-start.7
  147.9 1.7 %collective-permute-start.10 = (bf16[64,256]{1,0:T(8,128)(2,1)S(1)}, bf16[64,256]{1,0:T(8,128)(2,1)S(1)}, u32[]{:S(2)}, u32[]{:S(2)}) collective-permute-start(bf16[64,256]{1,0:T(8,128)(2,1)S(1)} %get-tuple-element.44), channel_id=1, source_target_pairs={{0,5},{1,4},{2,7},{3,6},{4,1},{5,0},{6,3},{7,2},{8,13},{9,12},{10,... | collective-permute-start | bytes 98312 | tf_op jit(solution)/shard_map/ppermute | solution.py:361
  152.3 2.1 %collective-permute-done.11.refs_6_ = bf16[64,256]{1,0:T(8,128)(2,1)S(1)} collective-permute-done((bf16[64,256]{1,0:T(8,128)(2,1)S(1)}, bf16[64,256]{1,0:T(8,128)(2,1)S(1)}, u32[]{:S(2)}, u32[]{:S(2)}) %collective-permute-start.11) | collective-permute-done | bytes 32800 | tf_op jit(solution)/shard_map/ppermute | solution.py:361
  156.7 1.6 %mix.1 = bf16[64,4096]{1,0:T(8,128)(2,1)} custom-call(s32[2,64]{1,0:T(2,128)S(1)} %bitcast.6, f32[2,64]{1,0:T(2,128)S(1)} %bitcast.7, bf16[16,4,4096]{2,1,0:T(4,128)(2,1)S(1)} %all-to-all-done.3.refs_0_, bf16[16,4,4096]{2,1,0:T(4,128)(2,1)S(1)} %all-to-all-done.4.refs_1_), custom_call_target="tpu_custom_call" | custom-call | flops 1000 | bytes 1000 | tf_op jit(solution)/shard_map/mix/pallas_call | solution.py:375
  (28 shorter events, 8.0 us)
Async XLA Ops:
  25.8 18.6 %all-to-all-start.1 = ((bf16[16,4,4096]{2,1,0:T(4,128)(2,1)}), bf16[16,4,4096]{2,1,0:T(4,128)(2,1)S(1)}, u32[]{:S(2)}, u32[]{:S(2)}) async-start(bf16[16,4,4096]{2,1,0:T(4,128)(2,1)} %get-tuple-element.28), calls=%async_computation.1 | async-start | bytes 1048576 | tf_op jit(solution)/shard_map/all_to_all | solution.py:287
  30.0 14.5 %collective-permute-start = (bf16[16,4,4096]{2,1,0:T(4,128)(2,1)S(1)}, bf16[16,4,4096]{2,1,0:T(4,128)(2,1)S(1)}, u32[]{:S(2)}, u32[]{:S(2)}) collective-permute-start(bf16[16,4,4096]{2,1,0:T(4,128)(2,1)S(1)} %all_to_all.25.refs_0_), channel_id=1, source_target_pairs={{0,16},{16,0},{1,17},{17,1},{2,18},{18,2},{3,19},{19,3},{4,20},{20... | collective-permute-start | bytes 1572872 | tf_op jit(solution)/shard_map/ppermute | solution.py:293
  44.4 50.5 %all-to-all-start.2 = ((bf16[8,192,256]{2,1,0:T(8,128)(2,1)}), bf16[8,192,256]{2,1,0:T(8,128)(2,1)S(1)}, u32[]{:S(2)}, u32[]{:S(2)}) async-start(bf16[8,192,256]{2,1,0:T(8,128)(2,1)} %pack.1), calls=%async_computation.2 | async-start | bytes 1572864 | tf_op jit(solution)/shard_map/all_to_all | solution.py:324
  48.0 14.3 %collective-permute-start.1 = (bf16[16,4,4096]{2,1,0:T(4,128)(2,1)S(1)}, bf16[16,4,4096]{2,1,0:T(4,128)(2,1)S(1)}, u32[]{:S(2)}, u32[]{:S(2)}) collective-permute-start(bf16[16,4,4096]{2,1,0:T(4,128)(2,1)S(1)} %all-to-all-done.1.refs_0_), channel_id=1, source_target_pairs={{0,16},{16,0},{1,17},{17,1},{2,18},{18,2},{3,19},{19,3},{4,20},{20... | collective-permute-start | bytes 1572872 | tf_op jit(solution)/shard_map/ppermute | solution.py:293
  77.8 78.8 %copy-start = (s32[64,2]{0,1:T(2,128)S(1)}, s32[64,2]{0,1:T(2,128)}, u32[]{:S(2)}) copy-start(s32[64,2]{0,1:T(2,128)} %param.15) | copy-start | bytes 1540
  77.9 78.8 %copy-start.1 = (f32[64,2]{0,1:T(2,128)S(1)}, f32[64,2]{0,1:T(2,128)}, u32[]{:S(2)}) copy-start(f32[64,2]{0,1:T(2,128)} %param.16) | copy-start | bytes 1540
  77.9 17.0 %collective-permute-start.13 = (bf16[16,4,4096]{2,1,0:T(4,128)(2,1)}, bf16[16,4,4096]{2,1,0:T(4,128)(2,1)}, u32[]{:S(2)}, u32[]{:S(2)}) collective-permute-start(bf16[16,4,4096]{2,1,0:T(4,128)(2,1)} %get-tuple-element.49), channel_id=1, source_target_pairs={{0,16},{16,0},{1,17},{17,1},{2,18},{18,2},{3,19},{19,3},{4,20},{20... | collective-permute-start | bytes 1572872 | tf_op jit(solution)/shard_map/ppermute | solution.py:329
  94.3 13.3 %collective-permute-start.2 = (bf16[16,4,4096]{2,1,0:T(4,128)(2,1)S(1)}, bf16[16,4,4096]{2,1,0:T(4,128)(2,1)S(1)}, u32[]{:S(2)}, u32[]{:S(2)}) collective-permute-start(bf16[16,4,4096]{2,1,0:T(4,128)(2,1)S(1)} %get-tuple-element.37), channel_id=1, source_target_pairs={{0,16},{16,0},{1,17},{17,1},{2,18},{18,2},{3,19},{19,3},{4,20},{20... | collective-permute-start | bytes 1572872 | tf_op jit(solution)/shard_map/ppermute | solution.py:329
  97.3 20.2 %all-to-all-start.4 = ((bf16[16,4,4096]{2,1,0:T(4,128)(2,1)}), bf16[16,4,4096]{2,1,0:T(4,128)(2,1)S(1)}, u32[]{:S(2)}, u32[]{:S(2)}) async-start(bf16[16,4,4096]{2,1,0:T(4,128)(2,1)} %add_convert_fusion), calls=%async_computation.4 | async-start | bytes 1048576 | tf_op jit(solution)/shard_map/all_to_all | solution.py:374
  117.5 39.1 %all-to-all-start.3 = ((bf16[16,4,4096]{2,1,0:T(4,128)(2,1)}), bf16[16,4,4096]{2,1,0:T(4,128)(2,1)S(1)}, u32[]{:S(2)}, u32[]{:S(2)}) async-start(bf16[16,4,4096]{2,1,0:T(4,128)(2,1)} %add_convert_fusion.1), calls=%async_computation.3 | async-start | bytes 1048576 | tf_op jit(solution)/shard_map/all_to_all | solution.py:374
  121.8 20.7 %collective-permute-start.5 = (bf16[128,256]{1,0:T(8,128)(2,1)S(1)}, bf16[128,256]{1,0:T(8,128)(2,1)S(1)}, u32[]{:S(2)}, u32[]{:S(2)}) collective-permute-start(bf16[128,256]{1,0:T(8,128)(2,1)S(1)} %sums.1.refs_0_), channel_id=1, source_target_pairs={{0,24},{1,25},{2,26},{3,27},{4,28},{5,29},{6,30},{7,31},{8,16},{9,... | collective-permute-start | bytes 196616 | tf_op jit(solution)/shard_map/ppermute | solution.py:347
  125.7 16.9 %collective-permute-start.4 = (bf16[128,256]{1,0:T(8,128)(2,1)S(1)}, bf16[128,256]{1,0:T(8,128)(2,1)S(1)}, u32[]{:S(2)}, u32[]{:S(2)}) collective-permute-start(bf16[128,256]{1,0:T(8,128)(2,1)S(1)} %sums.1.refs_0_), channel_id=1, source_target_pairs={{0,16},{1,17},{2,18},{3,19},{4,20},{5,21},{6,22},{7,23},{8,24},{9,... | collective-permute-start | bytes 196616 | tf_op jit(solution)/shard_map/ppermute | solution.py:347
  126.2 16.4 %collective-permute-start.3 = (bf16[128,256]{1,0:T(8,128)(2,1)S(1)}, bf16[128,256]{1,0:T(8,128)(2,1)S(1)}, u32[]{:S(2)}, u32[]{:S(2)}) collective-permute-start(bf16[128,256]{1,0:T(8,128)(2,1)S(1)} %sums.1.refs_0_), channel_id=1, source_target_pairs={{0,8},{1,9},{2,10},{3,11},{4,12},{5,13},{6,14},{7,15},{8,0},{9,1},... | collective-permute-start | bytes 196616 | tf_op jit(solution)/shard_map/ppermute | solution.py:347
  145.9 3.6 %collective-permute-start.6 = (bf16[64,256]{1,0:T(8,128)(2,1)S(1)}, bf16[64,256]{1,0:T(8,128)(2,1)S(1)}, u32[]{:S(2)}, u32[]{:S(2)}) collective-permute-start(bf16[64,256]{1,0:T(8,128)(2,1)S(1)} %get-tuple-element.40), channel_id=1, source_target_pairs={{0,1},{1,0},{2,3},{3,2},{4,5},{5,4},{6,7},{7,6},{8,9},{9,8},{10,11... | collective-permute-start | bytes 98312 | tf_op jit(solution)/shard_map/ppermute | solution.py:361
  146.0 4.8 %collective-permute-start.7 = (bf16[64,256]{1,0:T(8,128)(2,1)S(1)}, bf16[64,256]{1,0:T(8,128)(2,1)S(1)}, u32[]{:S(2)}, u32[]{:S(2)}) collective-permute-start(bf16[64,256]{1,0:T(8,128)(2,1)S(1)} %get-tuple-element.41), channel_id=1, source_target_pairs={{0,2},{1,3},{2,0},{3,1},{4,6},{5,7},{6,4},{7,5},{8,10},{9,11},{10,... | collective-permute-start | bytes 98312 | tf_op jit(solution)/shard_map/ppermute | solution.py:361
  147.5 4.8 %collective-permute-start.8 = (bf16[64,256]{1,0:T(8,128)(2,1)S(1)}, bf16[64,256]{1,0:T(8,128)(2,1)S(1)}, u32[]{:S(2)}, u32[]{:S(2)}) collective-permute-start(bf16[64,256]{1,0:T(8,128)(2,1)S(1)} %get-tuple-element.42), channel_id=1, source_target_pairs={{0,3},{1,2},{2,1},{3,0},{4,7},{5,6},{6,5},{7,4},{8,11},{9,10},{10,... | collective-permute-start | bytes 98312 | tf_op jit(solution)/shard_map/ppermute | solution.py:361
  147.9 4.4 %collective-permute-start.9 = (bf16[64,256]{1,0:T(8,128)(2,1)S(1)}, bf16[64,256]{1,0:T(8,128)(2,1)S(1)}, u32[]{:S(2)}, u32[]{:S(2)}) collective-permute-start(bf16[64,256]{1,0:T(8,128)(2,1)S(1)} %get-tuple-element.43), channel_id=1, source_target_pairs={{0,4},{1,5},{2,6},{3,7},{4,0},{5,1},{6,2},{7,3},{8,12},{9,13},{10,... | collective-permute-start | bytes 98312 | tf_op jit(solution)/shard_map/ppermute | solution.py:361
  147.9 4.4 %collective-permute-start.10 = (bf16[64,256]{1,0:T(8,128)(2,1)S(1)}, bf16[64,256]{1,0:T(8,128)(2,1)S(1)}, u32[]{:S(2)}, u32[]{:S(2)}) collective-permute-start(bf16[64,256]{1,0:T(8,128)(2,1)S(1)} %get-tuple-element.44), channel_id=1, source_target_pairs={{0,5},{1,4},{2,7},{3,6},{4,1},{5,0},{6,3},{7,2},{8,13},{9,12},{10,... | collective-permute-start | bytes 98312 | tf_op jit(solution)/shard_map/ppermute | solution.py:361
  149.6 4.8 %collective-permute-start.11 = (bf16[64,256]{1,0:T(8,128)(2,1)S(1)}, bf16[64,256]{1,0:T(8,128)(2,1)S(1)}, u32[]{:S(2)}, u32[]{:S(2)}) collective-permute-start(bf16[64,256]{1,0:T(8,128)(2,1)S(1)} %get-tuple-element.45), channel_id=1, source_target_pairs={{0,6},{1,7},{2,4},{3,5},{4,2},{5,3},{6,0},{7,1},{8,14},{9,15},{10,... | collective-permute-start | bytes 98312 | tf_op jit(solution)/shard_map/ppermute | solution.py:361
  150.8 4.6 %collective-permute-start.12 = (bf16[64,256]{1,0:T(8,128)(2,1)S(1)}, bf16[64,256]{1,0:T(8,128)(2,1)S(1)}, u32[]{:S(2)}, u32[]{:S(2)}) collective-permute-start(bf16[64,256]{1,0:T(8,128)(2,1)S(1)} %get-tuple-element.46), channel_id=1, source_target_pairs={{0,7},{1,6},{2,5},{3,4},{4,3},{5,2},{6,1},{7,0},{8,15},{9,14},{10,... | collective-permute-start | bytes 98312 | tf_op jit(solution)/shard_map/ppermute | solution.py:361

commit v7 on v5

--- a/solution.py
+++ b/solution.py
@@ -302,7 +302,7 @@
         cost_estimate=LITTLE,
         name="pack",
     )(queries, attn_keys, attn_values, *parts)
-    recv = [lax.all_to_all(send[0], "exp", 0, 0, tiled=True)]
+    recv = [lax.all_to_all(after(send[0], parts), "exp", 0, 0, tiled=True)]
     for rows in send[1:]:
         recv.append(lax.all_to_all(after(rows, recv[-1]), "exp", 0, 0, tiled=True))
     arrived = []
@@ -317,7 +317,7 @@
     position = jnp.stack([segment, place]).astype(jnp.int32)
     done, mine = [], []
     for chunk in range(chunks):
-        planes = [after(after(arrived[chunk][0], recv[-1]), parts)] + arrived[chunk][1:]
+        planes = [after(arrived[chunk][0], recv[-1] if chunk == 0 else pieces[0])] + arrived[chunk][1:]
         total = seq_count * exp_count * step
         pieces = pl.pallas_call(
             functools.partial(ffn_kernel, chunk * experts, seq_count),
@@ -339,7 +339,7 @@
             name="experts",
         )(*planes, gate_proj, up_proj, down_proj)
         done.append(pieces)
-    packed = after(packed, recv[-1])
+    packed = after(after(packed, recv[-1]), arrived[0])
     halves = [[half * group + j for j in range(group)] for half in range(SEG_DEV)]
     got = lax.all_to_all(packed, "exp", 0, 0, axis_index_groups=halves, tiled=True)
     for chunk, pieces in enumerate(done):

time: 151 us -> 138 us (0.914)
  waiting for transfers between devices: 47.7 us -> 33.5 us
  starting transfers between devices: 31.6 us -> 33.5 us
  blocking collectives: 21.8 us -> 20 us
    ppermute x2, waiting for transfers between devices: 12.7 us -> 0.01 us  [on_device(): planes.append(lax.ppermute(rows, 'seq', pairs))]
    ppermute x3, waiting for transfers between devices: 17.4 us -> 6.27 us  [on_device(): parts.append(lax.ppermute(sums, ('seq', 'exp'), pairs))]
    all_to_all x1, waiting for transfers between devices: 0.01 us -> 10.7 us  [on_device(): recv.append(lax.all_to_all(after(rows, recv[-1]), 'exp', 0, 0, tiled=True))]
    all_to_all x1, blocking collectives: 21.8 us -> 20 us  [on_device(): recv = [lax.all_to_all(after(send[0], parts), 'exp', 0, 0, tiled=True)]]
    all_to_all x2, starting transfers between devices: 8.43 us -> 10.2 us  [on_device(): back = [lax.all_to_all(rows, 'exp', 0, 0, tiled=True) for rows in mine]]
  transfers between devices with their start and end apart: 18 -> 18, of which waited for: 8 -> 9; matrix products, arithmetic and copies ran while one was open for 2% -> 3% of each run, Pallas kernels for 26% -> 28%
where the time goes in v7:
time: 138 us; the launch traced here: 137 us
  Pallas kernels  43.7 us (32%)
  starting transfers between devices  33.5 us (24%)
  waiting for transfers between devices  33.5 us (24%)
  blocking collectives  20 us (14%)
  other arithmetic  4.34 us (3%)
    pallas_call x2, Pallas kernels, on_device(): pl.pallas_call(functools.partial(ffn_kernel, chunk * experts, seq_count),...  30.8 us
    all_to_all x1, blocking collectives, on_device(): recv = [lax.all_to_all(after(send[0], parts), 'exp', 0, 0, tiled=True)]  20 us
    ppermute x7, waiting for transfers between devices, on_device(): lax.ppermute(rows, 'exp', [(i, i ^ other) for i in range(exp_count)])  11 us
    all_to_all x1, waiting for transfers between devices, on_device(): recv.append(lax.all_to_all(after(rows, recv[-1]), 'exp', 0, 0, tiled=True))  10.7 us
    all_to_all x2, starting transfers between devices, on_device(): back = [lax.all_to_all(rows, 'exp', 0, 0, tiled=True) for rows in mine]  10.2 us
    ppermute x7, starting transfers between devices, on_device(): lax.ppermute(rows, 'exp', [(i, i ^ other) for i in range(exp_count)])  6.76 us
    ppermute x3, waiting for transfers between devices, on_device(): parts.append(lax.ppermute(sums, ('seq', 'exp'), pairs))  6.27 us
    ppermute x3, starting transfers between devices, on_device(): parts.append(lax.ppermute(sums, ('seq', 'exp'), pairs))  5.63 us
  transfers between devices with their start and end apart: 18, of which 9 were waited for; matrix products, arithmetic and copies ran while one was open for 3% of the time, Pallas kernels for 28%

profile of v7, /device:TPU:0, one launch (start us, length us, event | category | flops | bytes accessed | tf_op | source)
XLA Modules:
  0.0 136.5 jit_solution(5360425960855385812)
XLA Ops:
  0.6 3.5 %prep.1 = (bf16[16,4,4096]{2,1,0:T(4,128)(2,1)}, bf16[16,4,4096]{2,1,0:T(4,128)(2,1)}, bf16[16,2048]{1,0:T(8,128)(2,1)}) custom-call(bf16[64,4096]{1,0:T(8,128)(2,1)} %tok_hbm.1, f32[1,4096]{1,0:T(1,128)} %bitcast.8, s32[2,64]{1,0:T(2,128)} %bitcast.5, bf16[64,2048]{1,0:T(8,128)(2,1)} %k_hbm.3, bf16[64,2048]{1,0:T(8,128)(2,1)} %v_hbm.3), custom_call_target="tpu_custom_call" | custom-call | flops 1000 | bytes 1000 | tf_op jit(solution)/shard_map/prep/pallas_call | solution.py:267
  4.2 4.1 %collective-permute-start = (bf16[16,2048]{1,0:T(8,128)(2,1)}, bf16[16,2048]{1,0:T(8,128)(2,1)S(1)}, u32[]{:S(2)}, u32[]{:S(2)}) collective-permute-start(bf16[16,2048]{1,0:T(8,128)(2,1)} %get-tuple-element.29.refs_0_), channel_id=1, source_target_pairs={{0,8},{1,9},{2,10},{3,11},{4,12},{5,13},{6,14},{7,15},{8,0},{9,1},... | collective-permute-start | bytes 196616 | tf_op jit(solution)/shard_map/ppermute | solution.py:293
  8.3 1.5 %collective-permute-start.1 = (bf16[16,2048]{1,0:T(8,128)(2,1)}, bf16[16,2048]{1,0:T(8,128)(2,1)S(1)}, u32[]{:S(2)}, u32[]{:S(2)}) collective-permute-start(bf16[16,2048]{1,0:T(8,128)(2,1)} %get-tuple-element.29.refs_0_), channel_id=1, source_target_pairs={{0,16},{1,17},{2,18},{3,19},{4,20},{5,21},{6,22},{7,23},{8,24},{9,... | collective-permute-start | bytes 196616 | tf_op jit(solution)/shard_map/ppermute | solution.py:293
  9.8 2.3 %collective-permute-done.refs_1_ = bf16[16,2048]{1,0:T(8,128)(2,1)S(1)} collective-permute-done((bf16[16,2048]{1,0:T(8,128)(2,1)}, bf16[16,2048]{1,0:T(8,128)(2,1)S(1)}, u32[]{:S(2)}, u32[]{:S(2)}) %collective-permute-start) | collective-permute-done | bytes 65568 | tf_op jit(solution)/shard_map/ppermute | solution.py:293
  12.8 3.3 %collective-permute-done.2.refs_3_ = bf16[16,2048]{1,0:T(8,128)(2,1)S(1)} collective-permute-done((bf16[16,2048]{1,0:T(8,128)(2,1)}, bf16[16,2048]{1,0:T(8,128)(2,1)S(1)}, u32[]{:S(2)}, u32[]{:S(2)}) %collective-permute-start.2) | collective-permute-done | bytes 65568 | tf_op jit(solution)/shard_map/ppermute | solution.py:293
  16.1 20.0 %all_to_all.25.refs_0_ = bf16[16,4,4096]{2,1,0:T(4,128)(2,1)S(1)} all-to-all(bf16[16,4,4096]{2,1,0:T(4,128)(2,1)} %get-tuple-element.32), channel_id=1, replica_groups=mesh['seq'=2,'exp'=16] {'exp'}, dimensions={0} | all-to-all | bytes 1048576 | tf_op jit(solution)/shard_map/all_to_all | solution.py:305
  36.1 4.1 %all-to-all-start.1 = ((bf16[16,4,4096]{2,1,0:T(4,128)(2,1)}), bf16[16,4,4096]{2,1,0:T(4,128)(2,1)S(1)}, u32[]{:S(2)}, u32[]{:S(2)}) async-start(bf16[16,4,4096]{2,1,0:T(4,128)(2,1)} %get-tuple-element.33), calls=%async_computation.1 | async-start | bytes 1048576 | tf_op jit(solution)/shard_map/all_to_all | solution.py:307
  40.8 3.2 %pack.1 = bf16[8,256,256]{2,1,0:T(8,128)(2,1)} custom-call(bf16[64,2048]{1,0:T(8,128)(2,1)} %q_hbm.1, bf16[64,2048]{1,0:T(8,128)(2,1)} %k_hbm.3, bf16[64,2048]{1,0:T(8,128)(2,1)} %v_hbm.3, bf16[16,2048]{1,0:T(8,128)(2,1)} %get-tuple-element.29.refs_0_, bf16[16,2048]{1,0:T(8,128)(2,1)} %copy-done.4, bf16[16,2048]{1,0:T(8,128)(2,1)} %copy-done.5, ...), custom_call_target="tpu_custom_call" | custom-call | flops 1000 | bytes 1000 | tf_op jit(solution)/shard_map/pack/pallas_call | solution.py:295
  44.0 10.7 %all-to-all-done.1.refs_0_ = bf16[16,4,4096]{2,1,0:T(4,128)(2,1)S(1)} async-done(((bf16[16,4,4096]{2,1,0:T(4,128)(2,1)}), bf16[16,4,4096]{2,1,0:T(4,128)(2,1)S(1)}, u32[]{:S(2)}, u32[]{:S(2)}) %all-to-all-start.1) | async-done | bytes 524320 | tf_op jit(solution)/shard_map/all_to_all | solution.py:307
  54.6 3.6 %all-to-all-start.2 = ((bf16[8,256,256]{2,1,0:T(8,128)(2,1)}), bf16[8,256,256]{2,1,0:T(8,128)(2,1)S(1)}, u32[]{:S(2)}, u32[]{:S(2)}) async-start(bf16[8,256,256]{2,1,0:T(8,128)(2,1)} %pack.1), calls=%async_computation.2 | async-start | bytes 2097152 | tf_op jit(solution)/shard_map/all_to_all | solution.py:344
  58.8 15.4 %experts.2 = (bf16[16,4,4096]{2,1,0:T(4,128)(2,1)S(1)}, bf16[16,4,4096]{2,1,0:T(4,128)(2,1)}) custom-call(bf16[16,4,4096]{2,1,0:T(4,128)(2,1)S(1)} %all_to_all.25.refs_0_, bf16[16,4,4096]{2,1,0:T(4,128)(2,1)S(1)} %collective-permute-done.3.refs_1_, bf16[4,704,4096]{2,1,0:T(8,128)(2,1)} %refs_2_.3, bf16[4,704,4096]{2,1,0:T(8,128)(2,1)} %refs_3_.3, ...), custom_call_target="tpu_custom_call" | custom-call | flops 2214592512 | bytes 103809024 | tf_op jit(solution)/shard_map/experts/pallas_call | solution.py:322
  76.6 15.4 %experts.3 = (bf16[16,4,4096]{2,1,0:T(4,128)(2,1)S(1)}, bf16[16,4,4096]{2,1,0:T(4,128)(2,1)}) custom-call(bf16[16,4,4096]{2,1,0:T(4,128)(2,1)S(1)} %all-to-all-done.1.refs_0_, bf16[16,4,4096]{2,1,0:T(4,128)(2,1)S(1)} %collective-permute-done.4.refs_1_, bf16[4,704,4096]{2,1,0:T(8,128)(2,1)} %refs_2_.3, bf16[4,704,4096]{2,1,0:T(8,128)(2,1)} %refs_3_.3, ...), custom_call_target="tpu_custom_call" | custom-call | flops 2214592512 | bytes 103809024 | tf_op jit(solution)/shard_map/experts/pallas_call | solution.py:322
  92.6 2.1 %add_convert_fusion.1 = bf16[16,4,4096]{2,1,0:T(4,128)(2,1)} fusion(bf16[16,4,4096]{2,1,0:T(4,128)(2,1)} %collective-permute-done.5, bf16[16,4,4096]{2,1,0:T(4,128)(2,1)S(1)} %copy-done.1), kind=kLoop, calls=%fused_computation.1 | loop fusion | flops 1048576 | bytes 1572864 | tf_op jit(solution)/shard_map/convert_element_type | solution.py:350
  94.7 6.1 %all-to-all-start.3 = ((bf16[16,4,4096]{2,1,0:T(4,128)(2,1)}), bf16[16,4,4096]{2,1,0:T(4,128)(2,1)S(1)}, u32[]{:S(2)}, u32[]{:S(2)}) async-start(bf16[16,4,4096]{2,1,0:T(4,128)(2,1)} %add_convert_fusion.1), calls=%async_computation.3 | async-start | bytes 1048576 | tf_op jit(solution)/shard_map/all_to_all | solution.py:379
  100.9 3.2 %attend.1 = (bf16[64,256]{1,0:T(8,128)(2,1)S(1)}, bf16[64,256]{1,0:T(8,128)(2,1)S(1)}, bf16[64,256]{1,0:T(8,128)(2,1)S(1)}, bf16[64,256]{1,0:T(8,128)(2,1)S(1)},...) custom-call(s32[2]{0:T(128)S(1)} %pad_add_fusion.at_ref, ...), custom_call_target="tpu_custom_call" | custom-call | flops 1000 | bytes 1000 | tf_op jit(solution)/shard_map/attend/pallas_call | solution.py:352
  104.5 1.7 %collective-permute-start.7 = (bf16[64,256]{1,0:T(8,128)(2,1)S(1)}, bf16[64,256]{1,0:T(8,128)(2,1)S(1)}, u32[]{:S(2)}, u32[]{:S(2)}) collective-permute-start(bf16[64,256]{1,0:T(8,128)(2,1)S(1)} %get-tuple-element.46), channel_id=1, source_target_pairs={{0,2},{1,3},{2,0},{3,1},{4,6},{5,7},{6,4},{7,5},{8,10},{9,11},{10,... | collective-permute-start | bytes 98312 | tf_op jit(solution)/shard_map/ppermute | solution.py:365
  106.2 2.1 %add_convert_fusion = bf16[16,4,4096]{2,1,0:T(4,128)(2,1)} fusion(bf16[16,4,4096]{2,1,0:T(4,128)(2,1)} %collective-permute-done.13, bf16[16,4,4096]{2,1,0:T(4,128)(2,1)S(1)} %get-tuple-element.53), kind=kLoop, calls=%fused_computation | loop fusion | flops 1048576 | bytes 1572864 | tf_op jit(solution)/shard_map/convert_element_type | solution.py:350
  109.7 5.6 %all-to-all-done.3.refs_0_ = bf16[16,4,4096]{2,1,0:T(4,128)(2,1)S(1)} async-done(((bf16[16,4,4096]{2,1,0:T(4,128)(2,1)}), bf16[16,4,4096]{2,1,0:T(4,128)(2,1)S(1)}, u32[]{:S(2)}, u32[]{:S(2)}) %all-to-all-start.3) | async-done | bytes 524320 | tf_op jit(solution)/shard_map/all_to_all | solution.py:379
  115.2 4.1 %all-to-all-start.4 = ((bf16[16,4,4096]{2,1,0:T(4,128)(2,1)}), bf16[16,4,4096]{2,1,0:T(4,128)(2,1)S(1)}, u32[]{:S(2)}, u32[]{:S(2)}) async-start(bf16[16,4,4096]{2,1,0:T(4,128)(2,1)} %add_convert_fusion), calls=%async_computation.4 | async-start | bytes 1048576 | tf_op jit(solution)/shard_map/all_to_all | solution.py:379
  119.4 1.9 %collective-permute-start.9 = (bf16[64,256]{1,0:T(8,128)(2,1)S(1)}, bf16[64,256]{1,0:T(8,128)(2,1)S(1)}, u32[]{:S(2)}, u32[]{:S(2)}) collective-permute-start(bf16[64,256]{1,0:T(8,128)(2,1)S(1)} %get-tuple-element.48), channel_id=1, source_target_pairs={{0,4},{1,5},{2,6},{3,7},{4,0},{5,1},{6,2},{7,3},{8,12},{9,13},{10,... | collective-permute-start | bytes 98312 | tf_op jit(solution)/shard_map/ppermute | solution.py:365
  121.3 2.4 %collective-permute-start.11 = (bf16[64,256]{1,0:T(8,128)(2,1)S(1)}, bf16[64,256]{1,0:T(8,128)(2,1)S(1)}, u32[]{:S(2)}, u32[]{:S(2)}) collective-permute-start(bf16[64,256]{1,0:T(8,128)(2,1)S(1)} %get-tuple-element.50), channel_id=1, source_target_pairs={{0,6},{1,7},{2,4},{3,5},{4,2},{5,3},{6,0},{7,1},{8,14},{9,15},{10,... | collective-permute-start | bytes 98312 | tf_op jit(solution)/shard_map/ppermute | solution.py:365
  124.0 6.8 %collective-permute-done.9.refs_4_ = bf16[64,256]{1,0:T(8,128)(2,1)S(1)} collective-permute-done((bf16[64,256]{1,0:T(8,128)(2,1)S(1)}, bf16[64,256]{1,0:T(8,128)(2,1)S(1)}, u32[]{:S(2)}, u32[]{:S(2)}) %collective-permute-start.9) | collective-permute-done | bytes 32800 | tf_op jit(solution)/shard_map/ppermute | solution.py:365
  130.7 2.9 %collective-permute-done.11.refs_6_ = bf16[64,256]{1,0:T(8,128)(2,1)S(1)} collective-permute-done((bf16[64,256]{1,0:T(8,128)(2,1)S(1)}, bf16[64,256]{1,0:T(8,128)(2,1)S(1)}, u32[]{:S(2)}, u32[]{:S(2)}) %collective-permute-start.11) | collective-permute-done | bytes 32800 | tf_op jit(solution)/shard_map/ppermute | solution.py:365
  134.9 1.6 %mix.1 = bf16[64,4096]{1,0:T(8,128)(2,1)} custom-call(s32[2,64]{1,0:T(2,128)S(1)} %bitcast.6, f32[2,64]{1,0:T(2,128)S(1)} %bitcast.7, bf16[16,4,4096]{2,1,0:T(4,128)(2,1)S(1)} %all-to-all-done.3.refs_0_, bf16[16,4,4096]{2,1,0:T(4,128)(2,1)S(1)} %all-to-all-done.4.refs_1_), custom_call_target="tpu_custom_call" | custom-call | flops 1000 | bytes 1000 | tf_op jit(solution)/shard_map/mix/pallas_call | solution.py:380
  (37 shorter events, 8.1 us)
Async XLA Ops:
  4.2 8.0 %collective-permute-start = (bf16[16,2048]{1,0:T(8,128)(2,1)}, bf16[16,2048]{1,0:T(8,128)(2,1)S(1)}, u32[]{:S(2)}, u32[]{:S(2)}) collective-permute-start(bf16[16,2048]{1,0:T(8,128)(2,1)} %get-tuple-element.29.refs_0_), channel_id=1, source_target_pairs={{0,8},{1,9},{2,10},{3,11},{4,12},{5,13},{6,14},{7,15},{8,0},{9,1},... | collective-permute-start | bytes 196616 | tf_op jit(solution)/shard_map/ppermute | solution.py:293
  8.3 4.5 %collective-permute-start.1 = (bf16[16,2048]{1,0:T(8,128)(2,1)}, bf16[16,2048]{1,0:T(8,128)(2,1)S(1)}, u32[]{:S(2)}, u32[]{:S(2)}) collective-permute-start(bf16[16,2048]{1,0:T(8,128)(2,1)} %get-tuple-element.29.refs_0_), channel_id=1, source_target_pairs={{0,16},{1,17},{2,18},{3,19},{4,20},{5,21},{6,22},{7,23},{8,24},{9,... | collective-permute-start | bytes 196616 | tf_op jit(solution)/shard_map/ppermute | solution.py:293
  9.8 6.3 %collective-permute-start.2 = (bf16[16,2048]{1,0:T(8,128)(2,1)}, bf16[16,2048]{1,0:T(8,128)(2,1)S(1)}, u32[]{:S(2)}, u32[]{:S(2)}) collective-permute-start(bf16[16,2048]{1,0:T(8,128)(2,1)} %get-tuple-element.29.refs_0_), channel_id=1, source_target_pairs={{0,24},{1,25},{2,26},{3,27},{4,28},{5,29},{6,30},{7,31},{8,16},{9,... | collective-permute-start | bytes 196616 | tf_op jit(solution)/shard_map/ppermute | solution.py:293
  12.1 28.6 %copy-start.4 = (bf16[16,2048]{1,0:T(8,128)(2,1)}, bf16[16,2048]{1,0:T(8,128)(2,1)S(1)}, u32[]{:S(2)}) copy-start(bf16[16,2048]{1,0:T(8,128)(2,1)S(1)} %collective-permute-done.refs_1_) | copy-start | bytes 196612
  12.8 28.0 %copy-start.5 = (bf16[16,2048]{1,0:T(8,128)(2,1)}, bf16[16,2048]{1,0:T(8,128)(2,1)S(1)}, u32[]{:S(2)}) copy-start(bf16[16,2048]{1,0:T(8,128)(2,1)S(1)} %collective-permute-done.1.refs_2_) | copy-start | bytes 196612
  16.1 24.7 %copy-start.6 = (bf16[16,2048]{1,0:T(8,128)(2,1)}, bf16[16,2048]{1,0:T(8,128)(2,1)S(1)}, u32[]{:S(2)}) copy-start(bf16[16,2048]{1,0:T(8,128)(2,1)S(1)} %collective-permute-done.2.refs_3_) | copy-start | bytes 196612
  36.1 18.6 %all-to-all-start.1 = ((bf16[16,4,4096]{2,1,0:T(4,128)(2,1)}), bf16[16,4,4096]{2,1,0:T(4,128)(2,1)S(1)}, u32[]{:S(2)}, u32[]{:S(2)}) async-start(bf16[16,4,4096]{2,1,0:T(4,128)(2,1)} %get-tuple-element.33), calls=%async_computation.1 | async-start | bytes 1048576 | tf_op jit(solution)/shard_map/all_to_all | solution.py:307
  40.2 14.5 %collective-permute-start.3 = (bf16[16,4,4096]{2,1,0:T(4,128)(2,1)S(1)}, bf16[16,4,4096]{2,1,0:T(4,128)(2,1)S(1)}, u32[]{:S(2)}, u32[]{:S(2)}) collective-permute-start(bf16[16,4,4096]{2,1,0:T(4,128)(2,1)S(1)} %all_to_all.25.refs_0_), channel_id=1, source_target_pairs={{0,16},{16,0},{1,17},{17,1},{2,18},{18,2},{3,19},{19,3},{4,20},{20... | collective-permute-start | bytes 1572872 | tf_op jit(solution)/shard_map/ppermute | solution.py:313
  54.6 37.9 %all-to-all-start.2 = ((bf16[8,256,256]{2,1,0:T(8,128)(2,1)}), bf16[8,256,256]{2,1,0:T(8,128)(2,1)S(1)}, u32[]{:S(2)}, u32[]{:S(2)}) async-start(bf16[8,256,256]{2,1,0:T(8,128)(2,1)} %pack.1), calls=%async_computation.2 | async-start | bytes 2097152 | tf_op jit(solution)/shard_map/all_to_all | solution.py:344
  58.3 18.3 %collective-permute-start.4 = (bf16[16,4,4096]{2,1,0:T(4,128)(2,1)S(1)}, bf16[16,4,4096]{2,1,0:T(4,128)(2,1)S(1)}, u32[]{:S(2)}, u32[]{:S(2)}) collective-permute-start(bf16[16,4,4096]{2,1,0:T(4,128)(2,1)S(1)} %all-to-all-done.1.refs_0_), channel_id=1, source_target_pairs={{0,16},{16,0},{1,17},{17,1},{2,18},{18,2},{3,19},{19,3},{4,20},{20... | collective-permute-start | bytes 1572872 | tf_op jit(solution)/shard_map/ppermute | solution.py:313
  75.1 17.5 %collective-permute-start.5 = (bf16[16,4,4096]{2,1,0:T(4,128)(2,1)}, bf16[16,4,4096]{2,1,0:T(4,128)(2,1)}, u32[]{:S(2)}, u32[]{:S(2)}) collective-permute-start(bf16[16,4,4096]{2,1,0:T(4,128)(2,1)} %get-tuple-element.42), channel_id=1, source_target_pairs={{0,16},{16,0},{1,17},{17,1},{2,18},{18,2},{3,19},{19,3},{4,20},{20... | collective-permute-start | bytes 1572872 | tf_op jit(solution)/shard_map/ppermute | solution.py:349
  76.6 16.0 %copy-start.1 = (bf16[16,4,4096]{2,1,0:T(4,128)(2,1)S(1)}, bf16[16,4,4096]{2,1,0:T(4,128)(2,1)}, u32[]{:S(2)}) copy-start(bf16[16,4,4096]{2,1,0:T(4,128)(2,1)} %copy-done) | copy-start | bytes 1572868
  76.6 58.3 %copy-start.2 = (s32[64,2]{0,1:T(2,128)S(1)}, s32[64,2]{0,1:T(2,128)}, u32[]{:S(2)}) copy-start(s32[64,2]{0,1:T(2,128)} %param.15) | copy-start | bytes 1540
  76.6 58.3 %copy-start.3 = (f32[64,2]{0,1:T(2,128)S(1)}, f32[64,2]{0,1:T(2,128)}, u32[]{:S(2)}) copy-start(f32[64,2]{0,1:T(2,128)} %param.16) | copy-start | bytes 1540
  92.0 14.2 %collective-permute-start.13 = (bf16[16,4,4096]{2,1,0:T(4,128)(2,1)}, bf16[16,4,4096]{2,1,0:T(4,128)(2,1)}, u32[]{:S(2)}, u32[]{:S(2)}) collective-permute-start(bf16[16,4,4096]{2,1,0:T(4,128)(2,1)} %get-tuple-element.54), channel_id=1, source_target_pairs={{0,16},{16,0},{1,17},{17,1},{2,18},{18,2},{3,19},{19,3},{4,20},{20... | collective-permute-start | bytes 1572872 | tf_op jit(solution)/shard_map/ppermute | solution.py:349
  94.7 20.5 %all-to-all-start.3 = ((bf16[16,4,4096]{2,1,0:T(4,128)(2,1)}), bf16[16,4,4096]{2,1,0:T(4,128)(2,1)S(1)}, u32[]{:S(2)}, u32[]{:S(2)}) async-start(bf16[16,4,4096]{2,1,0:T(4,128)(2,1)} %add_convert_fusion.1), calls=%async_computation.3 | async-start | bytes 1048576 | tf_op jit(solution)/shard_map/all_to_all | solution.py:379
  104.1 4.3 %collective-permute-start.6 = (bf16[64,256]{1,0:T(8,128)(2,1)S(1)}, bf16[64,256]{1,0:T(8,128)(2,1)S(1)}, u32[]{:S(2)}, u32[]{:S(2)}) collective-permute-start(bf16[64,256]{1,0:T(8,128)(2,1)S(1)} %get-tuple-element.45), channel_id=1, source_target_pairs={{0,1},{1,0},{2,3},{3,2},{4,5},{5,4},{6,7},{7,6},{8,9},{9,8},{10,11... | collective-permute-start | bytes 98312 | tf_op jit(solution)/shard_map/ppermute | solution.py:365
  104.5 4.1 %collective-permute-start.7 = (bf16[64,256]{1,0:T(8,128)(2,1)S(1)}, bf16[64,256]{1,0:T(8,128)(2,1)S(1)}, u32[]{:S(2)}, u32[]{:S(2)}) collective-permute-start(bf16[64,256]{1,0:T(8,128)(2,1)S(1)} %get-tuple-element.46), channel_id=1, source_target_pairs={{0,2},{1,3},{2,0},{3,1},{4,6},{5,7},{6,4},{7,5},{8,10},{9,11},{10,... | collective-permute-start | bytes 98312 | tf_op jit(solution)/shard_map/ppermute | solution.py:365
  106.2 3.4 %collective-permute-start.8 = (bf16[64,256]{1,0:T(8,128)(2,1)S(1)}, bf16[64,256]{1,0:T(8,128)(2,1)S(1)}, u32[]{:S(2)}, u32[]{:S(2)}) collective-permute-start(bf16[64,256]{1,0:T(8,128)(2,1)S(1)} %get-tuple-element.47), channel_id=1, source_target_pairs={{0,3},{1,2},{2,1},{3,0},{4,7},{5,6},{6,5},{7,4},{8,11},{9,10},{10,... | collective-permute-start | bytes 98312 | tf_op jit(solution)/shard_map/ppermute | solution.py:365
  115.2 19.7 %all-to-all-start.4 = ((bf16[16,4,4096]{2,1,0:T(4,128)(2,1)}), bf16[16,4,4096]{2,1,0:T(4,128)(2,1)S(1)}, u32[]{:S(2)}, u32[]{:S(2)}) async-start(bf16[16,4,4096]{2,1,0:T(4,128)(2,1)} %add_convert_fusion), calls=%async_computation.4 | async-start | bytes 1048576 | tf_op jit(solution)/shard_map/all_to_all | solution.py:379
  119.4 11.4 %collective-permute-start.9 = (bf16[64,256]{1,0:T(8,128)(2,1)S(1)}, bf16[64,256]{1,0:T(8,128)(2,1)S(1)}, u32[]{:S(2)}, u32[]{:S(2)}) collective-permute-start(bf16[64,256]{1,0:T(8,128)(2,1)S(1)} %get-tuple-element.48), channel_id=1, source_target_pairs={{0,4},{1,5},{2,6},{3,7},{4,0},{5,1},{6,2},{7,3},{8,12},{9,13},{10,... | collective-permute-start | bytes 98312 | tf_op jit(solution)/shard_map/ppermute | solution.py:365
  121.3 9.5 %collective-permute-start.10 = (bf16[64,256]{1,0:T(8,128)(2,1)S(1)}, bf16[64,256]{1,0:T(8,128)(2,1)S(1)}, u32[]{:S(2)}, u32[]{:S(2)}) collective-permute-start(bf16[64,256]{1,0:T(8,128)(2,1)S(1)} %get-tuple-element.49), channel_id=1, source_target_pairs={{0,5},{1,4},{2,7},{3,6},{4,1},{5,0},{6,3},{7,2},{8,13},{9,12},{10,... | collective-permute-start | bytes 98312 | tf_op jit(solution)/shard_map/ppermute | solution.py:365
  121.3 12.4 %collective-permute-start.11 = (bf16[64,256]{1,0:T(8,128)(2,1)S(1)}, bf16[64,256]{1,0:T(8,128)(2,1)S(1)}, u32[]{:S(2)}, u32[]{:S(2)}) collective-permute-start(bf16[64,256]{1,0:T(8,128)(2,1)S(1)} %get-tuple-element.50), channel_id=1, source_target_pairs={{0,6},{1,7},{2,4},{3,5},{4,2},{5,3},{6,0},{7,1},{8,14},{9,15},{10,... | collective-permute-start | bytes 98312 | tf_op jit(solution)/shard_map/ppermute | solution.py:365
  123.7 10.0 %collective-permute-start.12 = (bf16[64,256]{1,0:T(8,128)(2,1)S(1)}, bf16[64,256]{1,0:T(8,128)(2,1)S(1)}, u32[]{:S(2)}, u32[]{:S(2)}) collective-permute-start(bf16[64,256]{1,0:T(8,128)(2,1)S(1)} %get-tuple-element.51), channel_id=1, source_target_pairs={{0,7},{1,6},{2,5},{3,4},{4,3},{5,2},{6,1},{7,0},{8,15},{9,14},{10,... | collective-permute-start | bytes 98312 | tf_op jit(solution)/shard_map/ppermute | solution.py:365
  (1 other events, 0.8 us)

commit v8 on v7

--- a/solution.py
+++ b/solution.py
@@ -81,8 +81,7 @@
         sum_ref[which * count : (which + 1) * count] = summed.astype(BF16)
 
 
-def pack_kernel(q_hbm, k_hbm, v_hbm, *refs):
-    sum_refs, out_ref, sem = refs[:-2], refs[-2], refs[-1]
+def pack_kernel(q_hbm, k_hbm, v_hbm, out_ref, sem):
     dests, _, width = out_ref.shape
     tokens = q_hbm.shape[0]
     copies = []
@@ -97,18 +96,16 @@
             )
     for copy in copies:
         copy.start()
-    for dest in range(dests):
-        lower = 3 * tokens
-        for ref in sum_refs:
-            upper = lower + ref.shape[0]
-            out_ref[dest, lower:upper] = ref[:, dest * width : (dest + 1) * width]
-            lower = upper
     for copy in copies:
         copy.wait()
 
 
-def attend_kernel(query_rows, tokens, segs, at_ref, recv_ref, *refs):
-    out_refs, mixed_ref = refs[:-1], refs[-1]
+def attend_kernel(query_rows, tokens, segs, at_ref, recv_ref, sum_hbm, *refs):
+    out_refs, (mixed_ref, sum_ref, sem) = refs[:-3], refs[-3:]
+    width = recv_ref.shape[2]
+    columns = pl.ds(pl.multiple_of(at_ref[1] * width, width), width)
+    copy = pltpu.make_async_copy(sum_hbm.at[:, :, columns], sum_ref, sem.at[0])
+    copy.start()
     sources, _, width = recv_ref.shape
     seg_len = sources * tokens
     query, key, value = (
@@ -116,12 +113,9 @@
     )
     sum_total = segs * SUMS
     per = SUMS // sources
-    sum_rows = [
-        recv_ref[:, 3 * tokens + at * per : 3 * tokens + (at + 1) * per].reshape(SUMS, width)
-        for at in range(2 * segs)
-    ]
-    sum_keys = jnp.concatenate(sum_rows[0::2], axis=0)
-    sum_values = jnp.concatenate(sum_rows[1::2], axis=0)
+    copy.wait()
+    sum_keys = sum_ref[:, :per].reshape(sum_total, width)
+    sum_values = sum_ref[:, per:].reshape(sum_total, width)
     scale = 1.0 / math.sqrt(HDIM)
     segment = at_ref[0]
     lane = lax.broadcasted_iota(jnp.int32, (1, width), 1)
@@ -133,7 +127,7 @@
             <= lax.broadcasted_iota(jnp.int32, (query_rows, last), 0) + first
         )
         summ_seg = lax.broadcasted_iota(jnp.int32, (query_rows, sum_total), 1) // SUMS
-        summ_ok = jnp.bitwise_xor(summ_seg, segment) < segment
+        summ_ok = summ_seg < segment
         mixed = jnp.zeros((query_rows, width), F32)
         for head in range(width // HDIM):
             mine = (lane >= head * HDIM) & (lane < (head + 1) * HDIM)
@@ -281,28 +275,18 @@
         name="prep",
     )(tokens, norm_gain.reshape(1, -1), expert_ids.T, attn_keys, attn_values)
 
-    def device(segment, j):
-        return (segment // SEG_DEV) * exp_count + (segment % SEG_DEV) * group + j
-
-    parts = [sums]
-    for other in range(1, segs):
-        pairs = []
-        for segment in range(segs):
-            for j in range(group):
-                pairs.append((device(segment, j), device(segment ^ other, j)))
-        parts.append(lax.ppermute(sums, ("seq", "exp"), pairs))
-    packed_rows = 3 * local_tokens + segs * 2 * local_tokens // block
+    gathered = lax.all_gather(sums, ("seq", "exp"), axis=0)
     packed = pl.pallas_call(
         pack_kernel,
-        out_shape=shape((group, packed_rows, width)),
-        in_specs=[ANY] * 3 + [VMEM] * segs,
+        out_shape=shape((group, 3 * local_tokens, width)),
+        in_specs=[ANY] * 3,
         out_specs=VMEM,
         scratch_shapes=[pltpu.SemaphoreType.DMA((3 * group,))],
         compiler_params=params(56),
         cost_estimate=LITTLE,
         name="pack",
-    )(queries, attn_keys, attn_values, *parts)
-    recv = [lax.all_to_all(after(send[0], parts), "exp", 0, 0, tiled=True)]
+    )(queries, attn_keys, attn_values)
+    recv = [lax.all_to_all(send[0], "exp", 0, 0, tiled=True)]
     for rows in send[1:]:
         recv.append(lax.all_to_all(after(rows, recv[-1]), "exp", 0, 0, tiled=True))
     arrived = []
@@ -352,13 +336,17 @@
     head_out = pl.pallas_call(
         functools.partial(attend_kernel, min(256, seg_len), local_tokens, segs),
         out_shape=[shape((local_tokens, width))] * group,
-        in_specs=[SMEM, VMEM],
+        in_specs=[SMEM, VMEM, ANY],
         out_specs=[VMEM] * group,
-        scratch_shapes=[pltpu.VMEM((group, local_tokens, width), BF16)],
+        scratch_shapes=[
+            pltpu.VMEM((group, local_tokens, width), BF16),
+            pltpu.VMEM((segs * group, sums.shape[0], width), BF16),
+            pltpu.SemaphoreType.DMA((1,)),
+        ],
         compiler_params=params(48),
         cost_estimate=LITTLE,
         name="attend",
-    )(position, got)
+    )(position, got, gathered)
     heads = [
         rows
         if other == 0

time: 138 us -> 141 us (1.022)
  blocking collectives: 20 us -> 0 us
  between operations: 0.74 us -> 14.1 us
  waiting for transfers between devices: 33.5 us -> 41.4 us
  starting transfers between devices: 33.5 us -> 37.4 us
  other arithmetic: 4.34 us -> 2.28 us
    all_to_all x1 -> x0, blocking collectives: 20 us -> none  [on_device(): recv = [lax.all_to_all(after(send[0], parts), 'exp', 0, 0, tiled=True)]]
    all_to_all x0 -> x1, waiting for transfers between devices: none -> 13.7 us  [on_device(): recv = [lax.all_to_all(send[0], 'exp', 0, 0, tiled=True)]]
    all_to_all x0 -> x1, starting transfers between devices: none -> 7.36 us  [on_device(): recv = [lax.all_to_all(send[0], 'exp', 0, 0, tiled=True)]]
    ppermute x3 -> x0, waiting for transfers between devices: 6.27 us -> none  [on_device(): parts.append(lax.ppermute(sums, ('seq', 'exp'), pairs))]
    ppermute x3 -> x0, starting transfers between devices: 5.63 us -> none  [on_device(): parts.append(lax.ppermute(sums, ('seq', 'exp'), pairs))]
    all_to_all x2, waiting for transfers between devices: 5.59 us -> 3.49 us  [on_device(): back = [lax.all_to_all(rows, 'exp', 0, 0, tiled=True) for rows in mine]]
    convert_element_type x2, other arithmetic: 4.26 us -> 2.21 us  [on_device(): mine.append(summed.astype(BF16))]
    ppermute x2, starting transfers between devices: 1.12 us -> 3.17 us  [on_device(): planes.append(lax.ppermute(rows, 'seq', pairs))]
  transfers between devices with their start and end apart: 18 -> 17, of which waited for: 9 -> 7; matrix products, arithmetic and copies ran while one was open for 3% -> 2% of each run, Pallas kernels for 28% -> 27%
where the time goes in v8:
time: 141 us; the launch traced here: 139 us
  Pallas kernels  42.7 us (30%)
  waiting for transfers between devices  41.4 us (29%)
  starting transfers between devices  37.4 us (27%)
  between operations  14.1 us (10%)
  other arithmetic  2.28 us (2%)
  local copies, waits for them, and re-layouts  1.6 us (1%)
    pallas_call x2, Pallas kernels, on_device(): pl.pallas_call(functools.partial(ffn_kernel, chunk * experts, seq_count),...  30.8 us
    all_to_all x1, waiting for transfers between devices, on_device(): recv = [lax.all_to_all(send[0], 'exp', 0, 0, tiled=True)]  13.7 us
    ppermute x7, waiting for transfers between devices, on_device(): lax.ppermute(rows, 'exp', [(i, i ^ other) for i in range(exp_count)])  12.4 us
    all_to_all x1, waiting for transfers between devices, on_device(): recv.append(lax.all_to_all(after(rows, recv[-1]), 'exp', 0, 0, tiled=True))  11.1 us
    all_to_all x2, starting transfers between devices, on_device(): back = [lax.all_to_all(rows, 'exp', 0, 0, tiled=True) for rows in mine]  10.2 us
    all_to_all x1, starting transfers between devices, on_device(): recv = [lax.all_to_all(send[0], 'exp', 0, 0, tiled=True)]  7.36 us
    ppermute x7, starting transfers between devices, on_device(): lax.ppermute(rows, 'exp', [(i, i ^ other) for i in range(exp_count)])  6.76 us
    all_to_all x1, starting transfers between devices, on_device(): recv.append(lax.all_to_all(after(rows, recv[-1]), 'exp', 0, 0, tiled=True))  4.1 us
  transfers between devices with their start and end apart: 17, of which 7 were waited for; matrix products, arithmetic and copies ran while one was open for 2% of the time, Pallas kernels for 27%

profile of v8, /device:TPU:0, one launch (start us, length us, event | category | flops | bytes accessed | tf_op | source)
XLA Modules:
  0.0 139.5 jit_solution(9961235265700755644)
XLA Ops:
  7.2 3.5 %prep.1 = (bf16[16,4,4096]{2,1,0:T(4,128)(2,1)}, bf16[16,4,4096]{2,1,0:T(4,128)(2,1)}, bf16[16,2048]{1,0:T(8,128)(2,1)}) custom-call(bf16[64,4096]{1,0:T(8,128)(2,1)} %tok_hbm.1, f32[1,4096]{1,0:T(1,128)} %bitcast.10, s32[2,64]{1,0:T(2,128)} %bitcast.7, bf16[64,2048]{1,0:T(8,128)(2,1)} %k_hbm.3, bf16[64,2048]{1,0:T(8,128)(2,1)} %v_hbm.3), custom_call_target="tpu_custom_call" | custom-call | flops 1000 | bytes 1000 | tf_op jit(solution)/shard_map/prep/pallas_call | solution.py:261
  10.7 7.4 %all-to-all-start = ((bf16[16,4,4096]{2,1,0:T(4,128)(2,1)}), bf16[16,4,4096]{2,1,0:T(4,128)(2,1)S(1)}, u32[]{:S(2)}, u32[]{:S(2)}) async-start(bf16[16,4,4096]{2,1,0:T(4,128)(2,1)} %get-tuple-element.29), calls=%async_computation | async-start | bytes 1048576 | tf_op jit(solution)/shard_map/all_to_all | solution.py:289
  18.8 13.7 %all-to-all-done.refs_0_ = bf16[16,4,4096]{2,1,0:T(4,128)(2,1)S(1)} async-done(((bf16[16,4,4096]{2,1,0:T(4,128)(2,1)}), bf16[16,4,4096]{2,1,0:T(4,128)(2,1)S(1)}, u32[]{:S(2)}, u32[]{:S(2)}) %all-to-all-start) | async-done | bytes 524320 | tf_op jit(solution)/shard_map/all_to_all | solution.py:289
  32.6 4.1 %all-to-all-start.1 = ((bf16[16,4,4096]{2,1,0:T(4,128)(2,1)}), bf16[16,4,4096]{2,1,0:T(4,128)(2,1)S(1)}, u32[]{:S(2)}, u32[]{:S(2)}) async-start(bf16[16,4,4096]{2,1,0:T(4,128)(2,1)} %get-tuple-element.30), calls=%async_computation.1 | async-start | bytes 1048576 | tf_op jit(solution)/shard_map/all_to_all | solution.py:291
  36.7 1.6 %collective-permute-start = (bf16[16,4,4096]{2,1,0:T(4,128)(2,1)S(1)}, bf16[16,4,4096]{2,1,0:T(4,128)(2,1)S(1)}, u32[]{:S(2)}, u32[]{:S(2)}) collective-permute-start(bf16[16,4,4096]{2,1,0:T(4,128)(2,1)S(1)} %all-to-all-done.refs_0_), channel_id=1, source_target_pairs={{0,16},{16,0},{1,17},{17,1},{2,18},{18,2},{3,19},{19,3},{4,20},{20... | collective-permute-start | bytes 1572872 | tf_op jit(solution)/shard_map/ppermute | solution.py:297
  38.2 2.2 %pack.1 = bf16[8,192,256]{2,1,0:T(8,128)(2,1)} custom-call(bf16[64,2048]{1,0:T(8,128)(2,1)} %q_hbm.1, bf16[64,2048]{1,0:T(8,128)(2,1)} %k_hbm.3, bf16[64,2048]{1,0:T(8,128)(2,1)} %v_hbm.3), custom_call_target="tpu_custom_call" | custom-call | flops 1000 | bytes 1000 | tf_op jit(solution)/shard_map/pack/pallas_call | solution.py:279
  40.4 11.1 %all-to-all-done.1.refs_0_ = bf16[16,4,4096]{2,1,0:T(4,128)(2,1)S(1)} async-done(((bf16[16,4,4096]{2,1,0:T(4,128)(2,1)}), bf16[16,4,4096]{2,1,0:T(4,128)(2,1)S(1)}, u32[]{:S(2)}, u32[]{:S(2)}) %all-to-all-start.1) | async-done | bytes 524320 | tf_op jit(solution)/shard_map/all_to_all | solution.py:291
  51.5 3.5 %all-to-all-start.2 = ((bf16[8,192,256]{2,1,0:T(8,128)(2,1)}), bf16[8,192,256]{2,1,0:T(8,128)(2,1)S(1)}, u32[]{:S(2)}, u32[]{:S(2)}) async-start(bf16[8,192,256]{2,1,0:T(8,128)(2,1)} %pack.1), calls=%async_computation.2 | async-start | bytes 1572864 | tf_op jit(solution)/shard_map/all_to_all | solution.py:328
  55.0 1.6 %collective-permute-start.1 = (bf16[16,4,4096]{2,1,0:T(4,128)(2,1)S(1)}, bf16[16,4,4096]{2,1,0:T(4,128)(2,1)S(1)}, u32[]{:S(2)}, u32[]{:S(2)}) collective-permute-start(bf16[16,4,4096]{2,1,0:T(4,128)(2,1)S(1)} %all-to-all-done.1.refs_0_), channel_id=1, source_target_pairs={{0,16},{16,0},{1,17},{17,1},{2,18},{18,2},{3,19},{19,3},{4,20},{20... | collective-permute-start | bytes 1572872 | tf_op jit(solution)/shard_map/ppermute | solution.py:297
  56.6 15.5 %experts.2 = (bf16[16,4,4096]{2,1,0:T(4,128)(2,1)S(1)}, bf16[16,4,4096]{2,1,0:T(4,128)(2,1)}) custom-call(bf16[16,4,4096]{2,1,0:T(4,128)(2,1)S(1)} %all-to-all-done.refs_0_, bf16[16,4,4096]{2,1,0:T(4,128)(2,1)S(1)} %collective-permute-done.refs_1_, bf16[4,704,4096]{2,1,0:T(8,128)(2,1)} %refs_2_.3, bf16[4,704,4096]{2,1,0:T(8,128)(2,1)} %refs_3_.3, ...), custom_call_target="tpu_custom_call" | custom-call | flops 2214592512 | bytes 103809024 | tf_op jit(solution)/shard_map/experts/pallas_call | solution.py:306
  72.7 15.3 %experts.3 = (bf16[16,4,4096]{2,1,0:T(4,128)(2,1)S(1)}, bf16[16,4,4096]{2,1,0:T(4,128)(2,1)}) custom-call(bf16[16,4,4096]{2,1,0:T(4,128)(2,1)S(1)} %all-to-all-done.1.refs_0_, bf16[16,4,4096]{2,1,0:T(4,128)(2,1)S(1)} %collective-permute-done.1.refs_1_, bf16[4,704,4096]{2,1,0:T(8,128)(2,1)} %refs_2_.3, bf16[4,704,4096]{2,1,0:T(8,128)(2,1)} %refs_3_.3, ...), custom_call_target="tpu_custom_call" | custom-call | flops 2214592512 | bytes 103809024 | tf_op jit(solution)/shard_map/experts/pallas_call | solution.py:306
  88.0 1.6 %collective-permute-start.10 = (bf16[16,4,4096]{2,1,0:T(4,128)(2,1)}, bf16[16,4,4096]{2,1,0:T(4,128)(2,1)S(1)}, u32[]{:S(2)}, u32[]{:S(2)}) collective-permute-start(bf16[16,4,4096]{2,1,0:T(4,128)(2,1)} %get-tuple-element.52), channel_id=1, source_target_pairs={{0,16},{16,0},{1,17},{17,1},{2,18},{18,2},{3,19},{19,3},{4,20},{20... | collective-permute-start | bytes 1572872 | tf_op jit(solution)/shard_map/ppermute | solution.py:333
  90.7 6.1 %all-to-all-start.3 = ((bf16[16,4,4096]{2,1,0:T(4,128)(2,1)}), bf16[16,4,4096]{2,1,0:T(4,128)(2,1)S(1)}, u32[]{:S(2)}, u32[]{:S(2)}) async-start(bf16[16,4,4096]{2,1,0:T(4,128)(2,1)} %add_convert_fusion.1), calls=%async_computation.3 | async-start | bytes 1048576 | tf_op jit(solution)/shard_map/all_to_all | solution.py:367
  96.9 1.6 %copy-done = bf16[512,2048]{1,0:T(8,128)(2,1)S(1)} copy-done((bf16[512,2048]{1,0:T(8,128)(2,1)S(1)}, bf16[512,2048]{1,0:T(8,128)(2,1)}, u32[]{:S(2)}) %copy-start) | copy-done | bytes 2097176
  98.5 3.3 %attend.1 = (bf16[64,256]{1,0:T(8,128)(2,1)S(1)}, bf16[64,256]{1,0:T(8,128)(2,1)S(1)}, bf16[64,256]{1,0:T(8,128)(2,1)S(1)}, bf16[64,256]{1,0:T(8,128)(2,1)S(1)},...) custom-call(s32[2]{0:T(128)S(1)} %pad_add_fusion.at_ref, ...), custom_call_target="tpu_custom_call" | custom-call | flops 1000 | bytes 1000 | tf_op jit(solution)/shard_map/attend/pallas_call | solution.py:336
  102.3 1.7 %collective-permute-start.4 = (bf16[64,256]{1,0:T(8,128)(2,1)S(1)}, bf16[64,256]{1,0:T(8,128)(2,1)S(1)}, u32[]{:S(2)}, u32[]{:S(2)}) collective-permute-start(bf16[64,256]{1,0:T(8,128)(2,1)S(1)} %get-tuple-element.44), channel_id=1, source_target_pairs={{0,2},{1,3},{2,0},{3,1},{4,6},{5,7},{6,4},{7,5},{8,10},{9,11},{10,... | collective-permute-start | bytes 98312 | tf_op jit(solution)/shard_map/ppermute | solution.py:353
  105.1 1.4 %collective-permute-done.4.refs_2_ = bf16[64,256]{1,0:T(8,128)(2,1)S(1)} collective-permute-done((bf16[64,256]{1,0:T(8,128)(2,1)S(1)}, bf16[64,256]{1,0:T(8,128)(2,1)S(1)}, u32[]{:S(2)}, u32[]{:S(2)}) %collective-permute-start.4) | collective-permute-done | bytes 32800 | tf_op jit(solution)/shard_map/ppermute | solution.py:353
  107.8 3.5 %all-to-all-done.3.refs_0_ = bf16[16,4,4096]{2,1,0:T(4,128)(2,1)S(1)} async-done(((bf16[16,4,4096]{2,1,0:T(4,128)(2,1)}), bf16[16,4,4096]{2,1,0:T(4,128)(2,1)S(1)}, u32[]{:S(2)}, u32[]{:S(2)}) %all-to-all-start.3) | async-done | bytes 524320 | tf_op jit(solution)/shard_map/all_to_all | solution.py:367
  111.3 4.1 %all-to-all-start.4 = ((bf16[16,4,4096]{2,1,0:T(4,128)(2,1)}), bf16[16,4,4096]{2,1,0:T(4,128)(2,1)S(1)}, u32[]{:S(2)}, u32[]{:S(2)}) async-start(bf16[16,4,4096]{2,1,0:T(4,128)(2,1)} %add_convert_fusion), calls=%async_computation.4 | async-start | bytes 1048576 | tf_op jit(solution)/shard_map/all_to_all | solution.py:367
  115.4 1.9 %collective-permute-start.6 = (bf16[64,256]{1,0:T(8,128)(2,1)S(1)}, bf16[64,256]{1,0:T(8,128)(2,1)S(1)}, u32[]{:S(2)}, u32[]{:S(2)}) collective-permute-start(bf16[64,256]{1,0:T(8,128)(2,1)S(1)} %get-tuple-element.46), channel_id=1, source_target_pairs={{0,4},{1,5},{2,6},{3,7},{4,0},{5,1},{6,2},{7,3},{8,12},{9,13},{10,... | collective-permute-start | bytes 98312 | tf_op jit(solution)/shard_map/ppermute | solution.py:353
  117.4 2.4 %collective-permute-start.8 = (bf16[64,256]{1,0:T(8,128)(2,1)S(1)}, bf16[64,256]{1,0:T(8,128)(2,1)S(1)}, u32[]{:S(2)}, u32[]{:S(2)}) collective-permute-start(bf16[64,256]{1,0:T(8,128)(2,1)S(1)} %get-tuple-element.48), channel_id=1, source_target_pairs={{0,6},{1,7},{2,4},{3,5},{4,2},{5,3},{6,0},{7,1},{8,14},{9,15},{10,... | collective-permute-start | bytes 98312 | tf_op jit(solution)/shard_map/ppermute | solution.py:353
  120.0 6.8 %collective-permute-done.6.refs_4_ = bf16[64,256]{1,0:T(8,128)(2,1)S(1)} collective-permute-done((bf16[64,256]{1,0:T(8,128)(2,1)S(1)}, bf16[64,256]{1,0:T(8,128)(2,1)S(1)}, u32[]{:S(2)}, u32[]{:S(2)}) %collective-permute-start.6) | collective-permute-done | bytes 32800 | tf_op jit(solution)/shard_map/ppermute | solution.py:353
  126.8 2.9 %collective-permute-done.8.refs_6_ = bf16[64,256]{1,0:T(8,128)(2,1)S(1)} collective-permute-done((bf16[64,256]{1,0:T(8,128)(2,1)S(1)}, bf16[64,256]{1,0:T(8,128)(2,1)S(1)}, u32[]{:S(2)}, u32[]{:S(2)}) %collective-permute-start.8) | collective-permute-done | bytes 32800 | tf_op jit(solution)/shard_map/ppermute | solution.py:353
  131.0 1.6 %mix.1 = bf16[64,4096]{1,0:T(8,128)(2,1)} custom-call(s32[2,64]{1,0:T(2,128)S(1)} %bitcast.8, f32[2,64]{1,0:T(2,128)S(1)} %bitcast.9, bf16[16,4,4096]{2,1,0:T(4,128)(2,1)S(1)} %all-to-all-done.3.refs_0_, bf16[16,4,4096]{2,1,0:T(4,128)(2,1)S(1)} %all-to-all-done.4.refs_1_), custom_call_target="tpu_custom_call" | custom-call | flops 1000 | bytes 1000 | tf_op jit(solution)/shard_map/mix/pallas_call | solution.py:368
  (27 shorter events, 6.9 us)
Async XLA Ops:
  10.7 21.8 %all-to-all-start = ((bf16[16,4,4096]{2,1,0:T(4,128)(2,1)}), bf16[16,4,4096]{2,1,0:T(4,128)(2,1)S(1)}, u32[]{:S(2)}, u32[]{:S(2)}) async-start(bf16[16,4,4096]{2,1,0:T(4,128)(2,1)} %get-tuple-element.29), calls=%async_computation | async-start | bytes 1048576 | tf_op jit(solution)/shard_map/all_to_all | solution.py:289
  18.1 78.8 %all-gather.3.cloned.1.call-start = ((), (), s32[]{:S(2)}) async-start(), calls=%async_computation.5 | async-start | bytes 2162688 | tf_op jit(solution)/shard_map/all_gather | solution.py:278
  32.6 18.9 %all-to-all-start.1 = ((bf16[16,4,4096]{2,1,0:T(4,128)(2,1)}), bf16[16,4,4096]{2,1,0:T(4,128)(2,1)S(1)}, u32[]{:S(2)}, u32[]{:S(2)}) async-start(bf16[16,4,4096]{2,1,0:T(4,128)(2,1)} %get-tuple-element.30), calls=%async_computation.1 | async-start | bytes 1048576 | tf_op jit(solution)/shard_map/all_to_all | solution.py:291
  36.7 14.8 %collective-permute-start = (bf16[16,4,4096]{2,1,0:T(4,128)(2,1)S(1)}, bf16[16,4,4096]{2,1,0:T(4,128)(2,1)S(1)}, u32[]{:S(2)}, u32[]{:S(2)}) collective-permute-start(bf16[16,4,4096]{2,1,0:T(4,128)(2,1)S(1)} %all-to-all-done.refs_0_), channel_id=1, source_target_pairs={{0,16},{16,0},{1,17},{17,1},{2,18},{18,2},{3,19},{19,3},{4,20},{20... | collective-permute-start | bytes 1572872 | tf_op jit(solution)/shard_map/ppermute | solution.py:297
  51.5 38.1 %all-to-all-start.2 = ((bf16[8,192,256]{2,1,0:T(8,128)(2,1)}), bf16[8,192,256]{2,1,0:T(8,128)(2,1)S(1)}, u32[]{:S(2)}, u32[]{:S(2)}) async-start(bf16[8,192,256]{2,1,0:T(8,128)(2,1)} %pack.1), calls=%async_computation.2 | async-start | bytes 1572864 | tf_op jit(solution)/shard_map/all_to_all | solution.py:328
  55.0 17.6 %collective-permute-start.1 = (bf16[16,4,4096]{2,1,0:T(4,128)(2,1)S(1)}, bf16[16,4,4096]{2,1,0:T(4,128)(2,1)S(1)}, u32[]{:S(2)}, u32[]{:S(2)}) collective-permute-start(bf16[16,4,4096]{2,1,0:T(4,128)(2,1)S(1)} %all-to-all-done.1.refs_0_), channel_id=1, source_target_pairs={{0,16},{16,0},{1,17},{17,1},{2,18},{18,2},{3,19},{19,3},{4,20},{20... | collective-permute-start | bytes 1572872 | tf_op jit(solution)/shard_map/ppermute | solution.py:297
  72.1 17.5 %collective-permute-start.2 = (bf16[16,4,4096]{2,1,0:T(4,128)(2,1)}, bf16[16,4,4096]{2,1,0:T(4,128)(2,1)S(1)}, u32[]{:S(2)}, u32[]{:S(2)}) collective-permute-start(bf16[16,4,4096]{2,1,0:T(4,128)(2,1)} %get-tuple-element.39), channel_id=1, source_target_pairs={{0,16},{16,0},{1,17},{17,1},{2,18},{18,2},{3,19},{19,3},{4,20},{20... | collective-permute-start | bytes 1572872 | tf_op jit(solution)/shard_map/ppermute | solution.py:333
  72.7 58.3 %copy-start.1 = (s32[64,2]{0,1:T(2,128)S(1)}, s32[64,2]{0,1:T(2,128)}, u32[]{:S(2)}) copy-start(s32[64,2]{0,1:T(2,128)} %param.15) | copy-start | bytes 1540
  72.7 58.3 %copy-start.2 = (f32[64,2]{0,1:T(2,128)S(1)}, f32[64,2]{0,1:T(2,128)}, u32[]{:S(2)}) copy-start(f32[64,2]{0,1:T(2,128)} %param.16) | copy-start | bytes 1540
  88.0 16.0 %collective-permute-start.10 = (bf16[16,4,4096]{2,1,0:T(4,128)(2,1)}, bf16[16,4,4096]{2,1,0:T(4,128)(2,1)S(1)}, u32[]{:S(2)}, u32[]{:S(2)}) collective-permute-start(bf16[16,4,4096]{2,1,0:T(4,128)(2,1)} %get-tuple-element.52), channel_id=1, source_target_pairs={{0,16},{16,0},{1,17},{17,1},{2,18},{18,2},{3,19},{19,3},{4,20},{20... | collective-permute-start | bytes 1572872 | tf_op jit(solution)/shard_map/ppermute | solution.py:333
  90.7 20.6 %all-to-all-start.3 = ((bf16[16,4,4096]{2,1,0:T(4,128)(2,1)}), bf16[16,4,4096]{2,1,0:T(4,128)(2,1)S(1)}, u32[]{:S(2)}, u32[]{:S(2)}) async-start(bf16[16,4,4096]{2,1,0:T(4,128)(2,1)} %add_convert_fusion.1), calls=%async_computation.3 | async-start | bytes 1048576 | tf_op jit(solution)/shard_map/all_to_all | solution.py:367
  96.9 1.6 %copy-start = (bf16[512,2048]{1,0:T(8,128)(2,1)S(1)}, bf16[512,2048]{1,0:T(8,128)(2,1)}, u32[]{:S(2)}) copy-start(bf16[512,2048]{1,0:T(8,128)(2,1)} %all-gather.3.cloned.1.call-done) | copy-start | bytes 6291460
  101.8 3.3 %collective-permute-start.3 = (bf16[64,256]{1,0:T(8,128)(2,1)S(1)}, bf16[64,256]{1,0:T(8,128)(2,1)S(1)}, u32[]{:S(2)}, u32[]{:S(2)}) collective-permute-start(bf16[64,256]{1,0:T(8,128)(2,1)S(1)} %get-tuple-element.43), channel_id=1, source_target_pairs={{0,1},{1,0},{2,3},{3,2},{4,5},{5,4},{6,7},{7,6},{8,9},{9,8},{10,11... | collective-permute-start | bytes 98312 | tf_op jit(solution)/shard_map/ppermute | solution.py:353
  102.3 4.2 %collective-permute-start.4 = (bf16[64,256]{1,0:T(8,128)(2,1)S(1)}, bf16[64,256]{1,0:T(8,128)(2,1)S(1)}, u32[]{:S(2)}, u32[]{:S(2)}) collective-permute-start(bf16[64,256]{1,0:T(8,128)(2,1)S(1)} %get-tuple-element.44), channel_id=1, source_target_pairs={{0,2},{1,3},{2,0},{3,1},{4,6},{5,7},{6,4},{7,5},{8,10},{9,11},{10,... | collective-permute-start | bytes 98312 | tf_op jit(solution)/shard_map/ppermute | solution.py:353
  104.0 3.9 %collective-permute-start.5 = (bf16[64,256]{1,0:T(8,128)(2,1)S(1)}, bf16[64,256]{1,0:T(8,128)(2,1)S(1)}, u32[]{:S(2)}, u32[]{:S(2)}) collective-permute-start(bf16[64,256]{1,0:T(8,128)(2,1)S(1)} %get-tuple-element.45), channel_id=1, source_target_pairs={{0,3},{1,2},{2,1},{3,0},{4,7},{5,6},{6,5},{7,4},{8,11},{9,10},{10,... | collective-permute-start | bytes 98312 | tf_op jit(solution)/shard_map/ppermute | solution.py:353
  111.3 19.7 %all-to-all-start.4 = ((bf16[16,4,4096]{2,1,0:T(4,128)(2,1)}), bf16[16,4,4096]{2,1,0:T(4,128)(2,1)S(1)}, u32[]{:S(2)}, u32[]{:S(2)}) async-start(bf16[16,4,4096]{2,1,0:T(4,128)(2,1)} %add_convert_fusion), calls=%async_computation.4 | async-start | bytes 1048576 | tf_op jit(solution)/shard_map/all_to_all | solution.py:367
  115.4 11.4 %collective-permute-start.6 = (bf16[64,256]{1,0:T(8,128)(2,1)S(1)}, bf16[64,256]{1,0:T(8,128)(2,1)S(1)}, u32[]{:S(2)}, u32[]{:S(2)}) collective-permute-start(bf16[64,256]{1,0:T(8,128)(2,1)S(1)} %get-tuple-element.46), channel_id=1, source_target_pairs={{0,4},{1,5},{2,6},{3,7},{4,0},{5,1},{6,2},{7,3},{8,12},{9,13},{10,... | collective-permute-start | bytes 98312 | tf_op jit(solution)/shard_map/ppermute | solution.py:353
  117.4 9.5 %collective-permute-start.7 = (bf16[64,256]{1,0:T(8,128)(2,1)S(1)}, bf16[64,256]{1,0:T(8,128)(2,1)S(1)}, u32[]{:S(2)}, u32[]{:S(2)}) collective-permute-start(bf16[64,256]{1,0:T(8,128)(2,1)S(1)} %get-tuple-element.47), channel_id=1, source_target_pairs={{0,5},{1,4},{2,7},{3,6},{4,1},{5,0},{6,3},{7,2},{8,13},{9,12},{10,... | collective-permute-start | bytes 98312 | tf_op jit(solution)/shard_map/ppermute | solution.py:353
  117.4 12.4 %collective-permute-start.8 = (bf16[64,256]{1,0:T(8,128)(2,1)S(1)}, bf16[64,256]{1,0:T(8,128)(2,1)S(1)}, u32[]{:S(2)}, u32[]{:S(2)}) collective-permute-start(bf16[64,256]{1,0:T(8,128)(2,1)S(1)} %get-tuple-element.48), channel_id=1, source_target_pairs={{0,6},{1,7},{2,4},{3,5},{4,2},{5,3},{6,0},{7,1},{8,14},{9,15},{10,... | collective-permute-start | bytes 98312 | tf_op jit(solution)/shard_map/ppermute | solution.py:353
  119.8 10.0 %collective-permute-start.9 = (bf16[64,256]{1,0:T(8,128)(2,1)S(1)}, bf16[64,256]{1,0:T(8,128)(2,1)S(1)}, u32[]{:S(2)}, u32[]{:S(2)}) collective-permute-start(bf16[64,256]{1,0:T(8,128)(2,1)S(1)} %get-tuple-element.49), channel_id=1, source_target_pairs={{0,7},{1,6},{2,5},{3,4},{4,3},{5,2},{6,1},{7,0},{8,15},{9,14},{10,... | collective-permute-start | bytes 98312 | tf_op jit(solution)/shard_map/ppermute | solution.py:353
Sparse Core Ops, SparseCore 0:
  22.3 59.8 all-gather.2

commit v9 on v6

--- a/solution.py
+++ b/solution.py
@@ -14,7 +14,6 @@
 SEG_DEV = 2
 CAP = 2
 CHUNKS = 2
-FLIGHT = 2
 
 EPS = 1e-05
 NEG = -1e30
@@ -169,16 +168,8 @@
         for which, ref in enumerate((gate_ref, up_ref, down_ref)):
             at = expert * 3 + which
             copy = pltpu.make_async_copy(ref.at[base + expert], buf.at[at], sem.at[at])
+            copy.start()
             copies.append(copy)
-    for copy in copies[:FLIGHT]:
-        copy.start()
-
-    def weight(at):
-        copies[at].wait()
-        if at + FLIGHT < len(copies):
-            copies[at + FLIGHT].start()
-        return buf[at]
-
     total = planes * sources * step
     for plane in range(planes):
         for source in range(sources):
@@ -193,10 +184,13 @@
     nt = (((1,), (1,)), ((), ()))
     for expert in range(experts):
         rows = x_ref[expert * per : (expert + 1) * per]
-        gate = lax.dot_general(rows, weight(expert * 3), nt, preferred_element_type=F32)
-        up = lax.dot_general(rows, weight(expert * 3 + 1), nt, preferred_element_type=F32)
+        copies[expert * 3].wait()
+        gate = lax.dot_general(rows, buf[expert * 3], nt, preferred_element_type=F32)
+        copies[expert * 3 + 1].wait()
+        up = lax.dot_general(rows, buf[expert * 3 + 1], nt, preferred_element_type=F32)
         hidden = (gate / (1.0 + jnp.exp(-gate)) * up).astype(BF16)
-        piece = jnp.dot(hidden, weight(expert * 3 + 2), preferred_element_type=F32)
+        copies[expert * 3 + 2].wait()
+        piece = jnp.dot(hidden, buf[expert * 3 + 2], preferred_element_type=F32)
         x_ref[expert * per : (expert + 1) * per] = piece.astype(BF16)
     inverse = (to // step) * CAP + (to % step // CAP) * per + to % CAP
     unsort = jnp.where(frm == inverse, 1.0, 0.0).astype(BF16)
@@ -297,7 +291,7 @@
     position = jnp.stack([segment, place]).astype(jnp.int32)
     done, mine = [], []
     for chunk in range(chunks):
-        planes = [after(arrived[chunk][0], recv[-1])] + arrived[chunk][1:]
+        planes = [after(arrived[chunk][0], recv[-1] if chunk == 0 else pieces[0])] + arrived[chunk][1:]
         total = seq_count * exp_count * step
         pieces = pl.pallas_call(
             functools.partial(ffn_kernel, chunk * experts, seq_count),
@@ -322,13 +316,6 @@
     packed = after(after(packed, recv[-1]), arrived[0])
     halves = [[half * group + j for j in range(group)] for half in range(SEG_DEV)]
     got = lax.all_to_all(packed, "exp", 0, 0, axis_index_groups=halves, tiled=True)
-    for chunk, pieces in enumerate(done):
-        summed = after(after(pieces[0], done[-1][0]), got).astype(F32)
-        for other in range(1, seq_count):
-            pairs = [(i, i ^ other) for i in range(seq_count)]
-            summed = summed + lax.ppermute(pieces[other], "seq", pairs).astype(F32)
-        mine.append(summed.astype(BF16))
-    got = after(got, mine[0])
     sums = pl.pallas_call(
         functools.partial(sums_kernel, seg_len // SUMS),
         out_shape=shape((2 * SUMS, width)),
@@ -345,6 +332,13 @@
             for j in range(group):
                 pairs.append((device(frm, j), device(frm ^ other, j)))
         parts.append(lax.ppermute(sums, ("seq", "exp"), pairs))
+    for chunk, pieces in enumerate(done):
+        summed = after(after(pieces[0], done[-1][0]), got).astype(F32)
+        for other in range(1, seq_count):
+            pairs = [(i, i ^ other) for i in range(seq_count)]
+            summed = summed + lax.ppermute(pieces[other], "seq", pairs).astype(F32)
+        mine.append(summed.astype(BF16))
+    got = after(got, mine[0])
     head_out = pl.pallas_call(
         functools.partial(attend_kernel, min(256, seg_len), local_tokens, segs),
         out_shape=[shape((local_tokens, width))] * group,
@@ -371,6 +365,7 @@
         name="place",
     )(position, *heads)
 
+    mine[-1] = after(mine[-1], parts)
     back = [lax.all_to_all(rows, "exp", 0, 0, tiled=True) for rows in mine]
     expert_mix = pl.pallas_call(
         mix_kernel,

time: 159 us -> 134 us (0.84)
  waiting for transfers between devices: 56.1 us -> 29.3 us
    ppermute x2, waiting for transfers between devices: 12.8 us -> 0.01 us  [on_device(): planes.append(lax.ppermute(rows, 'seq', pairs))]
    all_to_all x2, waiting for transfers between devices: 8.81 us -> 0.01 us  [on_device(): back = [lax.all_to_all(rows, 'exp', 0, 0, tiled=True) for rows in mine]]
    ppermute x2, waiting for transfers between devices: 4.58 us -> 0.01 us  [on_device(): summed = summed + lax.ppermute(pieces[other], 'seq', pairs).astype(F32)]
    ppermute x3, waiting for transfers between devices: 16.1 us -> 13.8 us  [on_device(): parts.append(lax.ppermute(sums, ('seq', 'exp'), pairs))]
    ppermute x7, waiting for transfers between devices: 3.1 us -> 4.78 us  [on_device(): lax.ppermute(rows, 'exp', [(i, i ^ other) for i in range(exp_count)])]
  transfers between devices with their start and end apart: 18 -> 18, of which waited for: 7 -> 6; matrix products, arithmetic and copies ran while one was open for 2% -> 4% of each run, Pallas kernels for 24% -> 28%
where the time goes in v9:
time: 134 us; the launch traced here: 133 us
  Pallas kernels  42 us (31%)
  starting transfers between devices  34.6 us (26%)
  waiting for transfers between devices  29.3 us (22%)
  blocking collectives  21.8 us (16%)
  other arithmetic  4.85 us (4%)
    pallas_call x2, Pallas kernels, on_device(): pl.pallas_call(functools.partial(ffn_kernel, chunk * experts, seq_count),...  29.9 us
    all_to_all x1, blocking collectives, on_device(): recv = [lax.all_to_all(send[0], 'exp', 0, 0, tiled=True)]  21.8 us
    ppermute x3, waiting for transfers between devices, on_device(): parts.append(lax.ppermute(sums, ('seq', 'exp'), pairs))  13.8 us
    all_to_all x1, waiting for transfers between devices, on_device(): recv.append(lax.all_to_all(after(rows, recv[-1]), 'exp', 0, 0, tiled=True))  10.7 us
    all_to_all x2, starting transfers between devices, on_device(): back = [lax.all_to_all(rows, 'exp', 0, 0, tiled=True) for rows in mine]  9.79 us
    ppermute x7, starting transfers between devices, on_device(): lax.ppermute(rows, 'exp', [(i, i ^ other) for i in range(exp_count)])  7.35 us
    ppermute x7, waiting for transfers between devices, on_device(): lax.ppermute(rows, 'exp', [(i, i ^ other) for i in range(exp_count)])  4.78 us
    convert_element_type x2, other arithmetic, on_device(): mine.append(summed.astype(BF16))  4.77 us
  transfers between devices with their start and end apart: 18, of which 6 were waited for; matrix products, arithmetic and copies ran while one was open for 4% of the time, Pallas kernels for 28%

profile of v9, /device:TPU:0, one launch (start us, length us, event | category | flops | bytes accessed | tf_op | source)
XLA Modules:
  0.0 133.3 jit_solution(9341397608441113033)
XLA Ops:
  0.6 3.4 %prep.1 = (bf16[16,4,4096]{2,1,0:T(4,128)(2,1)}, bf16[16,4,4096]{2,1,0:T(4,128)(2,1)}) custom-call(bf16[64,4096]{1,0:T(8,128)(2,1)} %tok_hbm.1, f32[1,4096]{1,0:T(1,128)} %bitcast.8, s32[2,64]{1,0:T(2,128)} %bitcast.5), custom_call_target="tpu_custom_call" | custom-call | flops 1000 | bytes 1000 | tf_op jit(solution)/shard_map/prep/pallas_call | solution.py:255
  4.0 21.8 %all_to_all.25.refs_0_ = bf16[16,4,4096]{2,1,0:T(4,128)(2,1)S(1)} all-to-all(bf16[16,4,4096]{2,1,0:T(4,128)(2,1)} %get-tuple-element.28), channel_id=1, replica_groups=mesh['seq'=2,'exp'=16] {'exp'}, dimensions={0} | all-to-all | bytes 1048576 | tf_op jit(solution)/shard_map/all_to_all | solution.py:279
  25.8 4.1 %all-to-all-start.1 = ((bf16[16,4,4096]{2,1,0:T(4,128)(2,1)}), bf16[16,4,4096]{2,1,0:T(4,128)(2,1)S(1)}, u32[]{:S(2)}, u32[]{:S(2)}) async-start(bf16[16,4,4096]{2,1,0:T(4,128)(2,1)} %get-tuple-element.29), calls=%async_computation.1 | async-start | bytes 1048576 | tf_op jit(solution)/shard_map/all_to_all | solution.py:281
  30.0 1.6 %collective-permute-start = (bf16[16,4,4096]{2,1,0:T(4,128)(2,1)S(1)}, bf16[16,4,4096]{2,1,0:T(4,128)(2,1)S(1)}, u32[]{:S(2)}, u32[]{:S(2)}) collective-permute-start(bf16[16,4,4096]{2,1,0:T(4,128)(2,1)S(1)} %all_to_all.25.refs_0_), channel_id=1, source_target_pairs={{0,16},{16,0},{1,17},{17,1},{2,18},{18,2},{3,19},{19,3},{4,20},{20... | collective-permute-start | bytes 1572872 | tf_op jit(solution)/shard_map/ppermute | solution.py:287
  31.5 2.2 %pack.1 = bf16[8,192,256]{2,1,0:T(8,128)(2,1)} custom-call(bf16[64,2048]{1,0:T(8,128)(2,1)} %q_hbm.1, bf16[64,2048]{1,0:T(8,128)(2,1)} %k_hbm.1, bf16[64,2048]{1,0:T(8,128)(2,1)} %v_hbm.1), custom_call_target="tpu_custom_call" | custom-call | flops 1000 | bytes 1000 | tf_op jit(solution)/shard_map/pack/pallas_call | solution.py:269
  33.7 10.7 %all-to-all-done.1.refs_0_ = bf16[16,4,4096]{2,1,0:T(4,128)(2,1)S(1)} async-done(((bf16[16,4,4096]{2,1,0:T(4,128)(2,1)}), bf16[16,4,4096]{2,1,0:T(4,128)(2,1)S(1)}, u32[]{:S(2)}, u32[]{:S(2)}) %all-to-all-start.1) | async-done | bytes 524320 | tf_op jit(solution)/shard_map/all_to_all | solution.py:281
  44.4 3.6 %all-to-all-start.2 = ((bf16[8,192,256]{2,1,0:T(8,128)(2,1)}), bf16[8,192,256]{2,1,0:T(8,128)(2,1)S(1)}, u32[]{:S(2)}, u32[]{:S(2)}) async-start(bf16[8,192,256]{2,1,0:T(8,128)(2,1)} %pack.1), calls=%async_computation.2 | async-start | bytes 1572864 | tf_op jit(solution)/shard_map/all_to_all | solution.py:318
  48.0 1.6 %collective-permute-start.1 = (bf16[16,4,4096]{2,1,0:T(4,128)(2,1)S(1)}, bf16[16,4,4096]{2,1,0:T(4,128)(2,1)S(1)}, u32[]{:S(2)}, u32[]{:S(2)}) collective-permute-start(bf16[16,4,4096]{2,1,0:T(4,128)(2,1)S(1)} %all-to-all-done.1.refs_0_), channel_id=1, source_target_pairs={{0,16},{16,0},{1,17},{17,1},{2,18},{18,2},{3,19},{19,3},{4,20},{20... | collective-permute-start | bytes 1572872 | tf_op jit(solution)/shard_map/ppermute | solution.py:287
  49.6 15.5 %experts.2 = (bf16[16,4,4096]{2,1,0:T(4,128)(2,1)S(1)}, bf16[16,4,4096]{2,1,0:T(4,128)(2,1)}) custom-call(bf16[16,4,4096]{2,1,0:T(4,128)(2,1)S(1)} %all_to_all.25.refs_0_, bf16[16,4,4096]{2,1,0:T(4,128)(2,1)S(1)} %collective-permute-done.refs_1_, bf16[4,704,4096]{2,1,0:T(8,128)(2,1)} %refs_2_.3, bf16[4,704,4096]{2,1,0:T(8,128)(2,1)} %refs_3_.3, ...), custom_call_target="tpu_custom_call" | custom-call | flops 2214592512 | bytes 103809024 | tf_op jit(solution)/shard_map/experts/pallas_call | solution.py:296
  65.6 14.5 %experts.3 = (bf16[16,4,4096]{2,1,0:T(4,128)(2,1)S(1)}, bf16[16,4,4096]{2,1,0:T(4,128)(2,1)S(1)}) custom-call(bf16[16,4,4096]{2,1,0:T(4,128)(2,1)S(1)} %all-to-all-done.1.refs_0_, bf16[16,4,4096]{2,1,0:T(4,128)(2,1)S(1)} %collective-permute-done.1.refs_1_, bf16[4,704,4096]{2,1,0:T(8,128)(2,1)} %refs_2_.3, bf16[4,704,4096]{2,1,0:T(8,128)(2,1)} %refs_3_.3, ...), custom_call_target="tpu_custom_call" | custom-call | flops 2214592512 | bytes 103809024 | tf_op jit(solution)/shard_map/experts/pallas_call | solution.py:296
  80.1 1.6 %collective-permute-start.13 = (bf16[16,4,4096]{2,1,0:T(4,128)(2,1)S(1)}, bf16[16,4,4096]{2,1,0:T(4,128)(2,1)}, u32[]{:S(2)}, u32[]{:S(2)}) collective-permute-start(bf16[16,4,4096]{2,1,0:T(4,128)(2,1)S(1)} %get-tuple-element.50), channel_id=1, source_target_pairs={{0,16},{16,0},{1,17},{17,1},{2,18},{18,2},{3,19},{19,3},{4,20},{20... | collective-permute-start | bytes 1572872 | tf_op jit(solution)/shard_map/ppermute | solution.py:339
  81.7 2.4 %add_convert_fusion.1 = bf16[16,4,4096]{2,1,0:T(4,128)(2,1)} fusion(bf16[16,4,4096]{2,1,0:T(4,128)(2,1)} %collective-permute-done.2, bf16[16,4,4096]{2,1,0:T(4,128)(2,1)S(1)} %get-tuple-element.37), kind=kLoop, calls=%fused_computation.1 | loop fusion | flops 1048576 | bytes 1572864 | tf_op jit(solution)/shard_map/convert_element_type | solution.py:340
  84.1 6.1 %all-to-all-start.3 = ((bf16[16,4,4096]{2,1,0:T(4,128)(2,1)}), bf16[16,4,4096]{2,1,0:T(4,128)(2,1)S(1)}, u32[]{:S(2)}, u32[]{:S(2)}) async-start(bf16[16,4,4096]{2,1,0:T(4,128)(2,1)} %add_convert_fusion.1), calls=%async_computation.3 | async-start | bytes 1048576 | tf_op jit(solution)/shard_map/all_to_all | solution.py:369
  90.3 2.9 %collective-permute-start.3 = (bf16[128,256]{1,0:T(8,128)(2,1)S(1)}, bf16[128,256]{1,0:T(8,128)(2,1)S(1)}, u32[]{:S(2)}, u32[]{:S(2)}) collective-permute-start(bf16[128,256]{1,0:T(8,128)(2,1)S(1)} %sums.1.refs_0_), channel_id=1, source_target_pairs={{0,8},{1,9},{2,10},{3,11},{4,12},{5,13},{6,14},{7,15},{8,0},{9,1},... | collective-permute-start | bytes 196616 | tf_op jit(solution)/shard_map/ppermute | solution.py:334
  94.8 2.4 %add_convert_fusion = bf16[16,4,4096]{2,1,0:T(4,128)(2,1)} fusion(bf16[16,4,4096]{2,1,0:T(4,128)(2,1)} %collective-permute-done.13, bf16[16,4,4096]{2,1,0:T(4,128)(2,1)S(1)} %get-tuple-element.49), kind=kLoop, calls=%fused_computation | loop fusion | flops 1048576 | bytes 1572864 | tf_op jit(solution)/shard_map/convert_element_type | solution.py:340
  97.2 12.9 %collective-permute-done.3.refs_1_ = bf16[128,256]{1,0:T(8,128)(2,1)S(1)} collective-permute-done((bf16[128,256]{1,0:T(8,128)(2,1)S(1)}, bf16[128,256]{1,0:T(8,128)(2,1)S(1)}, u32[]{:S(2)}, u32[]{:S(2)}) %collective-permute-start.3) | collective-permute-done | bytes 65568 | tf_op jit(solution)/shard_map/ppermute | solution.py:334
  111.0 3.7 %all-to-all-start.4 = ((bf16[16,4,4096]{2,1,0:T(4,128)(2,1)}), bf16[16,4,4096]{2,1,0:T(4,128)(2,1)S(1)}, u32[]{:S(2)}, u32[]{:S(2)}) async-start(bf16[16,4,4096]{2,1,0:T(4,128)(2,1)} %add_convert_fusion), calls=%async_computation.4 | async-start | bytes 1048576 | tf_op jit(solution)/shard_map/all_to_all | solution.py:369
  114.8 3.4 %attend.1 = (bf16[64,256]{1,0:T(8,128)(2,1)S(1)}, bf16[64,256]{1,0:T(8,128)(2,1)S(1)}, bf16[64,256]{1,0:T(8,128)(2,1)S(1)}, bf16[64,256]{1,0:T(8,128)(2,1)S(1)},...) custom-call(s32[2]{0:T(128)S(1)} %pad_add_fusion.at_ref, ...), custom_call_target="tpu_custom_call" | custom-call | flops 1000 | bytes 1000 | tf_op jit(solution)/shard_map/attend/pallas_call | solution.py:342
  118.7 1.7 %collective-permute-start.7 = (bf16[64,256]{1,0:T(8,128)(2,1)S(1)}, bf16[64,256]{1,0:T(8,128)(2,1)S(1)}, u32[]{:S(2)}, u32[]{:S(2)}) collective-permute-start(bf16[64,256]{1,0:T(8,128)(2,1)S(1)} %get-tuple-element.42), channel_id=1, source_target_pairs={{0,2},{1,3},{2,0},{3,1},{4,6},{5,7},{6,4},{7,5},{8,10},{9,11},{10,... | collective-permute-start | bytes 98312 | tf_op jit(solution)/shard_map/ppermute | solution.py:355
  120.4 1.7 %collective-permute-start.9 = (bf16[64,256]{1,0:T(8,128)(2,1)S(1)}, bf16[64,256]{1,0:T(8,128)(2,1)S(1)}, u32[]{:S(2)}, u32[]{:S(2)}) collective-permute-start(bf16[64,256]{1,0:T(8,128)(2,1)S(1)} %get-tuple-element.44), channel_id=1, source_target_pairs={{0,4},{1,5},{2,6},{3,7},{4,0},{5,1},{6,2},{7,3},{8,12},{9,13},{10,... | collective-permute-start | bytes 98312 | tf_op jit(solution)/shard_map/ppermute | solution.py:355
  122.2 2.6 %collective-permute-start.11 = (bf16[64,256]{1,0:T(8,128)(2,1)S(1)}, bf16[64,256]{1,0:T(8,128)(2,1)S(1)}, u32[]{:S(2)}, u32[]{:S(2)}) collective-permute-start(bf16[64,256]{1,0:T(8,128)(2,1)S(1)} %get-tuple-element.46), channel_id=1, source_target_pairs={{0,6},{1,7},{2,4},{3,5},{4,2},{5,3},{6,0},{7,1},{8,14},{9,15},{10,... | collective-permute-start | bytes 98312 | tf_op jit(solution)/shard_map/ppermute | solution.py:355
  126.2 3.3 %collective-permute-done.11.refs_6_ = bf16[64,256]{1,0:T(8,128)(2,1)S(1)} collective-permute-done((bf16[64,256]{1,0:T(8,128)(2,1)S(1)}, bf16[64,256]{1,0:T(8,128)(2,1)S(1)}, u32[]{:S(2)}, u32[]{:S(2)}) %collective-permute-start.11) | collective-permute-done | bytes 32800 | tf_op jit(solution)/shard_map/ppermute | solution.py:355
  130.4 1.3 place.1
  131.6 1.6 %mix.1 = bf16[64,4096]{1,0:T(8,128)(2,1)} custom-call(s32[2,64]{1,0:T(2,128)S(1)} %bitcast.6, f32[2,64]{1,0:T(2,128)S(1)} %bitcast.7, bf16[16,4,4096]{2,1,0:T(4,128)(2,1)S(1)} %all-to-all-done.3.refs_0_, bf16[16,4,4096]{2,1,0:T(4,128)(2,1)S(1)} %all-to-all-done.4.refs_1_), custom_call_target="tpu_custom_call" | custom-call | flops 1000 | bytes 1000 | tf_op jit(solution)/shard_map/mix/pallas_call | solution.py:370
  (28 shorter events, 6.1 us)
Async XLA Ops:
  25.8 18.6 %all-to-all-start.1 = ((bf16[16,4,4096]{2,1,0:T(4,128)(2,1)}), bf16[16,4,4096]{2,1,0:T(4,128)(2,1)S(1)}, u32[]{:S(2)}, u32[]{:S(2)}) async-start(bf16[16,4,4096]{2,1,0:T(4,128)(2,1)} %get-tuple-element.29), calls=%async_computation.1 | async-start | bytes 1048576 | tf_op jit(solution)/shard_map/all_to_all | solution.py:281
  30.0 14.5 %collective-permute-start = (bf16[16,4,4096]{2,1,0:T(4,128)(2,1)S(1)}, bf16[16,4,4096]{2,1,0:T(4,128)(2,1)S(1)}, u32[]{:S(2)}, u32[]{:S(2)}) collective-permute-start(bf16[16,4,4096]{2,1,0:T(4,128)(2,1)S(1)} %all_to_all.25.refs_0_), channel_id=1, source_target_pairs={{0,16},{16,0},{1,17},{17,1},{2,18},{18,2},{3,19},{19,3},{4,20},{20... | collective-permute-start | bytes 1572872 | tf_op jit(solution)/shard_map/ppermute | solution.py:287
  44.4 37.3 %all-to-all-start.2 = ((bf16[8,192,256]{2,1,0:T(8,128)(2,1)}), bf16[8,192,256]{2,1,0:T(8,128)(2,1)S(1)}, u32[]{:S(2)}, u32[]{:S(2)}) async-start(bf16[8,192,256]{2,1,0:T(8,128)(2,1)} %pack.1), calls=%async_computation.2 | async-start | bytes 1572864 | tf_op jit(solution)/shard_map/all_to_all | solution.py:318
  48.0 17.6 %collective-permute-start.1 = (bf16[16,4,4096]{2,1,0:T(4,128)(2,1)S(1)}, bf16[16,4,4096]{2,1,0:T(4,128)(2,1)S(1)}, u32[]{:S(2)}, u32[]{:S(2)}) collective-permute-start(bf16[16,4,4096]{2,1,0:T(4,128)(2,1)S(1)} %all-to-all-done.1.refs_0_), channel_id=1, source_target_pairs={{0,16},{16,0},{1,17},{17,1},{2,18},{18,2},{3,19},{19,3},{4,20},{20... | collective-permute-start | bytes 1572872 | tf_op jit(solution)/shard_map/ppermute | solution.py:287
  65.1 16.6 %collective-permute-start.2 = (bf16[16,4,4096]{2,1,0:T(4,128)(2,1)}, bf16[16,4,4096]{2,1,0:T(4,128)(2,1)}, u32[]{:S(2)}, u32[]{:S(2)}) collective-permute-start(bf16[16,4,4096]{2,1,0:T(4,128)(2,1)} %get-tuple-element.38), channel_id=1, source_target_pairs={{0,16},{16,0},{1,17},{17,1},{2,18},{18,2},{3,19},{19,3},{4,20},{20... | collective-permute-start | bytes 1572872 | tf_op jit(solution)/shard_map/ppermute | solution.py:339
  65.6 66.0 %copy-start = (s32[64,2]{0,1:T(2,128)S(1)}, s32[64,2]{0,1:T(2,128)}, u32[]{:S(2)}) copy-start(s32[64,2]{0,1:T(2,128)} %param.15) | copy-start | bytes 1540
  65.6 66.0 %copy-start.1 = (f32[64,2]{0,1:T(2,128)S(1)}, f32[64,2]{0,1:T(2,128)}, u32[]{:S(2)}) copy-start(f32[64,2]{0,1:T(2,128)} %param.16) | copy-start | bytes 1540
  80.1 14.7 %collective-permute-start.13 = (bf16[16,4,4096]{2,1,0:T(4,128)(2,1)S(1)}, bf16[16,4,4096]{2,1,0:T(4,128)(2,1)}, u32[]{:S(2)}, u32[]{:S(2)}) collective-permute-start(bf16[16,4,4096]{2,1,0:T(4,128)(2,1)S(1)} %get-tuple-element.50), channel_id=1, source_target_pairs={{0,16},{16,0},{1,17},{17,1},{2,18},{18,2},{3,19},{19,3},{4,20},{20... | collective-permute-start | bytes 1572872 | tf_op jit(solution)/shard_map/ppermute | solution.py:339
  84.1 26.9 %all-to-all-start.3 = ((bf16[16,4,4096]{2,1,0:T(4,128)(2,1)}), bf16[16,4,4096]{2,1,0:T(4,128)(2,1)S(1)}, u32[]{:S(2)}, u32[]{:S(2)}) async-start(bf16[16,4,4096]{2,1,0:T(4,128)(2,1)} %add_convert_fusion.1), calls=%async_computation.3 | async-start | bytes 1048576 | tf_op jit(solution)/shard_map/all_to_all | solution.py:369
  90.3 19.8 %collective-permute-start.3 = (bf16[128,256]{1,0:T(8,128)(2,1)S(1)}, bf16[128,256]{1,0:T(8,128)(2,1)S(1)}, u32[]{:S(2)}, u32[]{:S(2)}) collective-permute-start(bf16[128,256]{1,0:T(8,128)(2,1)S(1)} %sums.1.refs_0_), channel_id=1, source_target_pairs={{0,8},{1,9},{2,10},{3,11},{4,12},{5,13},{6,14},{7,15},{8,0},{9,1},... | collective-permute-start | bytes 196616 | tf_op jit(solution)/shard_map/ppermute | solution.py:334
  93.2 16.9 %collective-permute-start.4 = (bf16[128,256]{1,0:T(8,128)(2,1)S(1)}, bf16[128,256]{1,0:T(8,128)(2,1)S(1)}, u32[]{:S(2)}, u32[]{:S(2)}) collective-permute-start(bf16[128,256]{1,0:T(8,128)(2,1)S(1)} %sums.1.refs_0_), channel_id=1, source_target_pairs={{0,16},{1,17},{2,18},{3,19},{4,20},{5,21},{6,22},{7,23},{8,24},{9,... | collective-permute-start | bytes 196616 | tf_op jit(solution)/shard_map/ppermute | solution.py:334
  93.8 17.2 %collective-permute-start.5 = (bf16[128,256]{1,0:T(8,128)(2,1)S(1)}, bf16[128,256]{1,0:T(8,128)(2,1)S(1)}, u32[]{:S(2)}, u32[]{:S(2)}) collective-permute-start(bf16[128,256]{1,0:T(8,128)(2,1)S(1)} %sums.1.refs_0_), channel_id=1, source_target_pairs={{0,24},{1,25},{2,26},{3,27},{4,28},{5,29},{6,30},{7,31},{8,16},{9,... | collective-permute-start | bytes 196616 | tf_op jit(solution)/shard_map/ppermute | solution.py:334
  111.0 20.6 %all-to-all-start.4 = ((bf16[16,4,4096]{2,1,0:T(4,128)(2,1)}), bf16[16,4,4096]{2,1,0:T(4,128)(2,1)S(1)}, u32[]{:S(2)}, u32[]{:S(2)}) async-start(bf16[16,4,4096]{2,1,0:T(4,128)(2,1)} %add_convert_fusion), calls=%async_computation.4 | async-start | bytes 1048576 | tf_op jit(solution)/shard_map/all_to_all | solution.py:369
  118.2 4.0 %collective-permute-start.6 = (bf16[64,256]{1,0:T(8,128)(2,1)S(1)}, bf16[64,256]{1,0:T(8,128)(2,1)S(1)}, u32[]{:S(2)}, u32[]{:S(2)}) collective-permute-start(bf16[64,256]{1,0:T(8,128)(2,1)S(1)} %get-tuple-element.41), channel_id=1, source_target_pairs={{0,1},{1,0},{2,3},{3,2},{4,5},{5,4},{6,7},{7,6},{8,9},{9,8},{10,11... | collective-permute-start | bytes 98312 | tf_op jit(solution)/shard_map/ppermute | solution.py:355
  118.7 6.1 %collective-permute-start.7 = (bf16[64,256]{1,0:T(8,128)(2,1)S(1)}, bf16[64,256]{1,0:T(8,128)(2,1)S(1)}, u32[]{:S(2)}, u32[]{:S(2)}) collective-permute-start(bf16[64,256]{1,0:T(8,128)(2,1)S(1)} %get-tuple-element.42), channel_id=1, source_target_pairs={{0,2},{1,3},{2,0},{3,1},{4,6},{5,7},{6,4},{7,5},{8,10},{9,11},{10,... | collective-permute-start | bytes 98312 | tf_op jit(solution)/shard_map/ppermute | solution.py:355
  120.4 5.2 %collective-permute-start.8 = (bf16[64,256]{1,0:T(8,128)(2,1)S(1)}, bf16[64,256]{1,0:T(8,128)(2,1)S(1)}, u32[]{:S(2)}, u32[]{:S(2)}) collective-permute-start(bf16[64,256]{1,0:T(8,128)(2,1)S(1)} %get-tuple-element.43), channel_id=1, source_target_pairs={{0,3},{1,2},{2,1},{3,0},{4,7},{5,6},{6,5},{7,4},{8,11},{9,10},{10,... | collective-permute-start | bytes 98312 | tf_op jit(solution)/shard_map/ppermute | solution.py:355
  120.4 5.3 %collective-permute-start.9 = (bf16[64,256]{1,0:T(8,128)(2,1)S(1)}, bf16[64,256]{1,0:T(8,128)(2,1)S(1)}, u32[]{:S(2)}, u32[]{:S(2)}) collective-permute-start(bf16[64,256]{1,0:T(8,128)(2,1)S(1)} %get-tuple-element.44), channel_id=1, source_target_pairs={{0,4},{1,5},{2,6},{3,7},{4,0},{5,1},{6,2},{7,3},{8,12},{9,13},{10,... | collective-permute-start | bytes 98312 | tf_op jit(solution)/shard_map/ppermute | solution.py:355
  122.1 4.1 %collective-permute-start.10 = (bf16[64,256]{1,0:T(8,128)(2,1)S(1)}, bf16[64,256]{1,0:T(8,128)(2,1)S(1)}, u32[]{:S(2)}, u32[]{:S(2)}) collective-permute-start(bf16[64,256]{1,0:T(8,128)(2,1)S(1)} %get-tuple-element.45), channel_id=1, source_target_pairs={{0,5},{1,4},{2,7},{3,6},{4,1},{5,0},{6,3},{7,2},{8,13},{9,12},{10,... | collective-permute-start | bytes 98312 | tf_op jit(solution)/shard_map/ppermute | solution.py:355
  122.2 7.4 %collective-permute-start.11 = (bf16[64,256]{1,0:T(8,128)(2,1)S(1)}, bf16[64,256]{1,0:T(8,128)(2,1)S(1)}, u32[]{:S(2)}, u32[]{:S(2)}) collective-permute-start(bf16[64,256]{1,0:T(8,128)(2,1)S(1)} %get-tuple-element.46), channel_id=1, source_target_pairs={{0,6},{1,7},{2,4},{3,5},{4,2},{5,3},{6,0},{7,1},{8,14},{9,15},{10,... | collective-permute-start | bytes 98312 | tf_op jit(solution)/shard_map/ppermute | solution.py:355
  124.8 5.6 %collective-permute-start.12 = (bf16[64,256]{1,0:T(8,128)(2,1)S(1)}, bf16[64,256]{1,0:T(8,128)(2,1)S(1)}, u32[]{:S(2)}, u32[]{:S(2)}) collective-permute-start(bf16[64,256]{1,0:T(8,128)(2,1)S(1)} %get-tuple-element.47), channel_id=1, source_target_pairs={{0,7},{1,6},{2,5},{3,4},{4,3},{5,2},{6,1},{7,0},{8,15},{9,14},{10,... | collective-permute-start | bytes 98312 | tf_op jit(solution)/shard_map/ppermute | solution.py:355
